TPU v7x, 32 devices: a whole 2x2x4 slice. The times are simulated.
32 devices in a mesh: dp: 4 (over y, x), seq: 8 (over z, core).
Axes of the slice: x: 2, y: 2, z: 4, core: 2. Of those that a mesh axis runs over, the one named last changes fastest.
Arguments:
- tokens: bfloat16 [4, 2048, 4096], P('dp', 'seq'), may hold values from -6 to 6
- w_qkv: bfloat16 [4096, 768], P('dp'), may hold values from -0.09375 to 0.09375
- norm_gain: float32 [256], replicated, may hold values from 0.1 to 1.9
- w_out: bfloat16 [256, 4096], P(None, 'dp'), may hold values from -0.375 to 0.375
Outputs:
- mixed: bfloat16 [4, 2048, 4096], P('dp', 'seq')
All inputs are finite; a program needn't handle non-finite values.
Results may differ from a plain program's by a relative error of at most 0.015.
Values may be sent and summed in bfloat16 or wider, within the bound.
No kernel may reach another device: no remote copies, remote signals or barrier semaphores. Data moves between devices by JAX's collectives and lax.ppermute only.
A program may use at most 64 MiB of HBM per device.

v0:
```python
import functools

import jax
import jax.numpy as jnp
from jax import lax
from jax.experimental import pallas as pl
from jax.experimental.pallas import tpu as pltpu
from jax.sharding import PartitionSpec as P

HEAD = 128
CORES = 2
VMEM_LIMIT = 24 * 1024 * 1024
FIRST_LIMIT = 53 * 1024 * 1024
CUT_LIMIT = 52 * 1024 * 1024
VMEM = pl.BlockSpec(memory_space=pltpu.VMEM)
HBM = pl.BlockSpec(memory_space=pltpu.HBM)


def flip(x, axis, size, mask):
    return lax.ppermute(x, axis, [(i, i ^ mask) for i in range(size)])


def dot(a, b, contract=((1,), (0,))):
    return lax.dot_general(a, b, (contract, ((), ())), preferred_element_type=jnp.float32)


def position():
    return lax.axis_index("dp"), lax.rem(lax.axis_index("seq"), CORES)


def parity():
    return lax.rem(lax.axis_index("seq") // CORES, 2)


def quarter_of():
    return lax.rem(lax.axis_index("seq") // CORES, 4)


def cut_qkv(first, w_qkv, out, sem):
    _, core = position()
    feat = w_qkv.shape[1] // 3
    rows = pl.ds(pl.multiple_of(first(), 16), out.shape[0])
    copies = []
    for j in range(3):
        cols = pl.ds(pl.multiple_of(j * feat + core * HEAD, HEAD), HEAD)
        target = out.at[:, j * HEAD : (j + 1) * HEAD]
        copies.append(pltpu.make_async_copy(w_qkv.at[rows, cols], target, sem.at[j]))
        copies[-1].start()
    for copy in copies:
        copy.wait()


def cut_out(w_out, mine, theirs, part):
    _, core = position()
    rows = pl.ds(pl.multiple_of(core * HEAD, HEAD), HEAD)
    other = pl.ds(pl.multiple_of((1 - core) * HEAD, HEAD), HEAD)
    mine[...] = w_out[rows, :]
    theirs[...] = w_out[other, :]
    half = part.shape[1]
    part[...] = w_out[rows, pl.ds(pl.multiple_of(parity() * half, half), half)]


def product(tok_a, tok_b, pieces, places):
    cols = [
        pl.ds(pl.multiple_of(place, 128), piece.shape[0]) for piece, place in zip(pieces, places)
    ]
    tok = jnp.concatenate(
        [jnp.concatenate([ref[:, c] for c in cols], axis=1) for ref in (tok_a, tok_b)], axis=0
    )
    weights = jnp.concatenate([piece[...] for piece in pieces], axis=0)
    return dot(tok, weights)


def places_near(shard, offsets):
    at = lax.axis_index("dp")
    return [(at ^ offset) * shard for offset in offsets]


def places_far(shard):
    start = places_near(shard, (3,))[0]
    mine = quarter_of()
    return [start + (mine ^ mask) * (shard // 4) for mask in (0, 2, 1, 3)]


def project(count, places, tok_a, tok_b, *refs):
    pieces, before, total = refs[:count], refs[count:-1], refs[-1]
    term = product(tok_a, tok_b, pieces, places())
    total[...] = before[0][...] + term if before else term


def project_states(count, places, tok_a, tok_b, *refs):
    pieces, before = refs[:count], refs[count:-4]
    act_out, value_out, state_out, chip_out = refs[-4:]
    proj = product(tok_a, tok_b, pieces, places())
    if before:
        proj = before[0][...] + proj
    rows = value_out.shape[1]
    chip = None
    for b in range(CORES):
        part = proj[b * rows : (b + 1) * rows, :]
        act = part[:, : 2 * HEAD]
        act = (act / (1.0 + jnp.exp(-act))).astype(jnp.bfloat16)
        values = part[:, 2 * HEAD :].astype(jnp.bfloat16)
        state = dot(act[:, HEAD:], values, ((0,), (0,)))
        chip = state if chip is None else chip + state
        act_out[b] = act
        value_out[b] = values
        state_out[b] = state
    chip_out[...] = chip.astype(jnp.bfloat16)


def attend(act, values, *refs):
    if len(refs) > 1:
        own_half, other_half, intra_out, columns_out = refs
        half = own_half.shape[1]
        columns_out[:, pl.ds(pl.multiple_of(parity() * half, half), half)] = own_half[...]
        columns_out[:, pl.ds(pl.multiple_of((1 - parity()) * half, half), half)] = other_half[...]
    else:
        intra_out = refs[0]
    rows = intra_out.shape[1]
    row = lax.broadcasted_iota(jnp.int32, (rows, rows), 0)
    col = lax.broadcasted_iota(jnp.int32, (rows, rows), 1)
    for b in range(CORES):
        scores = dot(act[b, :, :HEAD], act[b, :, HEAD:], ((1,), (1,)))
        scores = jnp.where(row >= col, scores, 0.0).astype(jnp.bfloat16)
        intra_out[b] = dot(scores, values[b])


def normalise(steps, act, state, intra, gain, *refs):
    got, (own_out, other_out) = refs[:steps], refs[steps:]
    _, core = position()
    chip_at = lax.axis_index("seq") // CORES
    base = jnp.zeros((HEAD, HEAD), jnp.float32)
    for step, ref in enumerate(got):
        base = base + jnp.where((chip_at >> step) % 2 == 1, ref[...].astype(jnp.float32), 0.0)
    odd = core == 1
    own_prefix = jnp.where(odd, base + state[1], base)
    other_prefix = jnp.where(odd, base, base + state[0])
    scale = gain[pl.ds(core, 1), :]
    for b, (prefix, out) in enumerate(((own_prefix, own_out), (other_prefix, other_out))):
        attended = dot(act[b, :, :HEAD], prefix.astype(jnp.bfloat16)) + intra[b]
        meansq = jnp.mean(attended * attended, axis=-1, keepdims=True)
        out[...] = (attended * lax.rsqrt(meansq + 1e-06) * scale).astype(jnp.bfloat16)


def mix(count, places, own, other, *refs):
    mine, theirs, (out, stage, sem) = refs[:count], refs[count : 2 * count], refs[2 * count :]
    normed = jnp.concatenate([own[...], other[...]], axis=1)
    copies = []
    slot = 0
    for my_rows, their_rows, place in zip(mine, theirs, places()):
        width = my_rows.shape[1]
        step = min(width, 512)
        for at_col in range(0, width, step):
            part = slice(at_col, at_col + step)
            weights = jnp.concatenate([my_rows[:, part], their_rows[:, part]], axis=0)
            here = stage.at[:, slot : slot + step]
            here[...] = dot(normed, weights).astype(jnp.bfloat16)
            cols = pl.ds(pl.multiple_of(place + at_col, 128), step)
            copies.append(pltpu.make_async_copy(here, out.at[:, cols], sem.at[len(copies)]))
            copies[-1].start()
            slot += step
    for copy in copies:
        copy.wait()


def places_out(width):
    at = lax.axis_index("dp")
    return [(at ^ offset) * width for offset in range(4)]


def shards(n, blocks, tokens, w_qkv, norm_gain, w_out):
    tok_own = tokens[0]
    rows, depth = tok_own.shape
    shard = w_qkv.shape[0]
    heads = norm_gain.shape[0] // HEAD
    bf16, f32 = jnp.bfloat16, jnp.float32

    def call(kernel, outs, ins, out_specs, in_specs, scratch=(), flops=0, moved=0, limit=VMEM_LIMIT):
        return pl.pallas_call(
            kernel,
            out_shape=outs,
            in_specs=in_specs,
            out_specs=out_specs,
            scratch_shapes=scratch,
            compiler_params=pltpu.CompilerParams(vmem_limit_bytes=limit),
            cost_estimate=pl.CostEstimate(flops=flops, bytes_accessed=moved, transcendentals=0),
        )(*ins)

    def array(shape, kind):
        return jax.ShapeDtypeStruct(shape, kind)

    def add_product(pieces, places, total=None):
        extra = [] if total is None else [total]
        return call(
            functools.partial(project, len(pieces), places),
            array((CORES * rows, 3 * HEAD), f32),
            [tok_own, tok_other, *pieces, *extra],
            VMEM, [VMEM] * (2 + len(pieces) + len(extra)),
            flops=rows * HEAD * (1 if total is not None else 1000000),
        )

    tok_other = flip(tok_own, "seq", blocks, 1)
    width = w_out.shape[1]
    grid = n == 4 and blocks % (4 * CORES) == 0 and shard % 512 == 0 and width % 256 == 0

    def cut(first, size, limit):
        return call(
            functools.partial(cut_qkv, first), array((size, 3 * HEAD), bf16), [w_qkv], VMEM, [HBM],
            scratch=[pltpu.SemaphoreType.DMA((3,))], limit=limit,
        )

    out_cut = functools.partial(
        call, cut_out, [array((HEAD, width), bf16)] * 2 + [array((HEAD, width // 2), bf16)],
        [w_out], [VMEM] * 3, [VMEM]
    )
    total = None
    if grid:
        quarter = shard // 4
        part = cut(lambda: quarter_of() * quarter, quarter, FIRST_LIMIT)
        far = [flip(part, "dp", n, 3)]
        own = cut(lambda: 0, shard, CUT_LIMIT)
        from_x = flip(own, "dp", n, 1)
        from_y = flip(own, "dp", n, 2)
        far.append(flip(far[0], "seq", blocks, CORES * 2))
        far.append(flip(far[0], "seq", blocks, CORES))
        here, own = lax.optimization_barrier((far[0], own))
        total = add_product([own], functools.partial(places_near, shard, (0,)))
        passed, total = lax.optimization_barrier((far[1], total))
        far.append(flip(passed, "seq", blocks, CORES))
        own_mine, own_theirs, own_part = out_cut()
        send_part, total, far[1] = lax.optimization_barrier((own_part, total, far[1]))
        out_d = flip(send_part, "dp", n, 3)
        out_e = flip(out_d, "seq", blocks, CORES)
        sent, total, far[1] = lax.optimization_barrier((own_mine, total, far[1]))
        out_x = flip(sent, "dp", n, 1)
        out_y = flip(sent, "dp", n, 2)
        total = add_product(far[:3], lambda: places_far(shard)[:3], total)
        total = add_product([from_x, from_y], functools.partial(places_near, shard, (1, 2)), total)
        pieces, places = far[3:], lambda: places_far(shard)[3:]
    else:
        whole = cut(lambda: 0, shard, CUT_LIMIT)
        pieces, places = [lax.all_gather(whole, "dp", axis=0, tiled=True)], lambda: [0]
    extra = [] if total is None else [total]

    act, values, state, chip = call(
        functools.partial(project_states, len(pieces), places),
        [
            array((CORES, rows, 2 * HEAD), bf16),
            array((CORES, rows, HEAD), bf16),
            array((CORES, HEAD, HEAD), f32),
            array((HEAD, HEAD), bf16),
        ],
        [tok_own, tok_other, *pieces, *extra],
        [VMEM] * 4, [VMEM] * (2 + len(pieces) + len(extra)),
        flops=2 * CORES * rows * sum(piece.shape[0] for piece in pieces) * 3 * HEAD,
    )
    got, group = [], chip
    for step in range((blocks // CORES).bit_length() - 1):
        if got:
            group = (group.astype(f32) + got[-1].astype(f32)).astype(bf16)
            if grid:
                group, out_d = lax.optimization_barrier((group, out_d))
        got.append(flip(group, "seq", blocks, CORES << step))
    scored, halves, outs = act, [], [array((CORES, rows, HEAD), f32)]
    if grid:
        scored, out_x, out_y = lax.optimization_barrier((act, out_x, out_y))
        halves = [out_d, out_e]
        outs.append(array((HEAD, width), bf16))
    intra, *columns = call(
        attend, outs, [scored, values, *halves], [VMEM] * len(outs), [VMEM] * (2 + len(halves)),
        flops=rows * HEAD * 1000000,
    )
    if grid:
        out_x, out_y, columns[0], got[-1] = lax.optimization_barrier(
            (out_x, out_y, columns[0], got[-1])
        )
        mine = [own_mine, out_x, out_y, *columns]
        theirs = [own_theirs] + [flip(piece, "seq", blocks, 1) for piece in mine[1:]]
    normed_own, normed_other = call(
        functools.partial(normalise, len(got)),
        [array((rows, HEAD), bf16)] * 2,
        [act, state, intra, norm_gain.reshape(heads, HEAD), *got],
        [VMEM] * 2, [VMEM] * (4 + len(got)),
    )
    normed_got = flip(normed_other, "seq", blocks, 1)

    if grid:
        places = functools.partial(places_out, width)
    else:
        mine = [lax.all_gather(out_cut()[0], "dp", axis=1, tiled=True)]
        theirs = [flip(mine[0], "seq", blocks, 1)]
        places = lambda: [0]
    mixed = call(
        functools.partial(mix, len(mine), places),
        array((rows, n * width), bf16),
        [normed_own, normed_got, *mine, *theirs],
        HBM, [VMEM] * (2 + 2 * len(mine)),
        scratch=[pltpu.VMEM((rows, n * width), bf16), pltpu.SemaphoreType.DMA((16,))],
        flops=2 * rows * 2 * HEAD * n * width, moved=2 * rows * n * width,
    )
    return mixed[None]


def solution(mesh):
    n, blocks = mesh.shape["dp"], mesh.shape["seq"]
    return jax.shard_map(
        functools.partial(shards, n, blocks),
        mesh=mesh,
        in_specs=(P("dp", "seq", None), P("dp", None), P(), P(None, "dp")),
        out_specs=P("dp", "seq", None),
        check_vma=False,
    )
```

profile of v0, /device:TPU:0, one launch (start us, length us, event | category | flops | bytes accessed | tf_op | source)
XLA Modules:
  0.0 43.4 jit_solution(8435725958527580909)
XLA Ops:
  0.0 0.5 %collective-permute-start = (bf16[256,4096]{1,0:T(8,128)(2,1)}, bf16[256,4096]{1,0:T(8,128)(2,1)S(1)}, u32[]{:S(2)}, u32[]{:S(2)}) collective-permute-start(bf16[256,4096]{1,0:T(8,128)(2,1)} %bitcast.3), channel_id=1, source_target_pairs={{0,1},{1,0},{2,3},{3,2},{4,5},{5,4},{6,7},{7,6},{8,9},{9,8},{10,11... | collective-permute-start | bytes 6291464 | tf_op jit(solution)/shard_map/ppermute | solution.py:20
  0.5 1.1 %shard_map.46 = bf16[256,384]{1,0:T(8,128)(2,1)S(1)} custom-call(bf16[1024,768]{1,0:T(8,128)(2,1)} %w_qkv.3), custom_call_target="tpu_custom_call" | custom-call | tf_op jit(solution)/shard_map/pallas_call | solution.py:180
  1.6 3.5 %collective-permute-start.1 = (bf16[256,384]{1,0:T(8,128)(2,1)S(1)}, bf16[256,384]{1,0:T(8,128)(2,1)S(1)}, u32[]{:S(2)}, u32[]{:S(2)}) collective-permute-start(bf16[256,384]{1,0:T(8,128)(2,1)S(1)} %shard_map.46), channel_id=1, source_target_pairs={{0,24},{8,16},{16,8},{24,0},{1,25},{9,17},{17,9},{25,1},{2,26},{10... | collective-permute-start | bytes 589832 | tf_op jit(solution)/shard_map/ppermute | solution.py:20
  5.1 1.1 %shard_map.47.refs_0_ = bf16[1024,384]{1,0:T(8,128)(2,1)S(1)} custom-call(bf16[1024,768]{1,0:T(8,128)(2,1)} %w_qkv.3), custom_call_target="tpu_custom_call" | custom-call | tf_op jit(solution)/shard_map/pallas_call | solution.py:180
  6.2 0.0 copy-start.1
  6.2 0.6 %collective-permute-start.4 = (bf16[1024,384]{1,0:T(8,128)(2,1)S(1)}, bf16[1024,384]{1,0:T(8,128)(2,1)S(1)}, u32[]{:S(2)}, u32[]{:S(2)}) collective-permute-start(bf16[1024,384]{1,0:T(8,128)(2,1)S(1)} %shard_map.47.refs_0_), channel_id=1, source_target_pairs={{0,8},{8,0},{16,24},{24,16},{1,9},{9,1},{17,25},{25,17},{2,10},{10... | collective-permute-start | bytes 2359304 | tf_op jit(solution)/shard_map/ppermute | solution.py:20
  6.8 0.1 collective-permute-start.5
  6.9 3.9 %collective-permute-done.1.refs_0_ = bf16[256,384]{1,0:T(8,128)(2,1)S(1)} collective-permute-done((bf16[256,384]{1,0:T(8,128)(2,1)S(1)}, bf16[256,384]{1,0:T(8,128)(2,1)S(1)}, u32[]{:S(2)}, u32[]{:S(2)}) %collective-permute-start.1) | collective-permute-done | bytes 196640 | tf_op jit(solution)/shard_map/ppermute | solution.py:20
  10.8 3.0 %collective-permute-start.2 = (bf16[256,384]{1,0:T(8,128)(2,1)S(1)}, bf16[256,384]{1,0:T(8,128)(2,1)S(1)}, u32[]{:S(2)}, u32[]{:S(2)}) collective-permute-start(bf16[256,384]{1,0:T(8,128)(2,1)S(1)} %collective-permute-done.1.refs_0_), channel_id=1, source_target_pairs={{0,4},{1,5},{2,6},{3,7},{4,0},{5,1},{6,2},{7,3},{8,12},{9,13},{10,... | collective-permute-start | bytes 589832 | tf_op jit(solution)/shard_map/ppermute | solution.py:20
  13.8 1.6 %collective-permute-start.6 = (bf16[256,384]{1,0:T(8,128)(2,1)S(1)}, bf16[256,384]{1,0:T(8,128)(2,1)S(1)}, u32[]{:S(2)}, u32[]{:S(2)}) collective-permute-start(bf16[256,384]{1,0:T(8,128)(2,1)S(1)} %collective-permute-done.1.refs_0_), channel_id=1, source_target_pairs={{0,2},{1,3},{2,0},{3,1},{4,6},{5,7},{6,4},{7,5},{8,10},{9,11},{10,... | collective-permute-start | bytes 589832 | tf_op jit(solution)/shard_map/ppermute | solution.py:20
  15.4 0.7 %shard_map.48.refs_3_ = f32[512,384]{1,0:T(8,128)S(1)} custom-call(bf16[256,4096]{1,0:T(8,128)(2,1)S(1)} %bitcast.4, bf16[256,4096]{1,0:T(8,128)(2,1)S(1)} %collective-permute-done.tok_b, bf16[1024,384]{1,0:T(8,128)(2,1)S(1)} %shard_map.47.refs_0_), custom_call_target="tpu_custom_call" | custom-call | flops 32768000000 | tf_op jit(solution)/shard_map/pallas_call | solution.py:180
  16.1 6.2 %collective-permute-done.2.refs_1_ = bf16[256,384]{1,0:T(8,128)(2,1)S(1)} collective-permute-done((bf16[256,384]{1,0:T(8,128)(2,1)S(1)}, bf16[256,384]{1,0:T(8,128)(2,1)S(1)}, u32[]{:S(2)}, u32[]{:S(2)}) %collective-permute-start.2) | collective-permute-done | bytes 196640 | tf_op jit(solution)/shard_map/ppermute | solution.py:20
  22.3 0.5 %collective-permute-start.3 = (bf16[256,384]{1,0:T(8,128)(2,1)S(1)}, bf16[256,384]{1,0:T(8,128)(2,1)S(1)}, u32[]{:S(2)}, u32[]{:S(2)}) collective-permute-start(bf16[256,384]{1,0:T(8,128)(2,1)S(1)} %collective-permute-done.2.refs_1_), channel_id=1, source_target_pairs={{0,2},{1,3},{2,0},{3,1},{4,6},{5,7},{6,4},{7,5},{8,10},{9,11},{10,... | collective-permute-start | bytes 589832 | tf_op jit(solution)/shard_map/ppermute | solution.py:20
  22.9 2.6 %collective-permute-start.10 = (bf16[128,512]{1,0:T(8,128)(2,1)S(1)}, bf16[128,512]{1,0:T(8,128)(2,1)S(1)}, u32[]{:S(2)}, u32[]{:S(2)}) collective-permute-start(bf16[128,512]{1,0:T(8,128)(2,1)S(1)} %get-tuple-element.49), channel_id=1, source_target_pairs={{0,24},{8,16},{16,8},{24,0},{1,25},{9,17},{17,9},{25,1},{2,26},{10... | collective-permute-start | bytes 393224 | tf_op jit(solution)/shard_map/ppermute | solution.py:20
  25.4 0.5 %collective-permute-start.7 = (bf16[128,1024]{1,0:T(8,128)(2,1)S(1)}, bf16[128,1024]{1,0:T(8,128)(2,1)S(1)}, u32[]{:S(2)}, u32[]{:S(2)}) collective-permute-start(bf16[128,1024]{1,0:T(8,128)(2,1)S(1)} %get-tuple-element.45.refs_0_), channel_id=1, source_target_pairs={{0,8},{8,0},{16,24},{24,16},{1,9},{9,1},{17,25},{25,17},{2,10},{10... | collective-permute-start | bytes 786440 | tf_op jit(solution)/shard_map/ppermute | solution.py:20
  26.0 0.6 %shard_map.50.refs_2_ = f32[512,384]{1,0:T(8,128)S(1)} custom-call(bf16[256,4096]{1,0:T(8,128)(2,1)S(1)} %bitcast.5, bf16[256,4096]{1,0:T(8,128)(2,1)S(1)} %collective-permute-done.tok_b, bf16[256,384]{1,0:T(8,128)(2,1)S(1)} %collective-permute-done.1.refs_0_, bf16[256,384]{1,0:T(8,128)(2,1)S(1)} %collective-permute-done.2.refs_1_, ...), custom_call_target="tpu_custom_call" | custom-call | flops 32768 | tf_op jit(solution)/shard_map/pallas_call | solution.py:180
  26.5 1.7 %collective-permute-done.4.refs_0_ = bf16[1024,384]{1,0:T(8,128)(2,1)S(1)} collective-permute-done((bf16[1024,384]{1,0:T(8,128)(2,1)S(1)}, bf16[1024,384]{1,0:T(8,128)(2,1)S(1)}, u32[]{:S(2)}, u32[]{:S(2)}) %collective-permute-start.4) | collective-permute-done | bytes 786464 | tf_op jit(solution)/shard_map/ppermute | solution.py:20
  28.2 0.0 collective-permute-start.8
  28.2 1.3 %shard_map.51.refs_1_ = f32[512,384]{1,0:T(8,128)S(1)} custom-call(bf16[256,4096]{1,0:T(8,128)(2,1)S(1)} %bitcast.6, bf16[256,4096]{1,0:T(8,128)(2,1)S(1)} %collective-permute-done.tok_b, bf16[1024,384]{1,0:T(8,128)(2,1)S(1)} %collective-permute-done.4.refs_0_, bf16[1024,384]{1,0:T(8,128)(2,1)S(1)} %collective-permute-done.5.refs_1_, ...), custom_call_target="tpu_custom_call" | custom-call | flops 32768 | tf_op jit(solution)/shard_map/pallas_call | solution.py:180
  29.5 0.5 %shard_map.52 = (bf16[2,256,256]{2,1,0:T(8,128)(2,1)S(1)}, bf16[2,256,128]{2,1,0:T(8,128)(2,1)S(1)}, f32[2,128,128]{2,1,0:T(8,128)S(1)}, bf16[128,128]{1,0:T(8,128)(2,1)S(1)}) custom-call(bf16[256,4096]{1,0:T(8,128)(2,1)S(1)} %bitcast.7, bf16[256,4096]{1,0:T(8,128)(2,1)S(1)} %collective-permute-done.tok_b, ...), custom_call_target="tpu_custom_call" | custom-call | flops 100663296 | tf_op jit(solution)/shard_map/pallas_call | solution.py:180
  30.1 2.1 %collective-permute-start.9 = (bf16[128,128]{1,0:T(8,128)(2,1)S(1)}, bf16[128,128]{1,0:T(8,128)(2,1)S(1)}, u32[]{:S(2)}, u32[]{:S(2)}) collective-permute-start(bf16[128,128]{1,0:T(8,128)(2,1)S(1)} %get-tuple-element.48), channel_id=1, source_target_pairs={{0,2},{1,3},{2,0},{3,1},{4,6},{5,7},{6,4},{7,5},{8,10},{9,11},{10,... | collective-permute-start | bytes 98312 | tf_op jit(solution)/shard_map/ppermute | solution.py:20
  32.1 0.4 collective-permute-start.11
  32.5 1.9 %collective-permute-done.9.refs_0_ = bf16[128,128]{1,0:T(8,128)(2,1)S(1)} collective-permute-done((bf16[128,128]{1,0:T(8,128)(2,1)S(1)}, bf16[128,128]{1,0:T(8,128)(2,1)S(1)}, u32[]{:S(2)}, u32[]{:S(2)}) %collective-permute-start.9) | collective-permute-done | bytes 32800 | tf_op jit(solution)/shard_map/ppermute | solution.py:20
  34.4 3.0 %collective-permute-start.12 = (bf16[128,128]{1,0:T(8,128)(2,1)S(1)}, bf16[128,128]{1,0:T(8,128)(2,1)S(1)}, u32[]{:S(2)}, u32[]{:S(2)}) collective-permute-start(bf16[128,128]{1,0:T(8,128)(2,1)S(1)} %add_convert_fusion), channel_id=1, source_target_pairs={{0,4},{1,5},{2,6},{3,7},{4,0},{5,1},{6,2},{7,3},{8,12},{9,13},{10,... | collective-permute-start | bytes 98312 | tf_op jit(solution)/shard_map/ppermute | solution.py:20
  37.4 0.0 collective-permute-done.11.refs_1_
  37.4 0.5 %shard_map.53 = (f32[2,256,128]{2,1,0:T(8,128)S(1)}, bf16[128,1024]{1,0:T(8,128)(2,1)S(1)}) custom-call(bf16[2,256,256]{2,1,0:T(8,128)(2,1)S(1)} %get-tuple-element.46.act, bf16[2,256,128]{2,1,0:T(8,128)(2,1)S(1)} %get-tuple-element.47.values, bf16[128,512]{1,0:T(8,128)(2,1)S(1)} %collective-permute-done.10.refs_0_, ...), custom_call_target="tpu_custom_call" | custom-call | flops 32768000000 | tf_op jit(solution)/shard_map/pallas_call | solution.py:180
  38.0 1.3 %collective-permute-done.12.refs_1_ = bf16[128,128]{1,0:T(8,128)(2,1)S(1)} collective-permute-done((bf16[128,128]{1,0:T(8,128)(2,1)S(1)}, bf16[128,128]{1,0:T(8,128)(2,1)S(1)}, u32[]{:S(2)}, u32[]{:S(2)}) %collective-permute-start.12) | collective-permute-done | bytes 32800 | tf_op jit(solution)/shard_map/ppermute | solution.py:20
  39.3 0.5 %collective-permute-start.15 = (bf16[128,1024]{1,0:T(8,128)(2,1)S(1)}, bf16[128,1024]{1,0:T(8,128)(2,1)S(1)}, u32[]{:S(2)}, u32[]{:S(2)}) collective-permute-start(bf16[128,1024]{1,0:T(8,128)(2,1)S(1)} %collective-permute-done.8.refs_2_), channel_id=1, source_target_pairs={{0,1},{1,0},{2,3},{3,2},{4,5},{5,4},{6,7},{7,6},{8,9},{9,8},{10,11... | collective-permute-start | bytes 786440 | tf_op jit(solution)/shard_map/ppermute | solution.py:20
  39.8 0.3 shard_map.54
  40.1 0.6 %collective-permute-start.13 = (bf16[256,128]{1,0:T(8,128)(2,1)S(1)}, bf16[256,128]{1,0:T(8,128)(2,1)S(1)}, u32[]{:S(2)}, u32[]{:S(2)}) collective-permute-start(bf16[256,128]{1,0:T(8,128)(2,1)S(1)} %get-tuple-element.58), channel_id=1, source_target_pairs={{0,1},{1,0},{2,3},{3,2},{4,5},{5,4},{6,7},{7,6},{8,9},{9,8},{10,11... | collective-permute-start | bytes 196616 | tf_op jit(solution)/shard_map/ppermute | solution.py:20
  40.7 1.0 %collective-permute-done.13.other = bf16[256,128]{1,0:T(8,128)(2,1)S(1)} collective-permute-done((bf16[256,128]{1,0:T(8,128)(2,1)S(1)}, bf16[256,128]{1,0:T(8,128)(2,1)S(1)}, u32[]{:S(2)}, u32[]{:S(2)}) %collective-permute-start.13) | collective-permute-done | bytes 65568 | tf_op jit(solution)/shard_map/ppermute | solution.py:20
  41.7 1.7 %shard_map.55 = bf16[256,4096]{1,0:T(8,128)(2,1)} custom-call(bf16[256,128]{1,0:T(8,128)(2,1)S(1)} %get-tuple-element.57.own, bf16[256,128]{1,0:T(8,128)(2,1)S(1)} %collective-permute-done.13.other, bf16[128,1024]{1,0:T(8,128)(2,1)S(1)} %get-tuple-element.45.refs_0_, bf16[128,1024]{1,0:T(8,128)(2,1)S(1)} %collective-permute-done.7.refs_1_, ...), custom_call_target="tpu_custom_call" | custom-call | flops 536870912 | bytes 2097152 | tf_op jit(solution)/shard_map/pallas_call | solution.py:180
  (19 shorter events, 0.1 us)
Async XLA Ops:
  0.0 15.4 %copy-start = (bf16[1,256,4096]{2,1,0:T(8,128)(2,1)S(1)}, bf16[1,256,4096]{2,1,0:T(8,128)(2,1)}, u32[]{:S(2)}) copy-start(bf16[1,256,4096]{2,1,0:T(8,128)(2,1)} %param.4) | copy-start | bytes 6291460
  0.0 15.4 %collective-permute-start = (bf16[256,4096]{1,0:T(8,128)(2,1)}, bf16[256,4096]{1,0:T(8,128)(2,1)S(1)}, u32[]{:S(2)}, u32[]{:S(2)}) collective-permute-start(bf16[256,4096]{1,0:T(8,128)(2,1)} %bitcast.3), channel_id=1, source_target_pairs={{0,1},{1,0},{2,3},{3,2},{4,5},{5,4},{6,7},{7,6},{8,9},{9,8},{10,11... | collective-permute-start | bytes 6291464 | tf_op jit(solution)/shard_map/ppermute | solution.py:20
  1.6 9.2 %collective-permute-start.1 = (bf16[256,384]{1,0:T(8,128)(2,1)S(1)}, bf16[256,384]{1,0:T(8,128)(2,1)S(1)}, u32[]{:S(2)}, u32[]{:S(2)}) collective-permute-start(bf16[256,384]{1,0:T(8,128)(2,1)S(1)} %shard_map.46), channel_id=1, source_target_pairs={{0,24},{8,16},{16,8},{24,0},{1,25},{9,17},{17,9},{25,1},{2,26},{10... | collective-permute-start | bytes 589832 | tf_op jit(solution)/shard_map/ppermute | solution.py:20
  6.2 16.6 %copy-start.1 = (bf16[256,1024]{1,0:T(8,128)(2,1)S(1)}, bf16[256,1024]{1,0:T(8,128)(2,1)}, u32[]{:S(2)}) copy-start(bf16[256,1024]{1,0:T(8,128)(2,1)} %w_out.1) | copy-start | bytes 1572868
  6.2 22.0 %collective-permute-start.4 = (bf16[1024,384]{1,0:T(8,128)(2,1)S(1)}, bf16[1024,384]{1,0:T(8,128)(2,1)S(1)}, u32[]{:S(2)}, u32[]{:S(2)}) collective-permute-start(bf16[1024,384]{1,0:T(8,128)(2,1)S(1)} %shard_map.47.refs_0_), channel_id=1, source_target_pairs={{0,8},{8,0},{16,24},{24,16},{1,9},{9,1},{17,25},{25,17},{2,10},{10... | collective-permute-start | bytes 2359304 | tf_op jit(solution)/shard_map/ppermute | solution.py:20
  6.8 21.4 %collective-permute-start.5 = (bf16[1024,384]{1,0:T(8,128)(2,1)S(1)}, bf16[1024,384]{1,0:T(8,128)(2,1)S(1)}, u32[]{:S(2)}, u32[]{:S(2)}) collective-permute-start(bf16[1024,384]{1,0:T(8,128)(2,1)S(1)} %shard_map.47.refs_0_), channel_id=1, source_target_pairs={{0,16},{8,24},{16,0},{24,8},{1,17},{9,25},{17,1},{25,9},{2,18},{10... | collective-permute-start | bytes 2359304 | tf_op jit(solution)/shard_map/ppermute | solution.py:20
  10.8 11.5 %collective-permute-start.2 = (bf16[256,384]{1,0:T(8,128)(2,1)S(1)}, bf16[256,384]{1,0:T(8,128)(2,1)S(1)}, u32[]{:S(2)}, u32[]{:S(2)}) collective-permute-start(bf16[256,384]{1,0:T(8,128)(2,1)S(1)} %collective-permute-done.1.refs_0_), channel_id=1, source_target_pairs={{0,4},{1,5},{2,6},{3,7},{4,0},{5,1},{6,2},{7,3},{8,12},{9,13},{10,... | collective-permute-start | bytes 589832 | tf_op jit(solution)/shard_map/ppermute | solution.py:20
  13.8 11.6 %collective-permute-start.6 = (bf16[256,384]{1,0:T(8,128)(2,1)S(1)}, bf16[256,384]{1,0:T(8,128)(2,1)S(1)}, u32[]{:S(2)}, u32[]{:S(2)}) collective-permute-start(bf16[256,384]{1,0:T(8,128)(2,1)S(1)} %collective-permute-done.1.refs_0_), channel_id=1, source_target_pairs={{0,2},{1,3},{2,0},{3,1},{4,6},{5,7},{6,4},{7,5},{8,10},{9,11},{10,... | collective-permute-start | bytes 589832 | tf_op jit(solution)/shard_map/ppermute | solution.py:20
  22.3 7.2 %collective-permute-start.3 = (bf16[256,384]{1,0:T(8,128)(2,1)S(1)}, bf16[256,384]{1,0:T(8,128)(2,1)S(1)}, u32[]{:S(2)}, u32[]{:S(2)}) collective-permute-start(bf16[256,384]{1,0:T(8,128)(2,1)S(1)} %collective-permute-done.2.refs_1_), channel_id=1, source_target_pairs={{0,2},{1,3},{2,0},{3,1},{4,6},{5,7},{6,4},{7,5},{8,10},{9,11},{10,... | collective-permute-start | bytes 589832 | tf_op jit(solution)/shard_map/ppermute | solution.py:20
  22.9 9.3 %collective-permute-start.10 = (bf16[128,512]{1,0:T(8,128)(2,1)S(1)}, bf16[128,512]{1,0:T(8,128)(2,1)S(1)}, u32[]{:S(2)}, u32[]{:S(2)}) collective-permute-start(bf16[128,512]{1,0:T(8,128)(2,1)S(1)} %get-tuple-element.49), channel_id=1, source_target_pairs={{0,24},{8,16},{16,8},{24,0},{1,25},{9,17},{17,9},{25,1},{2,26},{10... | collective-permute-start | bytes 393224 | tf_op jit(solution)/shard_map/ppermute | solution.py:20
  25.4 12.0 %collective-permute-start.7 = (bf16[128,1024]{1,0:T(8,128)(2,1)S(1)}, bf16[128,1024]{1,0:T(8,128)(2,1)S(1)}, u32[]{:S(2)}, u32[]{:S(2)}) collective-permute-start(bf16[128,1024]{1,0:T(8,128)(2,1)S(1)} %get-tuple-element.45.refs_0_), channel_id=1, source_target_pairs={{0,8},{8,0},{16,24},{24,16},{1,9},{9,1},{17,25},{25,17},{2,10},{10... | collective-permute-start | bytes 786440 | tf_op jit(solution)/shard_map/ppermute | solution.py:20
  28.2 9.2 %collective-permute-start.8 = (bf16[128,1024]{1,0:T(8,128)(2,1)S(1)}, bf16[128,1024]{1,0:T(8,128)(2,1)S(1)}, u32[]{:S(2)}, u32[]{:S(2)}) collective-permute-start(bf16[128,1024]{1,0:T(8,128)(2,1)S(1)} %get-tuple-element.45.refs_0_), channel_id=1, source_target_pairs={{0,16},{8,24},{16,0},{24,8},{1,17},{9,25},{17,1},{25,9},{2,18},{10... | collective-permute-start | bytes 786440 | tf_op jit(solution)/shard_map/ppermute | solution.py:20
  30.1 4.3 %collective-permute-start.9 = (bf16[128,128]{1,0:T(8,128)(2,1)S(1)}, bf16[128,128]{1,0:T(8,128)(2,1)S(1)}, u32[]{:S(2)}, u32[]{:S(2)}) collective-permute-start(bf16[128,128]{1,0:T(8,128)(2,1)S(1)} %get-tuple-element.48), channel_id=1, source_target_pairs={{0,2},{1,3},{2,0},{3,1},{4,6},{5,7},{6,4},{7,5},{8,10},{9,11},{10,... | collective-permute-start | bytes 98312 | tf_op jit(solution)/shard_map/ppermute | solution.py:20
  32.1 5.3 %collective-permute-start.11 = (bf16[128,512]{1,0:T(8,128)(2,1)S(1)}, bf16[128,512]{1,0:T(8,128)(2,1)S(1)}, u32[]{:S(2)}, u32[]{:S(2)}) collective-permute-start(bf16[128,512]{1,0:T(8,128)(2,1)S(1)} %collective-permute-done.10.refs_0_), channel_id=1, source_target_pairs={{0,2},{1,3},{2,0},{3,1},{4,6},{5,7},{6,4},{7,5},{8,10},{9,11},{10,... | collective-permute-start | bytes 393224 | tf_op jit(solution)/shard_map/ppermute | solution.py:20
  34.4 4.9 %collective-permute-start.12 = (bf16[128,128]{1,0:T(8,128)(2,1)S(1)}, bf16[128,128]{1,0:T(8,128)(2,1)S(1)}, u32[]{:S(2)}, u32[]{:S(2)}) collective-permute-start(bf16[128,128]{1,0:T(8,128)(2,1)S(1)} %add_convert_fusion), channel_id=1, source_target_pairs={{0,4},{1,5},{2,6},{3,7},{4,0},{5,1},{6,2},{7,3},{8,12},{9,13},{10,... | collective-permute-start | bytes 98312 | tf_op jit(solution)/shard_map/ppermute | solution.py:20
  37.4 2.4 %copy-start.2 = (f32[256]{0:T(256)S(1)}, f32[256]{0:T(256)}, u32[]{:S(2)}) copy-start(f32[256]{0:T(256)} %param.6) | copy-start | bytes 3076
  39.3 2.4 %collective-permute-start.14 = (bf16[128,1024]{1,0:T(8,128)(2,1)S(1)}, bf16[128,1024]{1,0:T(8,128)(2,1)S(1)}, u32[]{:S(2)}, u32[]{:S(2)}) collective-permute-start(bf16[128,1024]{1,0:T(8,128)(2,1)S(1)} %collective-permute-done.7.refs_1_), channel_id=1, source_target_pairs={{0,1},{1,0},{2,3},{3,2},{4,5},{5,4},{6,7},{7,6},{8,9},{9,8},{10,11... | collective-permute-start | bytes 786440 | tf_op jit(solution)/shard_map/ppermute | solution.py:20
  39.3 2.4 %collective-permute-start.15 = (bf16[128,1024]{1,0:T(8,128)(2,1)S(1)}, bf16[128,1024]{1,0:T(8,128)(2,1)S(1)}, u32[]{:S(2)}, u32[]{:S(2)}) collective-permute-start(bf16[128,1024]{1,0:T(8,128)(2,1)S(1)} %collective-permute-done.8.refs_2_), channel_id=1, source_target_pairs={{0,1},{1,0},{2,3},{3,2},{4,5},{5,4},{6,7},{7,6},{8,9},{9,8},{10,11... | collective-permute-start | bytes 786440 | tf_op jit(solution)/shard_map/ppermute | solution.py:20
  39.8 1.9 %collective-permute-start.16 = (bf16[128,1024]{1,0:T(8,128)(2,1)S(1)}, bf16[128,1024]{1,0:T(8,128)(2,1)S(1)}, u32[]{:S(2)}, u32[]{:S(2)}) collective-permute-start(bf16[128,1024]{1,0:T(8,128)(2,1)S(1)} %get-tuple-element.61.refs_3_), channel_id=1, source_target_pairs={{0,1},{1,0},{2,3},{3,2},{4,5},{5,4},{6,7},{7,6},{8,9},{9,8},{10,11... | collective-permute-start | bytes 786440 | tf_op jit(solution)/shard_map/ppermute | solution.py:20
  40.1 1.5 %collective-permute-start.13 = (bf16[256,128]{1,0:T(8,128)(2,1)S(1)}, bf16[256,128]{1,0:T(8,128)(2,1)S(1)}, u32[]{:S(2)}, u32[]{:S(2)}) collective-permute-start(bf16[256,128]{1,0:T(8,128)(2,1)S(1)} %get-tuple-element.58), channel_id=1, source_target_pairs={{0,1},{1,0},{2,3},{3,2},{4,5},{5,4},{6,7},{7,6},{8,9},{9,8},{10,11... | collective-permute-start | bytes 196616 | tf_op jit(solution)/shard_map/ppermute | solution.py:20
where the time goes:
time: 43.5 us; the launch traced here: 43.4 us
  starting transfers between devices  19.3 us (44%)
  waiting for transfers between devices  16 us (37%)
  Pallas kernels  7.88 us (18%)
    ppermute x17, starting transfers between devices, flip(): return lax.ppermute(x, axis, [(i, i ^ mask) for i in range(size)])  19.3 us
    ppermute x17, waiting for transfers between devices, flip(): return lax.ppermute(x, axis, [(i, i ^ mask) for i in range(size)])  16 us
    pallas_call x10, Pallas kernels, call(): pl.pallas_call(kernel, out_shape=outs, in_specs=in_specs, out_specs=out_s...  7.88 us
  transfers between devices with their start and end apart: 17, of which 6 were waited for; matrix products, arithmetic and copies ran while one was open for 0% of the time, Pallas kernels for 14%

commit v1 on v0

--- a/solution.py
+++ b/solution.py
@@ -272,16 +272,13 @@
         flops=rows * HEAD * 1000000,
     )
     if grid:
-        out_x, out_y, columns[0], got[-1] = lax.optimization_barrier(
-            (out_x, out_y, columns[0], got[-1])
-        )
         mine = [own_mine, out_x, out_y, *columns]
         theirs = [own_theirs] + [flip(piece, "seq", blocks, 1) for piece in mine[1:]]
     normed_own, normed_other = call(
         functools.partial(normalise, len(got)),
         [array((rows, HEAD), bf16)] * 2,
         [act, state, intra, norm_gain.reshape(heads, HEAD), *got],
-        [VMEM] * 2, [VMEM] * (4 + len(got)),
+        [VMEM] * 2, [VMEM] * (4 + len(got)), flops=rows * HEAD * 1000000,
     )
     normed_got = flip(normed_other, "seq", blocks, 1)
 

time: 43.5 us -> 42.8 us (0.984)
  transfers between devices with their start and end apart: 17 -> 17, of which waited for: 6 -> 6; matrix products, arithmetic and copies ran while one was open for 0% -> 0% of each run, Pallas kernels for 14% -> 15%
where the time goes in v1:
time: 42.8 us; the launch traced here: 42.6 us
  starting transfers between devices  19 us (44%)
  waiting for transfers between devices  15.6 us (36%)
  Pallas kernels  7.88 us (18%)
    ppermute x17, starting transfers between devices, flip(): return lax.ppermute(x, axis, [(i, i ^ mask) for i in range(size)])  19 us
    ppermute x17, waiting for transfers between devices, flip(): return lax.ppermute(x, axis, [(i, i ^ mask) for i in range(size)])  15.6 us
    pallas_call x10, Pallas kernels, call(): pl.pallas_call(kernel, out_shape=outs, in_specs=in_specs, out_specs=out_s...  7.88 us
  transfers between devices with their start and end apart: 17, of which 6 were waited for; matrix products, arithmetic and copies ran while one was open for 0% of the time, Pallas kernels for 15%

profile of v1, /device:TPU:0, one launch (start us, length us, event | category | flops | bytes accessed | tf_op | source)
XLA Modules:
  0.0 42.6 jit_solution(4049661709377466428)
XLA Ops:
  0.0 0.5 %collective-permute-start = (bf16[256,4096]{1,0:T(8,128)(2,1)}, bf16[256,4096]{1,0:T(8,128)(2,1)S(1)}, u32[]{:S(2)}, u32[]{:S(2)}) collective-permute-start(bf16[256,4096]{1,0:T(8,128)(2,1)} %bitcast.3), channel_id=1, source_target_pairs={{0,1},{1,0},{2,3},{3,2},{4,5},{5,4},{6,7},{7,6},{8,9},{9,8},{10,11... | collective-permute-start | bytes 6291464 | tf_op jit(solution)/shard_map/ppermute | solution.py:20
  0.5 1.1 %shard_map.46 = bf16[256,384]{1,0:T(8,128)(2,1)S(1)} custom-call(bf16[1024,768]{1,0:T(8,128)(2,1)} %w_qkv.3), custom_call_target="tpu_custom_call" | custom-call | tf_op jit(solution)/shard_map/pallas_call | solution.py:180
  1.6 3.5 %collective-permute-start.1 = (bf16[256,384]{1,0:T(8,128)(2,1)S(1)}, bf16[256,384]{1,0:T(8,128)(2,1)S(1)}, u32[]{:S(2)}, u32[]{:S(2)}) collective-permute-start(bf16[256,384]{1,0:T(8,128)(2,1)S(1)} %shard_map.46), channel_id=1, source_target_pairs={{0,24},{8,16},{16,8},{24,0},{1,25},{9,17},{17,9},{25,1},{2,26},{10... | collective-permute-start | bytes 589832 | tf_op jit(solution)/shard_map/ppermute | solution.py:20
  5.1 1.1 %shard_map.47.refs_0_ = bf16[1024,384]{1,0:T(8,128)(2,1)S(1)} custom-call(bf16[1024,768]{1,0:T(8,128)(2,1)} %w_qkv.3), custom_call_target="tpu_custom_call" | custom-call | tf_op jit(solution)/shard_map/pallas_call | solution.py:180
  6.2 0.0 copy-start.1
  6.2 0.6 %collective-permute-start.4 = (bf16[1024,384]{1,0:T(8,128)(2,1)S(1)}, bf16[1024,384]{1,0:T(8,128)(2,1)S(1)}, u32[]{:S(2)}, u32[]{:S(2)}) collective-permute-start(bf16[1024,384]{1,0:T(8,128)(2,1)S(1)} %shard_map.47.refs_0_), channel_id=1, source_target_pairs={{0,8},{8,0},{16,24},{24,16},{1,9},{9,1},{17,25},{25,17},{2,10},{10... | collective-permute-start | bytes 2359304 | tf_op jit(solution)/shard_map/ppermute | solution.py:20
  6.8 0.1 collective-permute-start.5
  6.9 3.9 %collective-permute-done.1.refs_0_ = bf16[256,384]{1,0:T(8,128)(2,1)S(1)} collective-permute-done((bf16[256,384]{1,0:T(8,128)(2,1)S(1)}, bf16[256,384]{1,0:T(8,128)(2,1)S(1)}, u32[]{:S(2)}, u32[]{:S(2)}) %collective-permute-start.1) | collective-permute-done | bytes 196640 | tf_op jit(solution)/shard_map/ppermute | solution.py:20
  10.8 3.0 %collective-permute-start.2 = (bf16[256,384]{1,0:T(8,128)(2,1)S(1)}, bf16[256,384]{1,0:T(8,128)(2,1)S(1)}, u32[]{:S(2)}, u32[]{:S(2)}) collective-permute-start(bf16[256,384]{1,0:T(8,128)(2,1)S(1)} %collective-permute-done.1.refs_0_), channel_id=1, source_target_pairs={{0,4},{1,5},{2,6},{3,7},{4,0},{5,1},{6,2},{7,3},{8,12},{9,13},{10,... | collective-permute-start | bytes 589832 | tf_op jit(solution)/shard_map/ppermute | solution.py:20
  13.8 1.6 %collective-permute-start.6 = (bf16[256,384]{1,0:T(8,128)(2,1)S(1)}, bf16[256,384]{1,0:T(8,128)(2,1)S(1)}, u32[]{:S(2)}, u32[]{:S(2)}) collective-permute-start(bf16[256,384]{1,0:T(8,128)(2,1)S(1)} %collective-permute-done.1.refs_0_), channel_id=1, source_target_pairs={{0,2},{1,3},{2,0},{3,1},{4,6},{5,7},{6,4},{7,5},{8,10},{9,11},{10,... | collective-permute-start | bytes 589832 | tf_op jit(solution)/shard_map/ppermute | solution.py:20
  15.4 0.7 %shard_map.48.refs_3_ = f32[512,384]{1,0:T(8,128)S(1)} custom-call(bf16[256,4096]{1,0:T(8,128)(2,1)S(1)} %bitcast.4, bf16[256,4096]{1,0:T(8,128)(2,1)S(1)} %collective-permute-done.tok_b, bf16[1024,384]{1,0:T(8,128)(2,1)S(1)} %shard_map.47.refs_0_), custom_call_target="tpu_custom_call" | custom-call | flops 32768000000 | tf_op jit(solution)/shard_map/pallas_call | solution.py:180
  16.1 6.2 %collective-permute-done.2.refs_1_ = bf16[256,384]{1,0:T(8,128)(2,1)S(1)} collective-permute-done((bf16[256,384]{1,0:T(8,128)(2,1)S(1)}, bf16[256,384]{1,0:T(8,128)(2,1)S(1)}, u32[]{:S(2)}, u32[]{:S(2)}) %collective-permute-start.2) | collective-permute-done | bytes 196640 | tf_op jit(solution)/shard_map/ppermute | solution.py:20
  22.3 0.5 %collective-permute-start.3 = (bf16[256,384]{1,0:T(8,128)(2,1)S(1)}, bf16[256,384]{1,0:T(8,128)(2,1)S(1)}, u32[]{:S(2)}, u32[]{:S(2)}) collective-permute-start(bf16[256,384]{1,0:T(8,128)(2,1)S(1)} %collective-permute-done.2.refs_1_), channel_id=1, source_target_pairs={{0,2},{1,3},{2,0},{3,1},{4,6},{5,7},{6,4},{7,5},{8,10},{9,11},{10,... | collective-permute-start | bytes 589832 | tf_op jit(solution)/shard_map/ppermute | solution.py:20
  22.9 2.6 %collective-permute-start.10 = (bf16[128,512]{1,0:T(8,128)(2,1)S(1)}, bf16[128,512]{1,0:T(8,128)(2,1)S(1)}, u32[]{:S(2)}, u32[]{:S(2)}) collective-permute-start(bf16[128,512]{1,0:T(8,128)(2,1)S(1)} %get-tuple-element.45), channel_id=1, source_target_pairs={{0,24},{8,16},{16,8},{24,0},{1,25},{9,17},{17,9},{25,1},{2,26},{10... | collective-permute-start | bytes 393224 | tf_op jit(solution)/shard_map/ppermute | solution.py:20
  25.4 0.5 %collective-permute-start.7 = (bf16[128,1024]{1,0:T(8,128)(2,1)S(1)}, bf16[128,1024]{1,0:T(8,128)(2,1)S(1)}, u32[]{:S(2)}, u32[]{:S(2)}) collective-permute-start(bf16[128,1024]{1,0:T(8,128)(2,1)S(1)} %get-tuple-element.41.refs_0_), channel_id=1, source_target_pairs={{0,8},{8,0},{16,24},{24,16},{1,9},{9,1},{17,25},{25,17},{2,10},{10... | collective-permute-start | bytes 786440 | tf_op jit(solution)/shard_map/ppermute | solution.py:20
  26.0 0.6 %shard_map.50.refs_2_ = f32[512,384]{1,0:T(8,128)S(1)} custom-call(bf16[256,4096]{1,0:T(8,128)(2,1)S(1)} %bitcast.5, bf16[256,4096]{1,0:T(8,128)(2,1)S(1)} %collective-permute-done.tok_b, bf16[256,384]{1,0:T(8,128)(2,1)S(1)} %collective-permute-done.1.refs_0_, bf16[256,384]{1,0:T(8,128)(2,1)S(1)} %collective-permute-done.2.refs_1_, ...), custom_call_target="tpu_custom_call" | custom-call | flops 32768 | tf_op jit(solution)/shard_map/pallas_call | solution.py:180
  26.5 1.7 %collective-permute-done.4.refs_0_ = bf16[1024,384]{1,0:T(8,128)(2,1)S(1)} collective-permute-done((bf16[1024,384]{1,0:T(8,128)(2,1)S(1)}, bf16[1024,384]{1,0:T(8,128)(2,1)S(1)}, u32[]{:S(2)}, u32[]{:S(2)}) %collective-permute-start.4) | collective-permute-done | bytes 786464 | tf_op jit(solution)/shard_map/ppermute | solution.py:20
  28.2 0.0 collective-permute-start.8
  28.2 1.3 %shard_map.51.refs_1_ = f32[512,384]{1,0:T(8,128)S(1)} custom-call(bf16[256,4096]{1,0:T(8,128)(2,1)S(1)} %bitcast.6, bf16[256,4096]{1,0:T(8,128)(2,1)S(1)} %collective-permute-done.tok_b, bf16[1024,384]{1,0:T(8,128)(2,1)S(1)} %collective-permute-done.4.refs_0_, bf16[1024,384]{1,0:T(8,128)(2,1)S(1)} %collective-permute-done.5.refs_1_, ...), custom_call_target="tpu_custom_call" | custom-call | flops 32768 | tf_op jit(solution)/shard_map/pallas_call | solution.py:180
  29.5 0.5 %shard_map.52 = (bf16[2,256,256]{2,1,0:T(8,128)(2,1)S(1)}, bf16[2,256,128]{2,1,0:T(8,128)(2,1)S(1)}, f32[2,128,128]{2,1,0:T(8,128)S(1)}, bf16[128,128]{1,0:T(8,128)(2,1)S(1)}) custom-call(bf16[256,4096]{1,0:T(8,128)(2,1)S(1)} %bitcast.7, bf16[256,4096]{1,0:T(8,128)(2,1)S(1)} %collective-permute-done.tok_b, ...), custom_call_target="tpu_custom_call" | custom-call | flops 100663296 | tf_op jit(solution)/shard_map/pallas_call | solution.py:180
  30.1 2.1 %collective-permute-start.9 = (bf16[128,128]{1,0:T(8,128)(2,1)S(1)}, bf16[128,128]{1,0:T(8,128)(2,1)S(1)}, u32[]{:S(2)}, u32[]{:S(2)}) collective-permute-start(bf16[128,128]{1,0:T(8,128)(2,1)S(1)} %get-tuple-element.44), channel_id=1, source_target_pairs={{0,2},{1,3},{2,0},{3,1},{4,6},{5,7},{6,4},{7,5},{8,10},{9,11},{10,... | collective-permute-start | bytes 98312 | tf_op jit(solution)/shard_map/ppermute | solution.py:20
  32.1 0.4 collective-permute-start.11
  32.5 1.9 %collective-permute-done.9.refs_0_ = bf16[128,128]{1,0:T(8,128)(2,1)S(1)} collective-permute-done((bf16[128,128]{1,0:T(8,128)(2,1)S(1)}, bf16[128,128]{1,0:T(8,128)(2,1)S(1)}, u32[]{:S(2)}, u32[]{:S(2)}) %collective-permute-start.9) | collective-permute-done | bytes 32800 | tf_op jit(solution)/shard_map/ppermute | solution.py:20
  34.4 3.0 %collective-permute-start.12 = (bf16[128,128]{1,0:T(8,128)(2,1)S(1)}, bf16[128,128]{1,0:T(8,128)(2,1)S(1)}, u32[]{:S(2)}, u32[]{:S(2)}) collective-permute-start(bf16[128,128]{1,0:T(8,128)(2,1)S(1)} %add_convert_fusion), channel_id=1, source_target_pairs={{0,4},{1,5},{2,6},{3,7},{4,0},{5,1},{6,2},{7,3},{8,12},{9,13},{10,... | collective-permute-start | bytes 98312 | tf_op jit(solution)/shard_map/ppermute | solution.py:20
  37.4 0.5 %collective-permute-start.15 = (bf16[128,1024]{1,0:T(8,128)(2,1)S(1)}, bf16[128,1024]{1,0:T(8,128)(2,1)S(1)}, u32[]{:S(2)}, u32[]{:S(2)}) collective-permute-start(bf16[128,1024]{1,0:T(8,128)(2,1)S(1)} %collective-permute-done.8.refs_2_), channel_id=1, source_target_pairs={{0,1},{1,0},{2,3},{3,2},{4,5},{5,4},{6,7},{7,6},{8,9},{9,8},{10,11... | collective-permute-start | bytes 786440 | tf_op jit(solution)/shard_map/ppermute | solution.py:20
  37.9 0.5 %shard_map.53 = (f32[2,256,128]{2,1,0:T(8,128)S(1)}, bf16[128,1024]{1,0:T(8,128)(2,1)S(1)}) custom-call(bf16[2,256,256]{2,1,0:T(8,128)(2,1)S(1)} %get-tuple-element.42.act, bf16[2,256,128]{2,1,0:T(8,128)(2,1)S(1)} %get-tuple-element.43.values, bf16[128,512]{1,0:T(8,128)(2,1)S(1)} %collective-permute-done.10.refs_0_, ...), custom_call_target="tpu_custom_call" | custom-call | flops 32768000000 | tf_op jit(solution)/shard_map/pallas_call | solution.py:180
  38.4 0.1 collective-permute-start.16
  38.6 0.7 %collective-permute-done.12.refs_1_ = bf16[128,128]{1,0:T(8,128)(2,1)S(1)} collective-permute-done((bf16[128,128]{1,0:T(8,128)(2,1)S(1)}, bf16[128,128]{1,0:T(8,128)(2,1)S(1)}, u32[]{:S(2)}, u32[]{:S(2)}) %collective-permute-start.12) | collective-permute-done | bytes 32800 | tf_op jit(solution)/shard_map/ppermute | solution.py:20
  39.3 0.3 shard_map.54
  39.6 0.1 collective-permute-start.13
  39.7 1.2 %collective-permute-done.13.other = bf16[256,128]{1,0:T(8,128)(2,1)S(1)} collective-permute-done((bf16[256,128]{1,0:T(8,128)(2,1)S(1)}, bf16[256,128]{1,0:T(8,128)(2,1)S(1)}, u32[]{:S(2)}, u32[]{:S(2)}) %collective-permute-start.13) | collective-permute-done | bytes 65568 | tf_op jit(solution)/shard_map/ppermute | solution.py:20
  40.9 1.7 %shard_map.55 = bf16[256,4096]{1,0:T(8,128)(2,1)} custom-call(bf16[256,128]{1,0:T(8,128)(2,1)S(1)} %get-tuple-element.49.own, bf16[256,128]{1,0:T(8,128)(2,1)S(1)} %collective-permute-done.13.other, bf16[128,1024]{1,0:T(8,128)(2,1)S(1)} %get-tuple-element.41.refs_0_, bf16[128,1024]{1,0:T(8,128)(2,1)S(1)} %collective-permute-done.7.refs_1_, ...), custom_call_target="tpu_custom_call" | custom-call | flops 536870912 | bytes 2097152 | tf_op jit(solution)/shard_map/pallas_call | solution.py:180
  (19 shorter events, 0.1 us)
Async XLA Ops:
  0.0 15.4 %copy-start = (bf16[1,256,4096]{2,1,0:T(8,128)(2,1)S(1)}, bf16[1,256,4096]{2,1,0:T(8,128)(2,1)}, u32[]{:S(2)}) copy-start(bf16[1,256,4096]{2,1,0:T(8,128)(2,1)} %param.4) | copy-start | bytes 6291460
  0.0 15.4 %collective-permute-start = (bf16[256,4096]{1,0:T(8,128)(2,1)}, bf16[256,4096]{1,0:T(8,128)(2,1)S(1)}, u32[]{:S(2)}, u32[]{:S(2)}) collective-permute-start(bf16[256,4096]{1,0:T(8,128)(2,1)} %bitcast.3), channel_id=1, source_target_pairs={{0,1},{1,0},{2,3},{3,2},{4,5},{5,4},{6,7},{7,6},{8,9},{9,8},{10,11... | collective-permute-start | bytes 6291464 | tf_op jit(solution)/shard_map/ppermute | solution.py:20
  1.6 9.2 %collective-permute-start.1 = (bf16[256,384]{1,0:T(8,128)(2,1)S(1)}, bf16[256,384]{1,0:T(8,128)(2,1)S(1)}, u32[]{:S(2)}, u32[]{:S(2)}) collective-permute-start(bf16[256,384]{1,0:T(8,128)(2,1)S(1)} %shard_map.46), channel_id=1, source_target_pairs={{0,24},{8,16},{16,8},{24,0},{1,25},{9,17},{17,9},{25,1},{2,26},{10... | collective-permute-start | bytes 589832 | tf_op jit(solution)/shard_map/ppermute | solution.py:20
  6.2 16.6 %copy-start.1 = (bf16[256,1024]{1,0:T(8,128)(2,1)S(1)}, bf16[256,1024]{1,0:T(8,128)(2,1)}, u32[]{:S(2)}) copy-start(bf16[256,1024]{1,0:T(8,128)(2,1)} %w_out.1) | copy-start | bytes 1572868
  6.2 22.0 %collective-permute-start.4 = (bf16[1024,384]{1,0:T(8,128)(2,1)S(1)}, bf16[1024,384]{1,0:T(8,128)(2,1)S(1)}, u32[]{:S(2)}, u32[]{:S(2)}) collective-permute-start(bf16[1024,384]{1,0:T(8,128)(2,1)S(1)} %shard_map.47.refs_0_), channel_id=1, source_target_pairs={{0,8},{8,0},{16,24},{24,16},{1,9},{9,1},{17,25},{25,17},{2,10},{10... | collective-permute-start | bytes 2359304 | tf_op jit(solution)/shard_map/ppermute | solution.py:20
  6.8 21.4 %collective-permute-start.5 = (bf16[1024,384]{1,0:T(8,128)(2,1)S(1)}, bf16[1024,384]{1,0:T(8,128)(2,1)S(1)}, u32[]{:S(2)}, u32[]{:S(2)}) collective-permute-start(bf16[1024,384]{1,0:T(8,128)(2,1)S(1)} %shard_map.47.refs_0_), channel_id=1, source_target_pairs={{0,16},{8,24},{16,0},{24,8},{1,17},{9,25},{17,1},{25,9},{2,18},{10... | collective-permute-start | bytes 2359304 | tf_op jit(solution)/shard_map/ppermute | solution.py:20
  10.8 11.5 %collective-permute-start.2 = (bf16[256,384]{1,0:T(8,128)(2,1)S(1)}, bf16[256,384]{1,0:T(8,128)(2,1)S(1)}, u32[]{:S(2)}, u32[]{:S(2)}) collective-permute-start(bf16[256,384]{1,0:T(8,128)(2,1)S(1)} %collective-permute-done.1.refs_0_), channel_id=1, source_target_pairs={{0,4},{1,5},{2,6},{3,7},{4,0},{5,1},{6,2},{7,3},{8,12},{9,13},{10,... | collective-permute-start | bytes 589832 | tf_op jit(solution)/shard_map/ppermute | solution.py:20
  13.8 11.6 %collective-permute-start.6 = (bf16[256,384]{1,0:T(8,128)(2,1)S(1)}, bf16[256,384]{1,0:T(8,128)(2,1)S(1)}, u32[]{:S(2)}, u32[]{:S(2)}) collective-permute-start(bf16[256,384]{1,0:T(8,128)(2,1)S(1)} %collective-permute-done.1.refs_0_), channel_id=1, source_target_pairs={{0,2},{1,3},{2,0},{3,1},{4,6},{5,7},{6,4},{7,5},{8,10},{9,11},{10,... | collective-permute-start | bytes 589832 | tf_op jit(solution)/shard_map/ppermute | solution.py:20
  22.3 7.2 %collective-permute-start.3 = (bf16[256,384]{1,0:T(8,128)(2,1)S(1)}, bf16[256,384]{1,0:T(8,128)(2,1)S(1)}, u32[]{:S(2)}, u32[]{:S(2)}) collective-permute-start(bf16[256,384]{1,0:T(8,128)(2,1)S(1)} %collective-permute-done.2.refs_1_), channel_id=1, source_target_pairs={{0,2},{1,3},{2,0},{3,1},{4,6},{5,7},{6,4},{7,5},{8,10},{9,11},{10,... | collective-permute-start | bytes 589832 | tf_op jit(solution)/shard_map/ppermute | solution.py:20
  22.9 9.3 %collective-permute-start.10 = (bf16[128,512]{1,0:T(8,128)(2,1)S(1)}, bf16[128,512]{1,0:T(8,128)(2,1)S(1)}, u32[]{:S(2)}, u32[]{:S(2)}) collective-permute-start(bf16[128,512]{1,0:T(8,128)(2,1)S(1)} %get-tuple-element.45), channel_id=1, source_target_pairs={{0,24},{8,16},{16,8},{24,0},{1,25},{9,17},{17,9},{25,1},{2,26},{10... | collective-permute-start | bytes 393224 | tf_op jit(solution)/shard_map/ppermute | solution.py:20
  25.4 12.0 %collective-permute-start.7 = (bf16[128,1024]{1,0:T(8,128)(2,1)S(1)}, bf16[128,1024]{1,0:T(8,128)(2,1)S(1)}, u32[]{:S(2)}, u32[]{:S(2)}) collective-permute-start(bf16[128,1024]{1,0:T(8,128)(2,1)S(1)} %get-tuple-element.41.refs_0_), channel_id=1, source_target_pairs={{0,8},{8,0},{16,24},{24,16},{1,9},{9,1},{17,25},{25,17},{2,10},{10... | collective-permute-start | bytes 786440 | tf_op jit(solution)/shard_map/ppermute | solution.py:20
  28.2 9.2 %collective-permute-start.8 = (bf16[128,1024]{1,0:T(8,128)(2,1)S(1)}, bf16[128,1024]{1,0:T(8,128)(2,1)S(1)}, u32[]{:S(2)}, u32[]{:S(2)}) collective-permute-start(bf16[128,1024]{1,0:T(8,128)(2,1)S(1)} %get-tuple-element.41.refs_0_), channel_id=1, source_target_pairs={{0,16},{8,24},{16,0},{24,8},{1,17},{9,25},{17,1},{25,9},{2,18},{10... | collective-permute-start | bytes 786440 | tf_op jit(solution)/shard_map/ppermute | solution.py:20
  30.1 4.3 %collective-permute-start.9 = (bf16[128,128]{1,0:T(8,128)(2,1)S(1)}, bf16[128,128]{1,0:T(8,128)(2,1)S(1)}, u32[]{:S(2)}, u32[]{:S(2)}) collective-permute-start(bf16[128,128]{1,0:T(8,128)(2,1)S(1)} %get-tuple-element.44), channel_id=1, source_target_pairs={{0,2},{1,3},{2,0},{3,1},{4,6},{5,7},{6,4},{7,5},{8,10},{9,11},{10,... | collective-permute-start | bytes 98312 | tf_op jit(solution)/shard_map/ppermute | solution.py:20
  32.1 5.8 %collective-permute-start.11 = (bf16[128,512]{1,0:T(8,128)(2,1)S(1)}, bf16[128,512]{1,0:T(8,128)(2,1)S(1)}, u32[]{:S(2)}, u32[]{:S(2)}) collective-permute-start(bf16[128,512]{1,0:T(8,128)(2,1)S(1)} %collective-permute-done.10.refs_0_), channel_id=1, source_target_pairs={{0,2},{1,3},{2,0},{3,1},{4,6},{5,7},{6,4},{7,5},{8,10},{9,11},{10,... | collective-permute-start | bytes 393224 | tf_op jit(solution)/shard_map/ppermute | solution.py:20
  34.4 4.9 %collective-permute-start.12 = (bf16[128,128]{1,0:T(8,128)(2,1)S(1)}, bf16[128,128]{1,0:T(8,128)(2,1)S(1)}, u32[]{:S(2)}, u32[]{:S(2)}) collective-permute-start(bf16[128,128]{1,0:T(8,128)(2,1)S(1)} %add_convert_fusion), channel_id=1, source_target_pairs={{0,4},{1,5},{2,6},{3,7},{4,0},{5,1},{6,2},{7,3},{8,12},{9,13},{10,... | collective-permute-start | bytes 98312 | tf_op jit(solution)/shard_map/ppermute | solution.py:20
  37.4 3.5 %collective-permute-start.14 = (bf16[128,1024]{1,0:T(8,128)(2,1)S(1)}, bf16[128,1024]{1,0:T(8,128)(2,1)S(1)}, u32[]{:S(2)}, u32[]{:S(2)}) collective-permute-start(bf16[128,1024]{1,0:T(8,128)(2,1)S(1)} %collective-permute-done.7.refs_1_), channel_id=1, source_target_pairs={{0,1},{1,0},{2,3},{3,2},{4,5},{5,4},{6,7},{7,6},{8,9},{9,8},{10,11... | collective-permute-start | bytes 786440 | tf_op jit(solution)/shard_map/ppermute | solution.py:20
  37.4 3.5 %collective-permute-start.15 = (bf16[128,1024]{1,0:T(8,128)(2,1)S(1)}, bf16[128,1024]{1,0:T(8,128)(2,1)S(1)}, u32[]{:S(2)}, u32[]{:S(2)}) collective-permute-start(bf16[128,1024]{1,0:T(8,128)(2,1)S(1)} %collective-permute-done.8.refs_2_), channel_id=1, source_target_pairs={{0,1},{1,0},{2,3},{3,2},{4,5},{5,4},{6,7},{7,6},{8,9},{9,8},{10,11... | collective-permute-start | bytes 786440 | tf_op jit(solution)/shard_map/ppermute | solution.py:20
  37.9 1.4 %copy-start.2 = (f32[256]{0:T(256)S(1)}, f32[256]{0:T(256)}, u32[]{:S(2)}) copy-start(f32[256]{0:T(256)} %param.6) | copy-start | bytes 3076
  38.4 2.5 %collective-permute-start.16 = (bf16[128,1024]{1,0:T(8,128)(2,1)S(1)}, bf16[128,1024]{1,0:T(8,128)(2,1)S(1)}, u32[]{:S(2)}, u32[]{:S(2)}) collective-permute-start(bf16[128,1024]{1,0:T(8,128)(2,1)S(1)} %get-tuple-element.53.refs_3_), channel_id=1, source_target_pairs={{0,1},{1,0},{2,3},{3,2},{4,5},{5,4},{6,7},{7,6},{8,9},{9,8},{10,11... | collective-permute-start | bytes 786440 | tf_op jit(solution)/shard_map/ppermute | solution.py:20
  39.6 1.3 %collective-permute-start.13 = (bf16[256,128]{1,0:T(8,128)(2,1)S(1)}, bf16[256,128]{1,0:T(8,128)(2,1)S(1)}, u32[]{:S(2)}, u32[]{:S(2)}) collective-permute-start(bf16[256,128]{1,0:T(8,128)(2,1)S(1)} %get-tuple-element.50), channel_id=1, source_target_pairs={{0,1},{1,0},{2,3},{3,2},{4,5},{5,4},{6,7},{7,6},{8,9},{9,8},{10,11... | collective-permute-start | bytes 196616 | tf_op jit(solution)/shard_map/ppermute | solution.py:20

commit v2 on v1

--- a/solution.py
+++ b/solution.py
@@ -36,7 +36,8 @@
     return lax.rem(lax.axis_index("seq") // CORES, 4)
 
 
-def cut_qkv(first, w_qkv, out, sem):
+def cut_qkv(first, w_qkv, out, *refs):
+    pieces, sem = refs[:-1], refs[-1]
     _, core = position()
     feat = w_qkv.shape[1] // 3
     rows = pl.ds(pl.multiple_of(first(), 16), out.shape[0])
@@ -48,6 +49,10 @@
         copies[-1].start()
     for copy in copies:
         copy.wait()
+    at = 0
+    for piece in pieces:
+        piece[...] = out[at : at + piece.shape[0], :]
+        at += piece.shape[0]
 
 
 def cut_out(w_out, mine, theirs, part):
@@ -74,6 +79,11 @@
 def places_near(shard, offsets):
     at = lax.axis_index("dp")
     return [(at ^ offset) * shard for offset in offsets]
+
+
+def places_last(shard):
+    near_x, near_y = places_near(shard, (1, 2))
+    return [near_x + 3 * (shard // 4), near_y]
 
 
 def places_far(shard):
@@ -204,9 +214,10 @@
     width = w_out.shape[1]
     grid = n == 4 and blocks % (4 * CORES) == 0 and shard % 512 == 0 and width % 256 == 0
 
-    def cut(first, size, limit):
+    def cut(first, limit, *sizes):
         return call(
-            functools.partial(cut_qkv, first), array((size, 3 * HEAD), bf16), [w_qkv], VMEM, [HBM],
+            functools.partial(cut_qkv, first),
+            [array((size, 3 * HEAD), bf16) for size in sizes], [w_qkv], [VMEM] * len(sizes), [HBM],
             scratch=[pltpu.SemaphoreType.DMA((3,))], limit=limit,
         )
 
@@ -217,15 +228,18 @@
     total = None
     if grid:
         quarter = shard // 4
-        part = cut(lambda: quarter_of() * quarter, quarter, FIRST_LIMIT)
+        part = cut(lambda: quarter_of() * quarter, FIRST_LIMIT, quarter)[0]
         far = [flip(part, "dp", n, 3)]
-        own = cut(lambda: 0, shard, CUT_LIMIT)
-        from_x = flip(own, "dp", n, 1)
+        own, most, last = cut(lambda: 0, CUT_LIMIT, shard, 3 * quarter, quarter)
+        x_most = flip(most, "dp", n, 1)
+        send_last, here = lax.optimization_barrier((last, far[0]))
+        x_last = flip(send_last, "dp", n, 1)
         from_y = flip(own, "dp", n, 2)
         far.append(flip(far[0], "seq", blocks, CORES * 2))
-        far.append(flip(far[0], "seq", blocks, CORES))
         here, own = lax.optimization_barrier((far[0], own))
         total = add_product([own], functools.partial(places_near, shard, (0,)))
+        send_far, total = lax.optimization_barrier((far[0], total))
+        far.append(flip(send_far, "seq", blocks, CORES))
         passed, total = lax.optimization_barrier((far[1], total))
         far.append(flip(passed, "seq", blocks, CORES))
         own_mine, own_theirs, own_part = out_cut()
@@ -235,11 +249,13 @@
         sent, total, far[1] = lax.optimization_barrier((own_mine, total, far[1]))
         out_x = flip(sent, "dp", n, 1)
         out_y = flip(sent, "dp", n, 2)
-        total = add_product(far[:3], lambda: places_far(shard)[:3], total)
-        total = add_product([from_x, from_y], functools.partial(places_near, shard, (1, 2)), total)
+        total = add_product(
+            [x_most, *far[:3]], lambda: places_near(shard, (1,)) + places_far(shard)[:3], total
+        )
+        total = add_product([x_last, from_y], functools.partial(places_last, shard), total)
         pieces, places = far[3:], lambda: places_far(shard)[3:]
     else:
-        whole = cut(lambda: 0, shard, CUT_LIMIT)
+        whole = cut(lambda: 0, CUT_LIMIT, shard)[0]
         pieces, places = [lax.all_gather(whole, "dp", axis=0, tiled=True)], lambda: [0]
     extra = [] if total is None else [total]
 

time: 42.8 us -> 42.6 us (level)
  waiting for transfers between devices: 15.6 us -> 14.3 us
  starting transfers between devices: 19 us -> 20 us
    ppermute x17 -> x18, waiting for transfers between devices: 15.6 us -> 14.3 us  [flip(): return lax.ppermute(x, axis, [(i, i ^ mask) for i in range(size)])]
    ppermute x17 -> x18, starting transfers between devices: 19 us -> 20 us  [flip(): return lax.ppermute(x, axis, [(i, i ^ mask) for i in range(size)])]
  transfers between devices with their start and end apart: 17 -> 18, of which waited for: 6 -> 7; matrix products, arithmetic and copies ran while one was open for 0% -> 0% of each run, Pallas kernels for 15% -> 15%
where the time goes in v2:
time: 42.6 us; the launch traced here: 42.4 us
  starting transfers between devices  20 us (47%)
  waiting for transfers between devices  14.3 us (34%)
  Pallas kernels  7.96 us (19%)
    ppermute x18, starting transfers between devices, flip(): return lax.ppermute(x, axis, [(i, i ^ mask) for i in range(size)])  20 us
    ppermute x18, waiting for transfers between devices, flip(): return lax.ppermute(x, axis, [(i, i ^ mask) for i in range(size)])  14.3 us
    pallas_call x10, Pallas kernels, call(): pl.pallas_call(kernel, out_shape=outs, in_specs=in_specs, out_specs=out_s...  7.96 us
  transfers between devices with their start and end apart: 18, of which 7 were waited for; matrix products, arithmetic and copies ran while one was open for 0% of the time, Pallas kernels for 15%

profile of v2, /device:TPU:0, one launch (start us, length us, event | category | flops | bytes accessed | tf_op | source)
XLA Modules:
  0.0 42.4 jit_solution(10447243957366682899)
XLA Ops:
  0.0 0.5 %collective-permute-start = (bf16[256,4096]{1,0:T(8,128)(2,1)}, bf16[256,4096]{1,0:T(8,128)(2,1)S(1)}, u32[]{:S(2)}, u32[]{:S(2)}) collective-permute-start(bf16[256,4096]{1,0:T(8,128)(2,1)} %bitcast.3), channel_id=1, source_target_pairs={{0,1},{1,0},{2,3},{3,2},{4,5},{5,4},{6,7},{7,6},{8,9},{9,8},{10,11... | collective-permute-start | bytes 6291464 | tf_op jit(solution)/shard_map/ppermute | solution.py:20
  0.5 1.1 %shard_map.46 = bf16[256,384]{1,0:T(8,128)(2,1)S(1)} custom-call(bf16[1024,768]{1,0:T(8,128)(2,1)} %w_qkv.3), custom_call_target="tpu_custom_call" | custom-call | tf_op jit(solution)/shard_map/pallas_call | solution.py:190
  1.6 3.5 %collective-permute-start.1 = (bf16[256,384]{1,0:T(8,128)(2,1)S(1)}, bf16[256,384]{1,0:T(8,128)(2,1)S(1)}, u32[]{:S(2)}, u32[]{:S(2)}) collective-permute-start(bf16[256,384]{1,0:T(8,128)(2,1)S(1)} %shard_map.46), channel_id=1, source_target_pairs={{0,24},{8,16},{16,8},{24,0},{1,25},{9,17},{17,9},{25,1},{2,26},{10... | collective-permute-start | bytes 589832 | tf_op jit(solution)/shard_map/ppermute | solution.py:20
  5.1 1.2 %shard_map.47 = (bf16[1024,384]{1,0:T(8,128)(2,1)S(1)}, bf16[768,384]{1,0:T(8,128)(2,1)S(1)}, bf16[256,384]{1,0:T(8,128)(2,1)S(1)}) custom-call(bf16[1024,768]{1,0:T(8,128)(2,1)} %w_qkv.3), custom_call_target="tpu_custom_call" | custom-call | tf_op jit(solution)/shard_map/pallas_call | solution.py:190
  6.3 0.6 %collective-permute-start.6 = (bf16[768,384]{1,0:T(8,128)(2,1)S(1)}, bf16[768,384]{1,0:T(8,128)(2,1)S(1)}, u32[]{:S(2)}, u32[]{:S(2)}) collective-permute-start(bf16[768,384]{1,0:T(8,128)(2,1)S(1)} %get-tuple-element.42), channel_id=1, source_target_pairs={{0,8},{8,0},{16,24},{24,16},{1,9},{9,1},{17,25},{25,17},{2,10},{10... | collective-permute-start | bytes 1769480 | tf_op jit(solution)/shard_map/ppermute | solution.py:20
  7.0 3.9 %collective-permute-done.1.refs_1_ = bf16[256,384]{1,0:T(8,128)(2,1)S(1)} collective-permute-done((bf16[256,384]{1,0:T(8,128)(2,1)S(1)}, bf16[256,384]{1,0:T(8,128)(2,1)S(1)}, u32[]{:S(2)}, u32[]{:S(2)}) %collective-permute-start.1) | collective-permute-done | bytes 196640 | tf_op jit(solution)/shard_map/ppermute | solution.py:20
  10.8 3.0 %collective-permute-start.2 = (bf16[256,384]{1,0:T(8,128)(2,1)S(1)}, bf16[256,384]{1,0:T(8,128)(2,1)S(1)}, u32[]{:S(2)}, u32[]{:S(2)}) collective-permute-start(bf16[256,384]{1,0:T(8,128)(2,1)S(1)} %collective-permute-done.1.refs_1_), channel_id=1, source_target_pairs={{0,4},{1,5},{2,6},{3,7},{4,0},{5,1},{6,2},{7,3},{8,12},{9,13},{10,... | collective-permute-start | bytes 589832 | tf_op jit(solution)/shard_map/ppermute | solution.py:20
  13.8 0.7 %shard_map.48.refs_4_ = f32[512,384]{1,0:T(8,128)S(1)} custom-call(bf16[256,4096]{1,0:T(8,128)(2,1)S(1)} %bitcast.4, bf16[256,4096]{1,0:T(8,128)(2,1)S(1)} %collective-permute-done.tok_b, bf16[1024,384]{1,0:T(8,128)(2,1)S(1)} %get-tuple-element.37.refs_0_), custom_call_target="tpu_custom_call" | custom-call | flops 32768000000 | tf_op jit(solution)/shard_map/pallas_call | solution.py:190
  14.5 1.6 %collective-permute-start.7 = (bf16[256,384]{1,0:T(8,128)(2,1)S(1)}, bf16[256,384]{1,0:T(8,128)(2,1)S(1)}, u32[]{:S(2)}, u32[]{:S(2)}) collective-permute-start(bf16[256,384]{1,0:T(8,128)(2,1)S(1)} %collective-permute-done.1.refs_1_), channel_id=1, source_target_pairs={{0,2},{1,3},{2,0},{3,1},{4,6},{5,7},{6,4},{7,5},{8,10},{9,11},{10,... | collective-permute-start | bytes 589832 | tf_op jit(solution)/shard_map/ppermute | solution.py:20
  16.2 1.5 %collective-permute-start.4 = (bf16[256,384]{1,0:T(8,128)(2,1)S(1)}, bf16[256,384]{1,0:T(8,128)(2,1)S(1)}, u32[]{:S(2)}, u32[]{:S(2)}) collective-permute-start(bf16[256,384]{1,0:T(8,128)(2,1)S(1)} %get-tuple-element.41), channel_id=1, source_target_pairs={{0,8},{8,0},{16,24},{24,16},{1,9},{9,1},{17,25},{25,17},{2,10},{10... | collective-permute-start | bytes 589832 | tf_op jit(solution)/shard_map/ppermute | solution.py:20
  17.7 4.6 %collective-permute-done.2.refs_2_ = bf16[256,384]{1,0:T(8,128)(2,1)S(1)} collective-permute-done((bf16[256,384]{1,0:T(8,128)(2,1)S(1)}, bf16[256,384]{1,0:T(8,128)(2,1)S(1)}, u32[]{:S(2)}, u32[]{:S(2)}) %collective-permute-start.2) | collective-permute-done | bytes 196640 | tf_op jit(solution)/shard_map/ppermute | solution.py:20
  22.3 0.6 %collective-permute-start.3 = (bf16[256,384]{1,0:T(8,128)(2,1)S(1)}, bf16[256,384]{1,0:T(8,128)(2,1)S(1)}, u32[]{:S(2)}, u32[]{:S(2)}) collective-permute-start(bf16[256,384]{1,0:T(8,128)(2,1)S(1)} %collective-permute-done.2.refs_2_), channel_id=1, source_target_pairs={{0,2},{1,3},{2,0},{3,1},{4,6},{5,7},{6,4},{7,5},{8,10},{9,11},{10,... | collective-permute-start | bytes 589832 | tf_op jit(solution)/shard_map/ppermute | solution.py:20
  22.9 1.1 %collective-permute-done.6.refs_0_ = bf16[768,384]{1,0:T(8,128)(2,1)S(1)} collective-permute-done((bf16[768,384]{1,0:T(8,128)(2,1)S(1)}, bf16[768,384]{1,0:T(8,128)(2,1)S(1)}, u32[]{:S(2)}, u32[]{:S(2)}) %collective-permute-start.6) | collective-permute-done | bytes 589856 | tf_op jit(solution)/shard_map/ppermute | solution.py:20
  24.0 1.5 %collective-permute-start.11 = (bf16[128,512]{1,0:T(8,128)(2,1)S(1)}, bf16[128,512]{1,0:T(8,128)(2,1)S(1)}, u32[]{:S(2)}, u32[]{:S(2)}) collective-permute-start(bf16[128,512]{1,0:T(8,128)(2,1)S(1)} %get-tuple-element.57), channel_id=1, source_target_pairs={{0,24},{8,16},{16,8},{24,0},{1,25},{9,17},{17,9},{25,1},{2,26},{10... | collective-permute-start | bytes 393224 | tf_op jit(solution)/shard_map/ppermute | solution.py:20
  25.5 0.5 %collective-permute-start.8 = (bf16[128,1024]{1,0:T(8,128)(2,1)S(1)}, bf16[128,1024]{1,0:T(8,128)(2,1)S(1)}, u32[]{:S(2)}, u32[]{:S(2)}) collective-permute-start(bf16[128,1024]{1,0:T(8,128)(2,1)S(1)} %get-tuple-element.53.refs_0_), channel_id=1, source_target_pairs={{0,8},{8,0},{16,24},{24,16},{1,9},{9,1},{17,25},{25,17},{2,10},{10... | collective-permute-start | bytes 786440 | tf_op jit(solution)/shard_map/ppermute | solution.py:20
  26.0 1.0 %shard_map.50.refs_2_ = f32[512,384]{1,0:T(8,128)S(1)} custom-call(bf16[256,4096]{1,0:T(8,128)(2,1)S(1)} %bitcast.5, bf16[256,4096]{1,0:T(8,128)(2,1)S(1)} %collective-permute-done.tok_b, bf16[768,384]{1,0:T(8,128)(2,1)S(1)} %collective-permute-done.6.refs_0_, bf16[256,384]{1,0:T(8,128)(2,1)S(1)} %collective-permute-done.1.refs_1_, ...), custom_call_target="tpu_custom_call" | custom-call | flops 32768 | tf_op jit(solution)/shard_map/pallas_call | solution.py:190
  27.0 1.2 %collective-permute-done.4.refs_0_ = bf16[256,384]{1,0:T(8,128)(2,1)S(1)} collective-permute-done((bf16[256,384]{1,0:T(8,128)(2,1)S(1)}, bf16[256,384]{1,0:T(8,128)(2,1)S(1)}, u32[]{:S(2)}, u32[]{:S(2)}) %collective-permute-start.4) | collective-permute-done | bytes 196640 | tf_op jit(solution)/shard_map/ppermute | solution.py:20
  28.2 0.3 collective-permute-start.9
  28.5 0.9 %shard_map.51.refs_1_ = f32[512,384]{1,0:T(8,128)S(1)} custom-call(bf16[256,4096]{1,0:T(8,128)(2,1)S(1)} %bitcast.6, bf16[256,4096]{1,0:T(8,128)(2,1)S(1)} %collective-permute-done.tok_b, bf16[256,384]{1,0:T(8,128)(2,1)S(1)} %collective-permute-done.4.refs_0_, bf16[1024,384]{1,0:T(8,128)(2,1)S(1)} %collective-permute-done.5.refs_1_, ...), custom_call_target="tpu_custom_call" | custom-call | flops 32768 | tf_op jit(solution)/shard_map/pallas_call | solution.py:190
  29.4 0.5 %shard_map.52 = (bf16[2,256,256]{2,1,0:T(8,128)(2,1)S(1)}, bf16[2,256,128]{2,1,0:T(8,128)(2,1)S(1)}, f32[2,128,128]{2,1,0:T(8,128)S(1)}, bf16[128,128]{1,0:T(8,128)(2,1)S(1)}) custom-call(bf16[256,4096]{1,0:T(8,128)(2,1)S(1)} %bitcast.7, bf16[256,4096]{1,0:T(8,128)(2,1)S(1)} %collective-permute-done.tok_b, ...), custom_call_target="tpu_custom_call" | custom-call | flops 100663296 | tf_op jit(solution)/shard_map/pallas_call | solution.py:190
  30.0 1.8 %collective-permute-start.10 = (bf16[128,128]{1,0:T(8,128)(2,1)S(1)}, bf16[128,128]{1,0:T(8,128)(2,1)S(1)}, u32[]{:S(2)}, u32[]{:S(2)}) collective-permute-start(bf16[128,128]{1,0:T(8,128)(2,1)S(1)} %get-tuple-element.56), channel_id=1, source_target_pairs={{0,2},{1,3},{2,0},{3,1},{4,6},{5,7},{6,4},{7,5},{8,10},{9,11},{10,... | collective-permute-start | bytes 98312 | tf_op jit(solution)/shard_map/ppermute | solution.py:20
  31.7 1.2 %collective-permute-start.12 = (bf16[128,512]{1,0:T(8,128)(2,1)S(1)}, bf16[128,512]{1,0:T(8,128)(2,1)S(1)}, u32[]{:S(2)}, u32[]{:S(2)}) collective-permute-start(bf16[128,512]{1,0:T(8,128)(2,1)S(1)} %collective-permute-done.11.refs_0_), channel_id=1, source_target_pairs={{0,2},{1,3},{2,0},{3,1},{4,6},{5,7},{6,4},{7,5},{8,10},{9,11},{10,... | collective-permute-start | bytes 393224 | tf_op jit(solution)/shard_map/ppermute | solution.py:20
  32.9 1.3 %collective-permute-done.10.refs_0_ = bf16[128,128]{1,0:T(8,128)(2,1)S(1)} collective-permute-done((bf16[128,128]{1,0:T(8,128)(2,1)S(1)}, bf16[128,128]{1,0:T(8,128)(2,1)S(1)}, u32[]{:S(2)}, u32[]{:S(2)}) %collective-permute-start.10) | collective-permute-done | bytes 32800 | tf_op jit(solution)/shard_map/ppermute | solution.py:20
  34.2 2.7 %collective-permute-start.13 = (bf16[128,128]{1,0:T(8,128)(2,1)S(1)}, bf16[128,128]{1,0:T(8,128)(2,1)S(1)}, u32[]{:S(2)}, u32[]{:S(2)}) collective-permute-start(bf16[128,128]{1,0:T(8,128)(2,1)S(1)} %add_convert_fusion), channel_id=1, source_target_pairs={{0,4},{1,5},{2,6},{3,7},{4,0},{5,1},{6,2},{7,3},{8,12},{9,13},{10,... | collective-permute-start | bytes 98312 | tf_op jit(solution)/shard_map/ppermute | solution.py:20
  36.9 0.5 %collective-permute-start.16 = (bf16[128,1024]{1,0:T(8,128)(2,1)S(1)}, bf16[128,1024]{1,0:T(8,128)(2,1)S(1)}, u32[]{:S(2)}, u32[]{:S(2)}) collective-permute-start(bf16[128,1024]{1,0:T(8,128)(2,1)S(1)} %collective-permute-done.9.refs_2_), channel_id=1, source_target_pairs={{0,1},{1,0},{2,3},{3,2},{4,5},{5,4},{6,7},{7,6},{8,9},{9,8},{10,11... | collective-permute-start | bytes 786440 | tf_op jit(solution)/shard_map/ppermute | solution.py:20
  37.4 0.5 %shard_map.53 = (f32[2,256,128]{2,1,0:T(8,128)S(1)}, bf16[128,1024]{1,0:T(8,128)(2,1)S(1)}) custom-call(bf16[2,256,256]{2,1,0:T(8,128)(2,1)S(1)} %get-tuple-element.54.act, bf16[2,256,128]{2,1,0:T(8,128)(2,1)S(1)} %get-tuple-element.55.values, bf16[128,512]{1,0:T(8,128)(2,1)S(1)} %collective-permute-done.11.refs_0_, ...), custom_call_target="tpu_custom_call" | custom-call | flops 32768000000 | tf_op jit(solution)/shard_map/pallas_call | solution.py:190
  37.9 0.1 collective-permute-start.17
  38.0 1.0 %collective-permute-done.13.refs_1_ = bf16[128,128]{1,0:T(8,128)(2,1)S(1)} collective-permute-done((bf16[128,128]{1,0:T(8,128)(2,1)S(1)}, bf16[128,128]{1,0:T(8,128)(2,1)S(1)}, u32[]{:S(2)}, u32[]{:S(2)}) %collective-permute-start.13) | collective-permute-done | bytes 32800 | tf_op jit(solution)/shard_map/ppermute | solution.py:20
  39.1 0.3 shard_map.54
  39.4 0.1 collective-permute-start.14
  39.5 1.2 %collective-permute-done.14.other = bf16[256,128]{1,0:T(8,128)(2,1)S(1)} collective-permute-done((bf16[256,128]{1,0:T(8,128)(2,1)S(1)}, bf16[256,128]{1,0:T(8,128)(2,1)S(1)}, u32[]{:S(2)}, u32[]{:S(2)}) %collective-permute-start.14) | collective-permute-done | bytes 65568 | tf_op jit(solution)/shard_map/ppermute | solution.py:20
  40.7 1.7 %shard_map.55 = bf16[256,4096]{1,0:T(8,128)(2,1)} custom-call(bf16[256,128]{1,0:T(8,128)(2,1)S(1)} %get-tuple-element.61.own, bf16[256,128]{1,0:T(8,128)(2,1)S(1)} %collective-permute-done.14.other, bf16[128,1024]{1,0:T(8,128)(2,1)S(1)} %get-tuple-element.53.refs_0_, bf16[128,1024]{1,0:T(8,128)(2,1)S(1)} %collective-permute-done.8.refs_1_, ...), custom_call_target="tpu_custom_call" | custom-call | flops 536870912 | bytes 2097152 | tf_op jit(solution)/shard_map/pallas_call | solution.py:190
  (21 shorter events, 0.2 us)
Async XLA Ops:
  0.0 13.8 %copy-start = (bf16[1,256,4096]{2,1,0:T(8,128)(2,1)S(1)}, bf16[1,256,4096]{2,1,0:T(8,128)(2,1)}, u32[]{:S(2)}) copy-start(bf16[1,256,4096]{2,1,0:T(8,128)(2,1)} %param.4) | copy-start | bytes 6291460
  0.0 13.8 %collective-permute-start = (bf16[256,4096]{1,0:T(8,128)(2,1)}, bf16[256,4096]{1,0:T(8,128)(2,1)S(1)}, u32[]{:S(2)}, u32[]{:S(2)}) collective-permute-start(bf16[256,4096]{1,0:T(8,128)(2,1)} %bitcast.3), channel_id=1, source_target_pairs={{0,1},{1,0},{2,3},{3,2},{4,5},{5,4},{6,7},{7,6},{8,9},{9,8},{10,11... | collective-permute-start | bytes 6291464 | tf_op jit(solution)/shard_map/ppermute | solution.py:20
  1.6 9.2 %collective-permute-start.1 = (bf16[256,384]{1,0:T(8,128)(2,1)S(1)}, bf16[256,384]{1,0:T(8,128)(2,1)S(1)}, u32[]{:S(2)}, u32[]{:S(2)}) collective-permute-start(bf16[256,384]{1,0:T(8,128)(2,1)S(1)} %shard_map.46), channel_id=1, source_target_pairs={{0,24},{8,16},{16,8},{24,0},{1,25},{9,17},{17,9},{25,1},{2,26},{10... | collective-permute-start | bytes 589832 | tf_op jit(solution)/shard_map/ppermute | solution.py:20
  6.3 17.7 %collective-permute-start.6 = (bf16[768,384]{1,0:T(8,128)(2,1)S(1)}, bf16[768,384]{1,0:T(8,128)(2,1)S(1)}, u32[]{:S(2)}, u32[]{:S(2)}) collective-permute-start(bf16[768,384]{1,0:T(8,128)(2,1)S(1)} %get-tuple-element.42), channel_id=1, source_target_pairs={{0,8},{8,0},{16,24},{24,16},{1,9},{9,1},{17,25},{25,17},{2,10},{10... | collective-permute-start | bytes 1769480 | tf_op jit(solution)/shard_map/ppermute | solution.py:20
  6.9 16.0 %copy-start.1 = (bf16[256,1024]{1,0:T(8,128)(2,1)S(1)}, bf16[256,1024]{1,0:T(8,128)(2,1)}, u32[]{:S(2)}) copy-start(bf16[256,1024]{1,0:T(8,128)(2,1)} %w_out.1) | copy-start | bytes 1572868
  6.9 21.6 %collective-permute-start.5 = (bf16[1024,384]{1,0:T(8,128)(2,1)S(1)}, bf16[1024,384]{1,0:T(8,128)(2,1)S(1)}, u32[]{:S(2)}, u32[]{:S(2)}) collective-permute-start(bf16[1024,384]{1,0:T(8,128)(2,1)S(1)} %get-tuple-element.37.refs_0_), channel_id=1, source_target_pairs={{0,16},{8,24},{16,0},{24,8},{1,17},{9,25},{17,1},{25,9},{2,18},{10... | collective-permute-start | bytes 2359304 | tf_op jit(solution)/shard_map/ppermute | solution.py:20
  10.8 11.5 %collective-permute-start.2 = (bf16[256,384]{1,0:T(8,128)(2,1)S(1)}, bf16[256,384]{1,0:T(8,128)(2,1)S(1)}, u32[]{:S(2)}, u32[]{:S(2)}) collective-permute-start(bf16[256,384]{1,0:T(8,128)(2,1)S(1)} %collective-permute-done.1.refs_1_), channel_id=1, source_target_pairs={{0,4},{1,5},{2,6},{3,7},{4,0},{5,1},{6,2},{7,3},{8,12},{9,13},{10,... | collective-permute-start | bytes 589832 | tf_op jit(solution)/shard_map/ppermute | solution.py:20
  14.5 10.9 %collective-permute-start.7 = (bf16[256,384]{1,0:T(8,128)(2,1)S(1)}, bf16[256,384]{1,0:T(8,128)(2,1)S(1)}, u32[]{:S(2)}, u32[]{:S(2)}) collective-permute-start(bf16[256,384]{1,0:T(8,128)(2,1)S(1)} %collective-permute-done.1.refs_1_), channel_id=1, source_target_pairs={{0,2},{1,3},{2,0},{3,1},{4,6},{5,7},{6,4},{7,5},{8,10},{9,11},{10,... | collective-permute-start | bytes 589832 | tf_op jit(solution)/shard_map/ppermute | solution.py:20
  16.2 12.0 %collective-permute-start.4 = (bf16[256,384]{1,0:T(8,128)(2,1)S(1)}, bf16[256,384]{1,0:T(8,128)(2,1)S(1)}, u32[]{:S(2)}, u32[]{:S(2)}) collective-permute-start(bf16[256,384]{1,0:T(8,128)(2,1)S(1)} %get-tuple-element.41), channel_id=1, source_target_pairs={{0,8},{8,0},{16,24},{24,16},{1,9},{9,1},{17,25},{25,17},{2,10},{10... | collective-permute-start | bytes 589832 | tf_op jit(solution)/shard_map/ppermute | solution.py:20
  22.3 7.1 %collective-permute-start.3 = (bf16[256,384]{1,0:T(8,128)(2,1)S(1)}, bf16[256,384]{1,0:T(8,128)(2,1)S(1)}, u32[]{:S(2)}, u32[]{:S(2)}) collective-permute-start(bf16[256,384]{1,0:T(8,128)(2,1)S(1)} %collective-permute-done.2.refs_2_), channel_id=1, source_target_pairs={{0,2},{1,3},{2,0},{3,1},{4,6},{5,7},{6,4},{7,5},{8,10},{9,11},{10,... | collective-permute-start | bytes 589832 | tf_op jit(solution)/shard_map/ppermute | solution.py:20
  24.0 7.7 %collective-permute-start.11 = (bf16[128,512]{1,0:T(8,128)(2,1)S(1)}, bf16[128,512]{1,0:T(8,128)(2,1)S(1)}, u32[]{:S(2)}, u32[]{:S(2)}) collective-permute-start(bf16[128,512]{1,0:T(8,128)(2,1)S(1)} %get-tuple-element.57), channel_id=1, source_target_pairs={{0,24},{8,16},{16,8},{24,0},{1,25},{9,17},{17,9},{25,1},{2,26},{10... | collective-permute-start | bytes 393224 | tf_op jit(solution)/shard_map/ppermute | solution.py:20
  25.5 11.4 %collective-permute-start.8 = (bf16[128,1024]{1,0:T(8,128)(2,1)S(1)}, bf16[128,1024]{1,0:T(8,128)(2,1)S(1)}, u32[]{:S(2)}, u32[]{:S(2)}) collective-permute-start(bf16[128,1024]{1,0:T(8,128)(2,1)S(1)} %get-tuple-element.53.refs_0_), channel_id=1, source_target_pairs={{0,8},{8,0},{16,24},{24,16},{1,9},{9,1},{17,25},{25,17},{2,10},{10... | collective-permute-start | bytes 786440 | tf_op jit(solution)/shard_map/ppermute | solution.py:20
  28.2 8.7 %collective-permute-start.9 = (bf16[128,1024]{1,0:T(8,128)(2,1)S(1)}, bf16[128,1024]{1,0:T(8,128)(2,1)S(1)}, u32[]{:S(2)}, u32[]{:S(2)}) collective-permute-start(bf16[128,1024]{1,0:T(8,128)(2,1)S(1)} %get-tuple-element.53.refs_0_), channel_id=1, source_target_pairs={{0,16},{8,24},{16,0},{24,8},{1,17},{9,25},{17,1},{25,9},{2,18},{10... | collective-permute-start | bytes 786440 | tf_op jit(solution)/shard_map/ppermute | solution.py:20
  30.0 4.2 %collective-permute-start.10 = (bf16[128,128]{1,0:T(8,128)(2,1)S(1)}, bf16[128,128]{1,0:T(8,128)(2,1)S(1)}, u32[]{:S(2)}, u32[]{:S(2)}) collective-permute-start(bf16[128,128]{1,0:T(8,128)(2,1)S(1)} %get-tuple-element.56), channel_id=1, source_target_pairs={{0,2},{1,3},{2,0},{3,1},{4,6},{5,7},{6,4},{7,5},{8,10},{9,11},{10,... | collective-permute-start | bytes 98312 | tf_op jit(solution)/shard_map/ppermute | solution.py:20
  31.7 5.7 %collective-permute-start.12 = (bf16[128,512]{1,0:T(8,128)(2,1)S(1)}, bf16[128,512]{1,0:T(8,128)(2,1)S(1)}, u32[]{:S(2)}, u32[]{:S(2)}) collective-permute-start(bf16[128,512]{1,0:T(8,128)(2,1)S(1)} %collective-permute-done.11.refs_0_), channel_id=1, source_target_pairs={{0,2},{1,3},{2,0},{3,1},{4,6},{5,7},{6,4},{7,5},{8,10},{9,11},{10,... | collective-permute-start | bytes 393224 | tf_op jit(solution)/shard_map/ppermute | solution.py:20
  34.2 4.9 %collective-permute-start.13 = (bf16[128,128]{1,0:T(8,128)(2,1)S(1)}, bf16[128,128]{1,0:T(8,128)(2,1)S(1)}, u32[]{:S(2)}, u32[]{:S(2)}) collective-permute-start(bf16[128,128]{1,0:T(8,128)(2,1)S(1)} %add_convert_fusion), channel_id=1, source_target_pairs={{0,4},{1,5},{2,6},{3,7},{4,0},{5,1},{6,2},{7,3},{8,12},{9,13},{10,... | collective-permute-start | bytes 98312 | tf_op jit(solution)/shard_map/ppermute | solution.py:20
  36.9 3.9 %collective-permute-start.15 = (bf16[128,1024]{1,0:T(8,128)(2,1)S(1)}, bf16[128,1024]{1,0:T(8,128)(2,1)S(1)}, u32[]{:S(2)}, u32[]{:S(2)}) collective-permute-start(bf16[128,1024]{1,0:T(8,128)(2,1)S(1)} %collective-permute-done.8.refs_1_), channel_id=1, source_target_pairs={{0,1},{1,0},{2,3},{3,2},{4,5},{5,4},{6,7},{7,6},{8,9},{9,8},{10,11... | collective-permute-start | bytes 786440 | tf_op jit(solution)/shard_map/ppermute | solution.py:20
  36.9 3.9 %collective-permute-start.16 = (bf16[128,1024]{1,0:T(8,128)(2,1)S(1)}, bf16[128,1024]{1,0:T(8,128)(2,1)S(1)}, u32[]{:S(2)}, u32[]{:S(2)}) collective-permute-start(bf16[128,1024]{1,0:T(8,128)(2,1)S(1)} %collective-permute-done.9.refs_2_), channel_id=1, source_target_pairs={{0,1},{1,0},{2,3},{3,2},{4,5},{5,4},{6,7},{7,6},{8,9},{9,8},{10,11... | collective-permute-start | bytes 786440 | tf_op jit(solution)/shard_map/ppermute | solution.py:20
  37.4 1.7 %copy-start.2 = (f32[256]{0:T(256)S(1)}, f32[256]{0:T(256)}, u32[]{:S(2)}) copy-start(f32[256]{0:T(256)} %param.6) | copy-start | bytes 3076
  37.9 2.8 %collective-permute-start.17 = (bf16[128,1024]{1,0:T(8,128)(2,1)S(1)}, bf16[128,1024]{1,0:T(8,128)(2,1)S(1)}, u32[]{:S(2)}, u32[]{:S(2)}) collective-permute-start(bf16[128,1024]{1,0:T(8,128)(2,1)S(1)} %get-tuple-element.65.refs_3_), channel_id=1, source_target_pairs={{0,1},{1,0},{2,3},{3,2},{4,5},{5,4},{6,7},{7,6},{8,9},{9,8},{10,11... | collective-permute-start | bytes 786440 | tf_op jit(solution)/shard_map/ppermute | solution.py:20
  39.4 1.3 %collective-permute-start.14 = (bf16[256,128]{1,0:T(8,128)(2,1)S(1)}, bf16[256,128]{1,0:T(8,128)(2,1)S(1)}, u32[]{:S(2)}, u32[]{:S(2)}) collective-permute-start(bf16[256,128]{1,0:T(8,128)(2,1)S(1)} %get-tuple-element.62), channel_id=1, source_target_pairs={{0,1},{1,0},{2,3},{3,2},{4,5},{5,4},{6,7},{7,6},{8,9},{9,8},{10,11... | collective-permute-start | bytes 196616 | tf_op jit(solution)/shard_map/ppermute | solution.py:20

commit v3 on v2

--- a/solution.py
+++ b/solution.py
@@ -82,8 +82,8 @@
 
 
 def places_last(shard):
-    near_x, near_y = places_near(shard, (1, 2))
-    return [near_x + 3 * (shard // 4), near_y]
+    near_y, near_x = places_near(shard, (2, 1))
+    return [near_y + 3 * (shard // 4), near_x]
 
 
 def places_far(shard):
@@ -231,10 +231,10 @@
         part = cut(lambda: quarter_of() * quarter, FIRST_LIMIT, quarter)[0]
         far = [flip(part, "dp", n, 3)]
         own, most, last = cut(lambda: 0, CUT_LIMIT, shard, 3 * quarter, quarter)
-        x_most = flip(most, "dp", n, 1)
+        y_most = flip(most, "dp", n, 2)
         send_last, here = lax.optimization_barrier((last, far[0]))
-        x_last = flip(send_last, "dp", n, 1)
-        from_y = flip(own, "dp", n, 2)
+        y_last = flip(send_last, "dp", n, 2)
+        from_x = flip(own, "dp", n, 1)
         far.append(flip(far[0], "seq", blocks, CORES * 2))
         here, own = lax.optimization_barrier((far[0], own))
         total = add_product([own], functools.partial(places_near, shard, (0,)))
@@ -250,9 +250,9 @@
         out_x = flip(sent, "dp", n, 1)
         out_y = flip(sent, "dp", n, 2)
         total = add_product(
-            [x_most, *far[:3]], lambda: places_near(shard, (1,)) + places_far(shard)[:3], total
+            [y_most, *far[:3]], lambda: places_near(shard, (2,)) + places_far(shard)[:3], total
         )
-        total = add_product([x_last, from_y], functools.partial(places_last, shard), total)
+        total = add_product([y_last, from_x], functools.partial(places_last, shard), total)
         pieces, places = far[3:], lambda: places_far(shard)[3:]
     else:
         whole = cut(lambda: 0, CUT_LIMIT, shard)[0]

time: 42.6 us -> 43.7 us (1.026)
  starting transfers between devices: 20 us -> 21.6 us
    ppermute x18, starting transfers between devices: 20 us -> 21.6 us  [flip(): return lax.ppermute(x, axis, [(i, i ^ mask) for i in range(size)])]
    ppermute x18, waiting for transfers between devices: 14.3 us -> 13.9 us  [flip(): return lax.ppermute(x, axis, [(i, i ^ mask) for i in range(size)])]
  transfers between devices with their start and end apart: 18 -> 18, of which waited for: 7 -> 7; matrix products, arithmetic and copies ran while one was open for 0% -> 0% of each run, Pallas kernels for 15% -> 14%
where the time goes in v3:
time: 43.7 us; the launch traced here: 43.5 us
  starting transfers between devices  21.6 us (49%)
  waiting for transfers between devices  13.9 us (32%)
  Pallas kernels  7.95 us (18%)
    ppermute x18, starting transfers between devices, flip(): return lax.ppermute(x, axis, [(i, i ^ mask) for i in range(size)])  21.6 us
    ppermute x18, waiting for transfers between devices, flip(): return lax.ppermute(x, axis, [(i, i ^ mask) for i in range(size)])  13.9 us
    pallas_call x10, Pallas kernels, call(): pl.pallas_call(kernel, out_shape=outs, in_specs=in_specs, out_specs=out_s...  7.95 us
  transfers between devices with their start and end apart: 18, of which 7 were waited for; matrix products, arithmetic and copies ran while one was open for 0% of the time, Pallas kernels for 14%

profile of v3, /device:TPU:0, one launch (start us, length us, event | category | flops | bytes accessed | tf_op | source)
XLA Modules:
  0.0 43.5 jit_solution(4098216655915693034)
XLA Ops:
  0.0 0.5 %collective-permute-start = (bf16[256,4096]{1,0:T(8,128)(2,1)}, bf16[256,4096]{1,0:T(8,128)(2,1)S(1)}, u32[]{:S(2)}, u32[]{:S(2)}) collective-permute-start(bf16[256,4096]{1,0:T(8,128)(2,1)} %bitcast.3), channel_id=1, source_target_pairs={{0,1},{1,0},{2,3},{3,2},{4,5},{5,4},{6,7},{7,6},{8,9},{9,8},{10,11... | collective-permute-start | bytes 6291464 | tf_op jit(solution)/shard_map/ppermute | solution.py:20
  0.5 1.1 %shard_map.46 = bf16[256,384]{1,0:T(8,128)(2,1)S(1)} custom-call(bf16[1024,768]{1,0:T(8,128)(2,1)} %w_qkv.3), custom_call_target="tpu_custom_call" | custom-call | tf_op jit(solution)/shard_map/pallas_call | solution.py:190
  1.6 3.5 %collective-permute-start.1 = (bf16[256,384]{1,0:T(8,128)(2,1)S(1)}, bf16[256,384]{1,0:T(8,128)(2,1)S(1)}, u32[]{:S(2)}, u32[]{:S(2)}) collective-permute-start(bf16[256,384]{1,0:T(8,128)(2,1)S(1)} %shard_map.46), channel_id=1, source_target_pairs={{0,24},{8,16},{16,8},{24,0},{1,25},{9,17},{17,9},{25,1},{2,26},{10... | collective-permute-start | bytes 589832 | tf_op jit(solution)/shard_map/ppermute | solution.py:20
  5.1 1.2 %shard_map.47 = (bf16[1024,384]{1,0:T(8,128)(2,1)S(1)}, bf16[768,384]{1,0:T(8,128)(2,1)S(1)}, bf16[256,384]{1,0:T(8,128)(2,1)S(1)}) custom-call(bf16[1024,768]{1,0:T(8,128)(2,1)} %w_qkv.3), custom_call_target="tpu_custom_call" | custom-call | tf_op jit(solution)/shard_map/pallas_call | solution.py:190
  6.3 0.6 %collective-permute-start.6 = (bf16[768,384]{1,0:T(8,128)(2,1)S(1)}, bf16[768,384]{1,0:T(8,128)(2,1)S(1)}, u32[]{:S(2)}, u32[]{:S(2)}) collective-permute-start(bf16[768,384]{1,0:T(8,128)(2,1)S(1)} %get-tuple-element.42), channel_id=1, source_target_pairs={{0,16},{8,24},{16,0},{24,8},{1,17},{9,25},{17,1},{25,9},{2,18},{10... | collective-permute-start | bytes 1769480 | tf_op jit(solution)/shard_map/ppermute | solution.py:20
  6.9 0.1 collective-permute-start.5
  7.0 3.7 %collective-permute-done.1.refs_1_ = bf16[256,384]{1,0:T(8,128)(2,1)S(1)} collective-permute-done((bf16[256,384]{1,0:T(8,128)(2,1)S(1)}, bf16[256,384]{1,0:T(8,128)(2,1)S(1)}, u32[]{:S(2)}, u32[]{:S(2)}) %collective-permute-start.1) | collective-permute-done | bytes 196640 | tf_op jit(solution)/shard_map/ppermute | solution.py:20
  10.7 3.0 %collective-permute-start.2 = (bf16[256,384]{1,0:T(8,128)(2,1)S(1)}, bf16[256,384]{1,0:T(8,128)(2,1)S(1)}, u32[]{:S(2)}, u32[]{:S(2)}) collective-permute-start(bf16[256,384]{1,0:T(8,128)(2,1)S(1)} %collective-permute-done.1.refs_1_), channel_id=1, source_target_pairs={{0,4},{1,5},{2,6},{3,7},{4,0},{5,1},{6,2},{7,3},{8,12},{9,13},{10,... | collective-permute-start | bytes 589832 | tf_op jit(solution)/shard_map/ppermute | solution.py:20
  13.7 0.7 %shard_map.48.refs_4_ = f32[512,384]{1,0:T(8,128)S(1)} custom-call(bf16[256,4096]{1,0:T(8,128)(2,1)S(1)} %bitcast.4, bf16[256,4096]{1,0:T(8,128)(2,1)S(1)} %collective-permute-done.tok_b, bf16[1024,384]{1,0:T(8,128)(2,1)S(1)} %get-tuple-element.37.refs_0_), custom_call_target="tpu_custom_call" | custom-call | flops 32768000000 | tf_op jit(solution)/shard_map/pallas_call | solution.py:190
  14.4 1.6 %collective-permute-start.7 = (bf16[256,384]{1,0:T(8,128)(2,1)S(1)}, bf16[256,384]{1,0:T(8,128)(2,1)S(1)}, u32[]{:S(2)}, u32[]{:S(2)}) collective-permute-start(bf16[256,384]{1,0:T(8,128)(2,1)S(1)} %collective-permute-done.1.refs_1_), channel_id=1, source_target_pairs={{0,2},{1,3},{2,0},{3,1},{4,6},{5,7},{6,4},{7,5},{8,10},{9,11},{10,... | collective-permute-start | bytes 589832 | tf_op jit(solution)/shard_map/ppermute | solution.py:20
  16.0 1.7 %collective-permute-start.4 = (bf16[256,384]{1,0:T(8,128)(2,1)S(1)}, bf16[256,384]{1,0:T(8,128)(2,1)S(1)}, u32[]{:S(2)}, u32[]{:S(2)}) collective-permute-start(bf16[256,384]{1,0:T(8,128)(2,1)S(1)} %get-tuple-element.41), channel_id=1, source_target_pairs={{0,16},{8,24},{16,0},{24,8},{1,17},{9,25},{17,1},{25,9},{2,18},{10... | collective-permute-start | bytes 589832 | tf_op jit(solution)/shard_map/ppermute | solution.py:20
  17.7 4.5 %collective-permute-done.2.refs_2_ = bf16[256,384]{1,0:T(8,128)(2,1)S(1)} collective-permute-done((bf16[256,384]{1,0:T(8,128)(2,1)S(1)}, bf16[256,384]{1,0:T(8,128)(2,1)S(1)}, u32[]{:S(2)}, u32[]{:S(2)}) %collective-permute-start.2) | collective-permute-done | bytes 196640 | tf_op jit(solution)/shard_map/ppermute | solution.py:20
  22.3 0.5 %collective-permute-start.3 = (bf16[256,384]{1,0:T(8,128)(2,1)S(1)}, bf16[256,384]{1,0:T(8,128)(2,1)S(1)}, u32[]{:S(2)}, u32[]{:S(2)}) collective-permute-start(bf16[256,384]{1,0:T(8,128)(2,1)S(1)} %collective-permute-done.2.refs_2_), channel_id=1, source_target_pairs={{0,2},{1,3},{2,0},{3,1},{4,6},{5,7},{6,4},{7,5},{8,10},{9,11},{10,... | collective-permute-start | bytes 589832 | tf_op jit(solution)/shard_map/ppermute | solution.py:20
  22.9 0.3 collective-permute-done.6.refs_0_
  23.2 2.6 %collective-permute-start.11 = (bf16[128,512]{1,0:T(8,128)(2,1)S(1)}, bf16[128,512]{1,0:T(8,128)(2,1)S(1)}, u32[]{:S(2)}, u32[]{:S(2)}) collective-permute-start(bf16[128,512]{1,0:T(8,128)(2,1)S(1)} %get-tuple-element.57), channel_id=1, source_target_pairs={{0,24},{8,16},{16,8},{24,0},{1,25},{9,17},{17,9},{25,1},{2,26},{10... | collective-permute-start | bytes 393224 | tf_op jit(solution)/shard_map/ppermute | solution.py:20
  25.8 0.6 %collective-permute-start.8 = (bf16[128,1024]{1,0:T(8,128)(2,1)S(1)}, bf16[128,1024]{1,0:T(8,128)(2,1)S(1)}, u32[]{:S(2)}, u32[]{:S(2)}) collective-permute-start(bf16[128,1024]{1,0:T(8,128)(2,1)S(1)} %get-tuple-element.53.refs_0_), channel_id=1, source_target_pairs={{0,8},{8,0},{16,24},{24,16},{1,9},{9,1},{17,25},{25,17},{2,10},{10... | collective-permute-start | bytes 786440 | tf_op jit(solution)/shard_map/ppermute | solution.py:20
  26.4 1.0 %shard_map.50.refs_2_ = f32[512,384]{1,0:T(8,128)S(1)} custom-call(bf16[256,4096]{1,0:T(8,128)(2,1)S(1)} %bitcast.5, bf16[256,4096]{1,0:T(8,128)(2,1)S(1)} %collective-permute-done.tok_b, bf16[768,384]{1,0:T(8,128)(2,1)S(1)} %collective-permute-done.6.refs_0_, bf16[256,384]{1,0:T(8,128)(2,1)S(1)} %collective-permute-done.1.refs_1_, ...), custom_call_target="tpu_custom_call" | custom-call | flops 32768 | tf_op jit(solution)/shard_map/pallas_call | solution.py:190
  27.4 0.6 %collective-permute-done.4.refs_0_ = bf16[256,384]{1,0:T(8,128)(2,1)S(1)} collective-permute-done((bf16[256,384]{1,0:T(8,128)(2,1)S(1)}, bf16[256,384]{1,0:T(8,128)(2,1)S(1)}, u32[]{:S(2)}, u32[]{:S(2)}) %collective-permute-start.4) | collective-permute-done | bytes 196640 | tf_op jit(solution)/shard_map/ppermute | solution.py:20
  27.9 1.6 %collective-permute-start.9 = (bf16[128,1024]{1,0:T(8,128)(2,1)S(1)}, bf16[128,1024]{1,0:T(8,128)(2,1)S(1)}, u32[]{:S(2)}, u32[]{:S(2)}) collective-permute-start(bf16[128,1024]{1,0:T(8,128)(2,1)S(1)} %get-tuple-element.53.refs_0_), channel_id=1, source_target_pairs={{0,16},{8,24},{16,0},{24,8},{1,17},{9,25},{17,1},{25,9},{2,18},{10... | collective-permute-start | bytes 786440 | tf_op jit(solution)/shard_map/ppermute | solution.py:20
  29.6 0.8 %shard_map.51.refs_1_ = f32[512,384]{1,0:T(8,128)S(1)} custom-call(bf16[256,4096]{1,0:T(8,128)(2,1)S(1)} %bitcast.6, bf16[256,4096]{1,0:T(8,128)(2,1)S(1)} %collective-permute-done.tok_b, bf16[256,384]{1,0:T(8,128)(2,1)S(1)} %collective-permute-done.4.refs_0_, bf16[1024,384]{1,0:T(8,128)(2,1)S(1)} %collective-permute-done.5.refs_1_, ...), custom_call_target="tpu_custom_call" | custom-call | flops 32768 | tf_op jit(solution)/shard_map/pallas_call | solution.py:190
  30.4 0.5 %shard_map.52 = (bf16[2,256,256]{2,1,0:T(8,128)(2,1)S(1)}, bf16[2,256,128]{2,1,0:T(8,128)(2,1)S(1)}, f32[2,128,128]{2,1,0:T(8,128)S(1)}, bf16[128,128]{1,0:T(8,128)(2,1)S(1)}) custom-call(bf16[256,4096]{1,0:T(8,128)(2,1)S(1)} %bitcast.7, bf16[256,4096]{1,0:T(8,128)(2,1)S(1)} %collective-permute-done.tok_b, ...), custom_call_target="tpu_custom_call" | custom-call | flops 100663296 | tf_op jit(solution)/shard_map/pallas_call | solution.py:190
  31.0 1.6 %collective-permute-start.10 = (bf16[128,128]{1,0:T(8,128)(2,1)S(1)}, bf16[128,128]{1,0:T(8,128)(2,1)S(1)}, u32[]{:S(2)}, u32[]{:S(2)}) collective-permute-start(bf16[128,128]{1,0:T(8,128)(2,1)S(1)} %get-tuple-element.56), channel_id=1, source_target_pairs={{0,2},{1,3},{2,0},{3,1},{4,6},{5,7},{6,4},{7,5},{8,10},{9,11},{10,... | collective-permute-start | bytes 98312 | tf_op jit(solution)/shard_map/ppermute | solution.py:20
  32.6 0.5 %collective-permute-start.12 = (bf16[128,512]{1,0:T(8,128)(2,1)S(1)}, bf16[128,512]{1,0:T(8,128)(2,1)S(1)}, u32[]{:S(2)}, u32[]{:S(2)}) collective-permute-start(bf16[128,512]{1,0:T(8,128)(2,1)S(1)} %collective-permute-done.11.refs_0_), channel_id=1, source_target_pairs={{0,2},{1,3},{2,0},{3,1},{4,6},{5,7},{6,4},{7,5},{8,10},{9,11},{10,... | collective-permute-start | bytes 393224 | tf_op jit(solution)/shard_map/ppermute | solution.py:20
  33.1 2.2 %collective-permute-done.10.refs_0_ = bf16[128,128]{1,0:T(8,128)(2,1)S(1)} collective-permute-done((bf16[128,128]{1,0:T(8,128)(2,1)S(1)}, bf16[128,128]{1,0:T(8,128)(2,1)S(1)}, u32[]{:S(2)}, u32[]{:S(2)}) %collective-permute-start.10) | collective-permute-done | bytes 32800 | tf_op jit(solution)/shard_map/ppermute | solution.py:20
  35.3 2.4 %collective-permute-start.13 = (bf16[128,128]{1,0:T(8,128)(2,1)S(1)}, bf16[128,128]{1,0:T(8,128)(2,1)S(1)}, u32[]{:S(2)}, u32[]{:S(2)}) collective-permute-start(bf16[128,128]{1,0:T(8,128)(2,1)S(1)} %add_convert_fusion), channel_id=1, source_target_pairs={{0,4},{1,5},{2,6},{3,7},{4,0},{5,1},{6,2},{7,3},{8,12},{9,13},{10,... | collective-permute-start | bytes 98312 | tf_op jit(solution)/shard_map/ppermute | solution.py:20
  37.8 0.5 %collective-permute-start.16 = (bf16[128,1024]{1,0:T(8,128)(2,1)S(1)}, bf16[128,1024]{1,0:T(8,128)(2,1)S(1)}, u32[]{:S(2)}, u32[]{:S(2)}) collective-permute-start(bf16[128,1024]{1,0:T(8,128)(2,1)S(1)} %collective-permute-done.9.refs_2_), channel_id=1, source_target_pairs={{0,1},{1,0},{2,3},{3,2},{4,5},{5,4},{6,7},{7,6},{8,9},{9,8},{10,11... | collective-permute-start | bytes 786440 | tf_op jit(solution)/shard_map/ppermute | solution.py:20
  38.3 0.5 %shard_map.53 = (f32[2,256,128]{2,1,0:T(8,128)S(1)}, bf16[128,1024]{1,0:T(8,128)(2,1)S(1)}) custom-call(bf16[2,256,256]{2,1,0:T(8,128)(2,1)S(1)} %get-tuple-element.54.act, bf16[2,256,128]{2,1,0:T(8,128)(2,1)S(1)} %get-tuple-element.55.values, bf16[128,512]{1,0:T(8,128)(2,1)S(1)} %collective-permute-done.11.refs_0_, ...), custom_call_target="tpu_custom_call" | custom-call | flops 32768000000 | tf_op jit(solution)/shard_map/pallas_call | solution.py:190
  38.8 0.1 collective-permute-start.17
  38.9 1.3 %collective-permute-done.13.refs_1_ = bf16[128,128]{1,0:T(8,128)(2,1)S(1)} collective-permute-done((bf16[128,128]{1,0:T(8,128)(2,1)S(1)}, bf16[128,128]{1,0:T(8,128)(2,1)S(1)}, u32[]{:S(2)}, u32[]{:S(2)}) %collective-permute-start.13) | collective-permute-done | bytes 32800 | tf_op jit(solution)/shard_map/ppermute | solution.py:20
  40.2 0.3 shard_map.54
  40.6 1.2 %collective-permute-done.14.other = bf16[256,128]{1,0:T(8,128)(2,1)S(1)} collective-permute-done((bf16[256,128]{1,0:T(8,128)(2,1)S(1)}, bf16[256,128]{1,0:T(8,128)(2,1)S(1)}, u32[]{:S(2)}, u32[]{:S(2)}) %collective-permute-start.14) | collective-permute-done | bytes 65568 | tf_op jit(solution)/shard_map/ppermute | solution.py:20
  41.8 1.7 %shard_map.55 = bf16[256,4096]{1,0:T(8,128)(2,1)} custom-call(bf16[256,128]{1,0:T(8,128)(2,1)S(1)} %get-tuple-element.61.own, bf16[256,128]{1,0:T(8,128)(2,1)S(1)} %collective-permute-done.14.other, bf16[128,1024]{1,0:T(8,128)(2,1)S(1)} %get-tuple-element.53.refs_0_, bf16[128,1024]{1,0:T(8,128)(2,1)S(1)} %collective-permute-done.8.refs_1_, ...), custom_call_target="tpu_custom_call" | custom-call | flops 536870912 | bytes 2097152 | tf_op jit(solution)/shard_map/pallas_call | solution.py:190
  (21 shorter events, 0.2 us)
Async XLA Ops:
  0.0 13.7 %copy-start = (bf16[1,256,4096]{2,1,0:T(8,128)(2,1)S(1)}, bf16[1,256,4096]{2,1,0:T(8,128)(2,1)}, u32[]{:S(2)}) copy-start(bf16[1,256,4096]{2,1,0:T(8,128)(2,1)} %param.4) | copy-start | bytes 6291460
  0.0 13.7 %collective-permute-start = (bf16[256,4096]{1,0:T(8,128)(2,1)}, bf16[256,4096]{1,0:T(8,128)(2,1)S(1)}, u32[]{:S(2)}, u32[]{:S(2)}) collective-permute-start(bf16[256,4096]{1,0:T(8,128)(2,1)} %bitcast.3), channel_id=1, source_target_pairs={{0,1},{1,0},{2,3},{3,2},{4,5},{5,4},{6,7},{7,6},{8,9},{9,8},{10,11... | collective-permute-start | bytes 6291464 | tf_op jit(solution)/shard_map/ppermute | solution.py:20
  1.6 9.1 %collective-permute-start.1 = (bf16[256,384]{1,0:T(8,128)(2,1)S(1)}, bf16[256,384]{1,0:T(8,128)(2,1)S(1)}, u32[]{:S(2)}, u32[]{:S(2)}) collective-permute-start(bf16[256,384]{1,0:T(8,128)(2,1)S(1)} %shard_map.46), channel_id=1, source_target_pairs={{0,24},{8,16},{16,8},{24,0},{1,25},{9,17},{17,9},{25,1},{2,26},{10... | collective-permute-start | bytes 589832 | tf_op jit(solution)/shard_map/ppermute | solution.py:20
  6.3 16.9 %collective-permute-start.6 = (bf16[768,384]{1,0:T(8,128)(2,1)S(1)}, bf16[768,384]{1,0:T(8,128)(2,1)S(1)}, u32[]{:S(2)}, u32[]{:S(2)}) collective-permute-start(bf16[768,384]{1,0:T(8,128)(2,1)S(1)} %get-tuple-element.42), channel_id=1, source_target_pairs={{0,16},{8,24},{16,0},{24,8},{1,17},{9,25},{17,1},{25,9},{2,18},{10... | collective-permute-start | bytes 1769480 | tf_op jit(solution)/shard_map/ppermute | solution.py:20
  6.9 15.9 %copy-start.1 = (bf16[256,1024]{1,0:T(8,128)(2,1)S(1)}, bf16[256,1024]{1,0:T(8,128)(2,1)}, u32[]{:S(2)}) copy-start(bf16[256,1024]{1,0:T(8,128)(2,1)} %w_out.1) | copy-start | bytes 1572868
  6.9 22.7 %collective-permute-start.5 = (bf16[1024,384]{1,0:T(8,128)(2,1)S(1)}, bf16[1024,384]{1,0:T(8,128)(2,1)S(1)}, u32[]{:S(2)}, u32[]{:S(2)}) collective-permute-start(bf16[1024,384]{1,0:T(8,128)(2,1)S(1)} %get-tuple-element.37.refs_0_), channel_id=1, source_target_pairs={{0,8},{8,0},{16,24},{24,16},{1,9},{9,1},{17,25},{25,17},{2,10},{10... | collective-permute-start | bytes 2359304 | tf_op jit(solution)/shard_map/ppermute | solution.py:20
  10.7 11.6 %collective-permute-start.2 = (bf16[256,384]{1,0:T(8,128)(2,1)S(1)}, bf16[256,384]{1,0:T(8,128)(2,1)S(1)}, u32[]{:S(2)}, u32[]{:S(2)}) collective-permute-start(bf16[256,384]{1,0:T(8,128)(2,1)S(1)} %collective-permute-done.1.refs_1_), channel_id=1, source_target_pairs={{0,4},{1,5},{2,6},{3,7},{4,0},{5,1},{6,2},{7,3},{8,12},{9,13},{10,... | collective-permute-start | bytes 589832 | tf_op jit(solution)/shard_map/ppermute | solution.py:20
  14.4 11.4 %collective-permute-start.7 = (bf16[256,384]{1,0:T(8,128)(2,1)S(1)}, bf16[256,384]{1,0:T(8,128)(2,1)S(1)}, u32[]{:S(2)}, u32[]{:S(2)}) collective-permute-start(bf16[256,384]{1,0:T(8,128)(2,1)S(1)} %collective-permute-done.1.refs_1_), channel_id=1, source_target_pairs={{0,2},{1,3},{2,0},{3,1},{4,6},{5,7},{6,4},{7,5},{8,10},{9,11},{10,... | collective-permute-start | bytes 589832 | tf_op jit(solution)/shard_map/ppermute | solution.py:20
  16.0 11.9 %collective-permute-start.4 = (bf16[256,384]{1,0:T(8,128)(2,1)S(1)}, bf16[256,384]{1,0:T(8,128)(2,1)S(1)}, u32[]{:S(2)}, u32[]{:S(2)}) collective-permute-start(bf16[256,384]{1,0:T(8,128)(2,1)S(1)} %get-tuple-element.41), channel_id=1, source_target_pairs={{0,16},{8,24},{16,0},{24,8},{1,17},{9,25},{17,1},{25,9},{2,18},{10... | collective-permute-start | bytes 589832 | tf_op jit(solution)/shard_map/ppermute | solution.py:20
  22.3 8.2 %collective-permute-start.3 = (bf16[256,384]{1,0:T(8,128)(2,1)S(1)}, bf16[256,384]{1,0:T(8,128)(2,1)S(1)}, u32[]{:S(2)}, u32[]{:S(2)}) collective-permute-start(bf16[256,384]{1,0:T(8,128)(2,1)S(1)} %collective-permute-done.2.refs_2_), channel_id=1, source_target_pairs={{0,2},{1,3},{2,0},{3,1},{4,6},{5,7},{6,4},{7,5},{8,10},{9,11},{10,... | collective-permute-start | bytes 589832 | tf_op jit(solution)/shard_map/ppermute | solution.py:20
  23.2 9.4 %collective-permute-start.11 = (bf16[128,512]{1,0:T(8,128)(2,1)S(1)}, bf16[128,512]{1,0:T(8,128)(2,1)S(1)}, u32[]{:S(2)}, u32[]{:S(2)}) collective-permute-start(bf16[128,512]{1,0:T(8,128)(2,1)S(1)} %get-tuple-element.57), channel_id=1, source_target_pairs={{0,24},{8,16},{16,8},{24,0},{1,25},{9,17},{17,9},{25,1},{2,26},{10... | collective-permute-start | bytes 393224 | tf_op jit(solution)/shard_map/ppermute | solution.py:20
  25.8 11.9 %collective-permute-start.8 = (bf16[128,1024]{1,0:T(8,128)(2,1)S(1)}, bf16[128,1024]{1,0:T(8,128)(2,1)S(1)}, u32[]{:S(2)}, u32[]{:S(2)}) collective-permute-start(bf16[128,1024]{1,0:T(8,128)(2,1)S(1)} %get-tuple-element.53.refs_0_), channel_id=1, source_target_pairs={{0,8},{8,0},{16,24},{24,16},{1,9},{9,1},{17,25},{25,17},{2,10},{10... | collective-permute-start | bytes 786440 | tf_op jit(solution)/shard_map/ppermute | solution.py:20
  27.9 9.8 %collective-permute-start.9 = (bf16[128,1024]{1,0:T(8,128)(2,1)S(1)}, bf16[128,1024]{1,0:T(8,128)(2,1)S(1)}, u32[]{:S(2)}, u32[]{:S(2)}) collective-permute-start(bf16[128,1024]{1,0:T(8,128)(2,1)S(1)} %get-tuple-element.53.refs_0_), channel_id=1, source_target_pairs={{0,16},{8,24},{16,0},{24,8},{1,17},{9,25},{17,1},{25,9},{2,18},{10... | collective-permute-start | bytes 786440 | tf_op jit(solution)/shard_map/ppermute | solution.py:20
  31.0 4.3 %collective-permute-start.10 = (bf16[128,128]{1,0:T(8,128)(2,1)S(1)}, bf16[128,128]{1,0:T(8,128)(2,1)S(1)}, u32[]{:S(2)}, u32[]{:S(2)}) collective-permute-start(bf16[128,128]{1,0:T(8,128)(2,1)S(1)} %get-tuple-element.56), channel_id=1, source_target_pairs={{0,2},{1,3},{2,0},{3,1},{4,6},{5,7},{6,4},{7,5},{8,10},{9,11},{10,... | collective-permute-start | bytes 98312 | tf_op jit(solution)/shard_map/ppermute | solution.py:20
  32.6 5.7 %collective-permute-start.12 = (bf16[128,512]{1,0:T(8,128)(2,1)S(1)}, bf16[128,512]{1,0:T(8,128)(2,1)S(1)}, u32[]{:S(2)}, u32[]{:S(2)}) collective-permute-start(bf16[128,512]{1,0:T(8,128)(2,1)S(1)} %collective-permute-done.11.refs_0_), channel_id=1, source_target_pairs={{0,2},{1,3},{2,0},{3,1},{4,6},{5,7},{6,4},{7,5},{8,10},{9,11},{10,... | collective-permute-start | bytes 393224 | tf_op jit(solution)/shard_map/ppermute | solution.py:20
  35.3 4.9 %collective-permute-start.13 = (bf16[128,128]{1,0:T(8,128)(2,1)S(1)}, bf16[128,128]{1,0:T(8,128)(2,1)S(1)}, u32[]{:S(2)}, u32[]{:S(2)}) collective-permute-start(bf16[128,128]{1,0:T(8,128)(2,1)S(1)} %add_convert_fusion), channel_id=1, source_target_pairs={{0,4},{1,5},{2,6},{3,7},{4,0},{5,1},{6,2},{7,3},{8,12},{9,13},{10,... | collective-permute-start | bytes 98312 | tf_op jit(solution)/shard_map/ppermute | solution.py:20
  37.8 4.1 %collective-permute-start.15 = (bf16[128,1024]{1,0:T(8,128)(2,1)S(1)}, bf16[128,1024]{1,0:T(8,128)(2,1)S(1)}, u32[]{:S(2)}, u32[]{:S(2)}) collective-permute-start(bf16[128,1024]{1,0:T(8,128)(2,1)S(1)} %collective-permute-done.8.refs_1_), channel_id=1, source_target_pairs={{0,1},{1,0},{2,3},{3,2},{4,5},{5,4},{6,7},{7,6},{8,9},{9,8},{10,11... | collective-permute-start | bytes 786440 | tf_op jit(solution)/shard_map/ppermute | solution.py:20
  37.8 4.1 %collective-permute-start.16 = (bf16[128,1024]{1,0:T(8,128)(2,1)S(1)}, bf16[128,1024]{1,0:T(8,128)(2,1)S(1)}, u32[]{:S(2)}, u32[]{:S(2)}) collective-permute-start(bf16[128,1024]{1,0:T(8,128)(2,1)S(1)} %collective-permute-done.9.refs_2_), channel_id=1, source_target_pairs={{0,1},{1,0},{2,3},{3,2},{4,5},{5,4},{6,7},{7,6},{8,9},{9,8},{10,11... | collective-permute-start | bytes 786440 | tf_op jit(solution)/shard_map/ppermute | solution.py:20
  38.3 1.9 %copy-start.2 = (f32[256]{0:T(256)S(1)}, f32[256]{0:T(256)}, u32[]{:S(2)}) copy-start(f32[256]{0:T(256)} %param.6) | copy-start | bytes 3076
  38.8 3.0 %collective-permute-start.17 = (bf16[128,1024]{1,0:T(8,128)(2,1)S(1)}, bf16[128,1024]{1,0:T(8,128)(2,1)S(1)}, u32[]{:S(2)}, u32[]{:S(2)}) collective-permute-start(bf16[128,1024]{1,0:T(8,128)(2,1)S(1)} %get-tuple-element.65.refs_3_), channel_id=1, source_target_pairs={{0,1},{1,0},{2,3},{3,2},{4,5},{5,4},{6,7},{7,6},{8,9},{9,8},{10,11... | collective-permute-start | bytes 786440 | tf_op jit(solution)/shard_map/ppermute | solution.py:20
  40.5 1.3 %collective-permute-start.14 = (bf16[256,128]{1,0:T(8,128)(2,1)S(1)}, bf16[256,128]{1,0:T(8,128)(2,1)S(1)}, u32[]{:S(2)}, u32[]{:S(2)}) collective-permute-start(bf16[256,128]{1,0:T(8,128)(2,1)S(1)} %get-tuple-element.62), channel_id=1, source_target_pairs={{0,1},{1,0},{2,3},{3,2},{4,5},{5,4},{6,7},{7,6},{8,9},{9,8},{10,11... | collective-permute-start | bytes 196616 | tf_op jit(solution)/shard_map/ppermute | solution.py:20

commit v4 on v2

--- a/solution.py
+++ b/solution.py
@@ -90,6 +90,15 @@
     start = places_near(shard, (3,))[0]
     mine = quarter_of()
     return [start + (mine ^ mask) * (shard // 4) for mask in (0, 2, 1, 3)]
+
+
+def project_block(shard, tok, own, *refs):
+    before, out = refs[:-1], refs[-1]
+    rows = tok.shape[0]
+    cols = pl.ds(pl.multiple_of(places_near(shard, (0,))[0], 128), shard)
+    if before:
+        out[:rows, :] = before[0][...]
+    out[out.shape[0] - rows :, :] = dot(tok[:, cols], own[...])
 
 
 def project(count, places, tok_a, tok_b, *refs):
@@ -200,7 +209,7 @@
     def array(shape, kind):
         return jax.ShapeDtypeStruct(shape, kind)
 
-    def add_product(pieces, places, total=None):
+    def add_product(tok_other, pieces, places, total=None):
         extra = [] if total is None else [total]
         return call(
             functools.partial(project, len(pieces), places),
@@ -210,7 +219,6 @@
             flops=rows * HEAD * (1 if total is not None else 1000000),
         )
 
-    tok_other = flip(tok_own, "seq", blocks, 1)
     width = w_out.shape[1]
     grid = n == 4 and blocks % (4 * CORES) == 0 and shard % 512 == 0 and width % 256 == 0
 
@@ -231,13 +239,22 @@
         part = cut(lambda: quarter_of() * quarter, FIRST_LIMIT, quarter)[0]
         far = [flip(part, "dp", n, 3)]
         own, most, last = cut(lambda: 0, CUT_LIMIT, shard, 3 * quarter, quarter)
+        send_tok, _ = lax.optimization_barrier((tok_own, far[0]))
+        tok_other = flip(send_tok, "seq", blocks, 1)
         x_most = flip(most, "dp", n, 1)
         send_last, here = lax.optimization_barrier((last, far[0]))
         x_last = flip(send_last, "dp", n, 1)
         from_y = flip(own, "dp", n, 2)
         far.append(flip(far[0], "seq", blocks, CORES * 2))
         here, own = lax.optimization_barrier((far[0], own))
-        total = add_product([own], functools.partial(places_near, shard, (0,)))
+        first = call(
+            functools.partial(project_block, shard), array((rows, 3 * HEAD), f32),
+            [tok_own, own], VMEM, [VMEM] * 2, flops=rows * HEAD * 1000000,
+        )
+        total = call(
+            functools.partial(project_block, shard), array((CORES * rows, 3 * HEAD), f32),
+            [tok_other, own, first], VMEM, [VMEM] * 3, flops=rows * HEAD,
+        )
         send_far, total = lax.optimization_barrier((far[0], total))
         far.append(flip(send_far, "seq", blocks, CORES))
         passed, total = lax.optimization_barrier((far[1], total))
@@ -250,11 +267,12 @@
         out_x = flip(sent, "dp", n, 1)
         out_y = flip(sent, "dp", n, 2)
         total = add_product(
-            [x_most, *far[:3]], lambda: places_near(shard, (1,)) + places_far(shard)[:3], total
-        )
-        total = add_product([x_last, from_y], functools.partial(places_last, shard), total)
+            tok_other, [x_most, *far[:3]], lambda: places_near(shard, (1,)) + places_far(shard)[:3], total
+        )
+        total = add_product(tok_other, [x_last, from_y], functools.partial(places_last, shard), total)
         pieces, places = far[3:], lambda: places_far(shard)[3:]
     else:
+        tok_other = flip(tok_own, "seq", blocks, 1)
         whole = cut(lambda: 0, CUT_LIMIT, shard)[0]
         pieces, places = [lax.all_gather(whole, "dp", axis=0, tiled=True)], lambda: [0]
     extra = [] if total is None else [total]

time: 42.6 us -> 45.1 us (1.059)
  starting transfers between devices: 20 us -> 23.6 us
  waiting for transfers between devices: 14.3 us -> 13.1 us
    ppermute x18, starting transfers between devices: 20 us -> 23.6 us  [flip(): return lax.ppermute(x, axis, [(i, i ^ mask) for i in range(size)])]
    ppermute x18, waiting for transfers between devices: 14.3 us -> 13.1 us  [flip(): return lax.ppermute(x, axis, [(i, i ^ mask) for i in range(size)])]
    pallas_call x10 -> x11, Pallas kernels: 7.96 us -> 8.08 us  [call(): pl.pallas_call(kernel, out_shape=outs, in_specs=in_specs, out_specs=out_s...]
  transfers between devices with their start and end apart: 18 -> 18, of which waited for: 7 -> 6; matrix products, arithmetic and copies ran while one was open for 0% -> 0% of each run, Pallas kernels for 15% -> 12%
where the time goes in v4:
time: 45.1 us; the launch traced here: 44.9 us
  starting transfers between devices  23.6 us (52%)
  waiting for transfers between devices  13.1 us (29%)
  Pallas kernels  8.08 us (18%)
    ppermute x18, starting transfers between devices, flip(): return lax.ppermute(x, axis, [(i, i ^ mask) for i in range(size)])  23.6 us
    ppermute x18, waiting for transfers between devices, flip(): return lax.ppermute(x, axis, [(i, i ^ mask) for i in range(size)])  13.1 us
    pallas_call x11, Pallas kernels, call(): pl.pallas_call(kernel, out_shape=outs, in_specs=in_specs, out_specs=out_s...  8.08 us
  transfers between devices with their start and end apart: 18, of which 6 were waited for; matrix products, arithmetic and copies ran while one was open for 0% of the time, Pallas kernels for 12%

profile of v4, /device:TPU:0, one launch (start us, length us, event | category | flops | bytes accessed | tf_op | source)
XLA Modules:
  0.0 44.9 jit_solution(5239827624723518114)
XLA Ops:
  0.0 1.1 %shard_map.46 = bf16[256,384]{1,0:T(8,128)(2,1)S(1)} custom-call(bf16[1024,768]{1,0:T(8,128)(2,1)} %w_qkv.3), custom_call_target="tpu_custom_call" | custom-call | tf_op jit(solution)/shard_map/pallas_call | solution.py:199
  1.1 4.0 %collective-permute-start = (bf16[256,384]{1,0:T(8,128)(2,1)S(1)}, bf16[256,384]{1,0:T(8,128)(2,1)S(1)}, u32[]{:S(2)}, u32[]{:S(2)}) collective-permute-start(bf16[256,384]{1,0:T(8,128)(2,1)S(1)} %shard_map.46), channel_id=1, source_target_pairs={{0,24},{8,16},{16,8},{24,0},{1,25},{9,17},{17,9},{25,1},{2,26},{10... | collective-permute-start | bytes 589832 | tf_op jit(solution)/shard_map/ppermute | solution.py:20
  5.1 1.2 %shard_map.47 = (bf16[1024,384]{1,0:T(8,128)(2,1)S(1)}, bf16[768,384]{1,0:T(8,128)(2,1)S(1)}, bf16[256,384]{1,0:T(8,128)(2,1)S(1)}) custom-call(bf16[1024,768]{1,0:T(8,128)(2,1)} %w_qkv.3), custom_call_target="tpu_custom_call" | custom-call | tf_op jit(solution)/shard_map/pallas_call | solution.py:199
  6.3 0.6 %collective-permute-start.6 = (bf16[768,384]{1,0:T(8,128)(2,1)S(1)}, bf16[768,384]{1,0:T(8,128)(2,1)S(1)}, u32[]{:S(2)}, u32[]{:S(2)}) collective-permute-start(bf16[768,384]{1,0:T(8,128)(2,1)S(1)} %get-tuple-element.44), channel_id=1, source_target_pairs={{0,8},{8,0},{16,24},{24,16},{1,9},{9,1},{17,25},{25,17},{2,10},{10... | collective-permute-start | bytes 1769480 | tf_op jit(solution)/shard_map/ppermute | solution.py:20
  6.9 0.1 collective-permute-start.5
  6.9 3.8 %collective-permute-done.refs_1_ = bf16[256,384]{1,0:T(8,128)(2,1)S(1)} collective-permute-done((bf16[256,384]{1,0:T(8,128)(2,1)S(1)}, bf16[256,384]{1,0:T(8,128)(2,1)S(1)}, u32[]{:S(2)}, u32[]{:S(2)}) %collective-permute-start) | collective-permute-done | bytes 196640 | tf_op jit(solution)/shard_map/ppermute | solution.py:20
  10.8 3.1 %collective-permute-start.2 = (bf16[256,384]{1,0:T(8,128)(2,1)S(1)}, bf16[256,384]{1,0:T(8,128)(2,1)S(1)}, u32[]{:S(2)}, u32[]{:S(2)}) collective-permute-start(bf16[256,384]{1,0:T(8,128)(2,1)S(1)} %collective-permute-done.refs_1_), channel_id=1, source_target_pairs={{0,4},{1,5},{2,6},{3,7},{4,0},{5,1},{6,2},{7,3},{8,12},{9,13},{10,... | collective-permute-start | bytes 589832 | tf_op jit(solution)/shard_map/ppermute | solution.py:20
  13.9 0.4 shard_map.48.refs_0_
  14.3 0.6 %collective-permute-done.1.tok.tok_b = bf16[256,4096]{1,0:T(8,128)(2,1)S(1)} collective-permute-done((bf16[256,4096]{1,0:T(8,128)(2,1)S(1)}, bf16[256,4096]{1,0:T(8,128)(2,1)S(1)}, u32[]{:S(2)}, u32[]{:S(2)}) %collective-permute-start.1) | collective-permute-done | bytes 2097184 | tf_op jit(solution)/shard_map/ppermute | solution.py:20
  14.9 0.4 shard_map.49.refs_4_
  15.4 2.2 %collective-permute-start.7 = (bf16[256,384]{1,0:T(8,128)(2,1)S(1)}, bf16[256,384]{1,0:T(8,128)(2,1)S(1)}, u32[]{:S(2)}, u32[]{:S(2)}) collective-permute-start(bf16[256,384]{1,0:T(8,128)(2,1)S(1)} %collective-permute-done.refs_1_), channel_id=1, source_target_pairs={{0,2},{1,3},{2,0},{3,1},{4,6},{5,7},{6,4},{7,5},{8,10},{9,11},{10,... | collective-permute-start | bytes 589832 | tf_op jit(solution)/shard_map/ppermute | solution.py:20
  17.5 1.5 %collective-permute-start.4 = (bf16[256,384]{1,0:T(8,128)(2,1)S(1)}, bf16[256,384]{1,0:T(8,128)(2,1)S(1)}, u32[]{:S(2)}, u32[]{:S(2)}) collective-permute-start(bf16[256,384]{1,0:T(8,128)(2,1)S(1)} %get-tuple-element.43), channel_id=1, source_target_pairs={{0,8},{8,0},{16,24},{24,16},{1,9},{9,1},{17,25},{25,17},{2,10},{10... | collective-permute-start | bytes 589832 | tf_op jit(solution)/shard_map/ppermute | solution.py:20
  19.0 4.8 %collective-permute-done.2.refs_2_ = bf16[256,384]{1,0:T(8,128)(2,1)S(1)} collective-permute-done((bf16[256,384]{1,0:T(8,128)(2,1)S(1)}, bf16[256,384]{1,0:T(8,128)(2,1)S(1)}, u32[]{:S(2)}, u32[]{:S(2)}) %collective-permute-start.2) | collective-permute-done | bytes 196640 | tf_op jit(solution)/shard_map/ppermute | solution.py:20
  23.8 0.7 %collective-permute-start.3 = (bf16[256,384]{1,0:T(8,128)(2,1)S(1)}, bf16[256,384]{1,0:T(8,128)(2,1)S(1)}, u32[]{:S(2)}, u32[]{:S(2)}) collective-permute-start(bf16[256,384]{1,0:T(8,128)(2,1)S(1)} %collective-permute-done.2.refs_2_), channel_id=1, source_target_pairs={{0,2},{1,3},{2,0},{3,1},{4,6},{5,7},{6,4},{7,5},{8,10},{9,11},{10,... | collective-permute-start | bytes 589832 | tf_op jit(solution)/shard_map/ppermute | solution.py:20
  24.5 2.5 %collective-permute-start.11 = (bf16[128,512]{1,0:T(8,128)(2,1)S(1)}, bf16[128,512]{1,0:T(8,128)(2,1)S(1)}, u32[]{:S(2)}, u32[]{:S(2)}) collective-permute-start(bf16[128,512]{1,0:T(8,128)(2,1)S(1)} %get-tuple-element.59), channel_id=1, source_target_pairs={{0,24},{8,16},{16,8},{24,0},{1,25},{9,17},{17,9},{25,1},{2,26},{10... | collective-permute-start | bytes 393224 | tf_op jit(solution)/shard_map/ppermute | solution.py:20
  27.0 0.5 %collective-permute-start.8 = (bf16[128,1024]{1,0:T(8,128)(2,1)S(1)}, bf16[128,1024]{1,0:T(8,128)(2,1)S(1)}, u32[]{:S(2)}, u32[]{:S(2)}) collective-permute-start(bf16[128,1024]{1,0:T(8,128)(2,1)S(1)} %get-tuple-element.55.refs_0_), channel_id=1, source_target_pairs={{0,8},{8,0},{16,24},{24,16},{1,9},{9,1},{17,25},{25,17},{2,10},{10... | collective-permute-start | bytes 786440 | tf_op jit(solution)/shard_map/ppermute | solution.py:20
  27.6 1.0 %shard_map.51.refs_2_ = f32[512,384]{1,0:T(8,128)S(1)} custom-call(bf16[256,4096]{1,0:T(8,128)(2,1)S(1)} %bitcast.5, bf16[256,4096]{1,0:T(8,128)(2,1)S(1)} %collective-permute-done.1.tok.tok_b, bf16[768,384]{1,0:T(8,128)(2,1)S(1)} %collective-permute-done.6.refs_0_, bf16[256,384]{1,0:T(8,128)(2,1)S(1)} %collective-permute-done.refs_1_, ...), custom_call_target="tpu_custom_call" | custom-call | flops 32768 | tf_op jit(solution)/shard_map/pallas_call | solution.py:199
  28.6 1.5 %collective-permute-start.9 = (bf16[128,1024]{1,0:T(8,128)(2,1)S(1)}, bf16[128,1024]{1,0:T(8,128)(2,1)S(1)}, u32[]{:S(2)}, u32[]{:S(2)}) collective-permute-start(bf16[128,1024]{1,0:T(8,128)(2,1)S(1)} %get-tuple-element.55.refs_0_), channel_id=1, source_target_pairs={{0,16},{8,24},{16,0},{24,8},{1,17},{9,25},{17,1},{25,9},{2,18},{10... | collective-permute-start | bytes 786440 | tf_op jit(solution)/shard_map/ppermute | solution.py:20
  30.1 0.8 %shard_map.52.refs_1_ = f32[512,384]{1,0:T(8,128)S(1)} custom-call(bf16[256,4096]{1,0:T(8,128)(2,1)S(1)} %bitcast.6, bf16[256,4096]{1,0:T(8,128)(2,1)S(1)} %collective-permute-done.1.tok.tok_b, bf16[256,384]{1,0:T(8,128)(2,1)S(1)} %collective-permute-done.4.refs_0_, bf16[1024,384]{1,0:T(8,128)(2,1)S(1)} %collective-permute-done.5.refs_1_, ...), custom_call_target="tpu_custom_call" | custom-call | flops 32768 | tf_op jit(solution)/shard_map/pallas_call | solution.py:199
  31.0 0.5 %shard_map.53 = (bf16[2,256,256]{2,1,0:T(8,128)(2,1)S(1)}, bf16[2,256,128]{2,1,0:T(8,128)(2,1)S(1)}, f32[2,128,128]{2,1,0:T(8,128)S(1)}, bf16[128,128]{1,0:T(8,128)(2,1)S(1)}) custom-call(bf16[256,4096]{1,0:T(8,128)(2,1)S(1)} %bitcast.7, bf16[256,4096]{1,0:T(8,128)(2,1)S(1)} %collective-permute-done.1.tok.tok_b, ...), custom_call_target="tpu_custom_call" | custom-call | flops 100663296 | tf_op jit(solution)/shard_map/pallas_call | solution.py:199
  31.5 0.5 %collective-permute-start.10 = (bf16[128,128]{1,0:T(8,128)(2,1)S(1)}, bf16[128,128]{1,0:T(8,128)(2,1)S(1)}, u32[]{:S(2)}, u32[]{:S(2)}) collective-permute-start(bf16[128,128]{1,0:T(8,128)(2,1)S(1)} %get-tuple-element.58), channel_id=1, source_target_pairs={{0,2},{1,3},{2,0},{3,1},{4,6},{5,7},{6,4},{7,5},{8,10},{9,11},{10,... | collective-permute-start | bytes 98312 | tf_op jit(solution)/shard_map/ppermute | solution.py:20
  32.0 1.6 %collective-permute-start.12 = (bf16[128,512]{1,0:T(8,128)(2,1)S(1)}, bf16[128,512]{1,0:T(8,128)(2,1)S(1)}, u32[]{:S(2)}, u32[]{:S(2)}) collective-permute-start(bf16[128,512]{1,0:T(8,128)(2,1)S(1)} %collective-permute-done.11.refs_0_), channel_id=1, source_target_pairs={{0,2},{1,3},{2,0},{3,1},{4,6},{5,7},{6,4},{7,5},{8,10},{9,11},{10,... | collective-permute-start | bytes 393224 | tf_op jit(solution)/shard_map/ppermute | solution.py:20
  33.6 1.9 %collective-permute-done.10.refs_0_ = bf16[128,128]{1,0:T(8,128)(2,1)S(1)} collective-permute-done((bf16[128,128]{1,0:T(8,128)(2,1)S(1)}, bf16[128,128]{1,0:T(8,128)(2,1)S(1)}, u32[]{:S(2)}, u32[]{:S(2)}) %collective-permute-start.10) | collective-permute-done | bytes 32800 | tf_op jit(solution)/shard_map/ppermute | solution.py:20
  35.5 4.2 %collective-permute-start.13 = (bf16[128,128]{1,0:T(8,128)(2,1)S(1)}, bf16[128,128]{1,0:T(8,128)(2,1)S(1)}, u32[]{:S(2)}, u32[]{:S(2)}) collective-permute-start(bf16[128,128]{1,0:T(8,128)(2,1)S(1)} %add_convert_fusion), channel_id=1, source_target_pairs={{0,4},{1,5},{2,6},{3,7},{4,0},{5,1},{6,2},{7,3},{8,12},{9,13},{10,... | collective-permute-start | bytes 98312 | tf_op jit(solution)/shard_map/ppermute | solution.py:20
  39.7 0.5 %collective-permute-start.16 = (bf16[128,1024]{1,0:T(8,128)(2,1)S(1)}, bf16[128,1024]{1,0:T(8,128)(2,1)S(1)}, u32[]{:S(2)}, u32[]{:S(2)}) collective-permute-start(bf16[128,1024]{1,0:T(8,128)(2,1)S(1)} %collective-permute-done.9.refs_2_), channel_id=1, source_target_pairs={{0,1},{1,0},{2,3},{3,2},{4,5},{5,4},{6,7},{7,6},{8,9},{9,8},{10,11... | collective-permute-start | bytes 786440 | tf_op jit(solution)/shard_map/ppermute | solution.py:20
  40.2 0.5 %shard_map.54 = (f32[2,256,128]{2,1,0:T(8,128)S(1)}, bf16[128,1024]{1,0:T(8,128)(2,1)S(1)}) custom-call(bf16[2,256,256]{2,1,0:T(8,128)(2,1)S(1)} %get-tuple-element.56.act, bf16[2,256,128]{2,1,0:T(8,128)(2,1)S(1)} %get-tuple-element.57.values, bf16[128,512]{1,0:T(8,128)(2,1)S(1)} %collective-permute-done.11.refs_0_, ...), custom_call_target="tpu_custom_call" | custom-call | flops 32768000000 | tf_op jit(solution)/shard_map/pallas_call | solution.py:199
  40.7 0.1 collective-permute-start.17
  40.9 0.7 %collective-permute-done.13.refs_1_ = bf16[128,128]{1,0:T(8,128)(2,1)S(1)} collective-permute-done((bf16[128,128]{1,0:T(8,128)(2,1)S(1)}, bf16[128,128]{1,0:T(8,128)(2,1)S(1)}, u32[]{:S(2)}, u32[]{:S(2)}) %collective-permute-start.13) | collective-permute-done | bytes 32800 | tf_op jit(solution)/shard_map/ppermute | solution.py:20
  41.6 0.3 shard_map.55
  41.9 0.1 collective-permute-start.14
  42.0 1.2 %collective-permute-done.14.other = bf16[256,128]{1,0:T(8,128)(2,1)S(1)} collective-permute-done((bf16[256,128]{1,0:T(8,128)(2,1)S(1)}, bf16[256,128]{1,0:T(8,128)(2,1)S(1)}, u32[]{:S(2)}, u32[]{:S(2)}) %collective-permute-start.14) | collective-permute-done | bytes 65568 | tf_op jit(solution)/shard_map/ppermute | solution.py:20
  43.2 1.7 %shard_map.56 = bf16[256,4096]{1,0:T(8,128)(2,1)} custom-call(bf16[256,128]{1,0:T(8,128)(2,1)S(1)} %get-tuple-element.63.own, bf16[256,128]{1,0:T(8,128)(2,1)S(1)} %collective-permute-done.14.other, bf16[128,1024]{1,0:T(8,128)(2,1)S(1)} %get-tuple-element.55.refs_0_, bf16[128,1024]{1,0:T(8,128)(2,1)S(1)} %collective-permute-done.8.refs_1_, ...), custom_call_target="tpu_custom_call" | custom-call | flops 536870912 | bytes 2097152 | tf_op jit(solution)/shard_map/pallas_call | solution.py:199
  (22 shorter events, 0.1 us)
Async XLA Ops:
  0.0 10.8 %copy-start = (bf16[1,256,4096]{2,1,0:T(8,128)(2,1)S(1)}, bf16[1,256,4096]{2,1,0:T(8,128)(2,1)}, u32[]{:S(2)}) copy-start(bf16[1,256,4096]{2,1,0:T(8,128)(2,1)} %param.4) | copy-start | bytes 6291460
  1.1 9.7 %collective-permute-start = (bf16[256,384]{1,0:T(8,128)(2,1)S(1)}, bf16[256,384]{1,0:T(8,128)(2,1)S(1)}, u32[]{:S(2)}, u32[]{:S(2)}) collective-permute-start(bf16[256,384]{1,0:T(8,128)(2,1)S(1)} %shard_map.46), channel_id=1, source_target_pairs={{0,24},{8,16},{16,8},{24,0},{1,25},{9,17},{17,9},{25,1},{2,26},{10... | collective-permute-start | bytes 589832 | tf_op jit(solution)/shard_map/ppermute | solution.py:20
  6.3 18.2 %collective-permute-start.6 = (bf16[768,384]{1,0:T(8,128)(2,1)S(1)}, bf16[768,384]{1,0:T(8,128)(2,1)S(1)}, u32[]{:S(2)}, u32[]{:S(2)}) collective-permute-start(bf16[768,384]{1,0:T(8,128)(2,1)S(1)} %get-tuple-element.44), channel_id=1, source_target_pairs={{0,8},{8,0},{16,24},{24,16},{1,9},{9,1},{17,25},{25,17},{2,10},{10... | collective-permute-start | bytes 1769480 | tf_op jit(solution)/shard_map/ppermute | solution.py:20
  6.9 23.2 %collective-permute-start.5 = (bf16[1024,384]{1,0:T(8,128)(2,1)S(1)}, bf16[1024,384]{1,0:T(8,128)(2,1)S(1)}, u32[]{:S(2)}, u32[]{:S(2)}) collective-permute-start(bf16[1024,384]{1,0:T(8,128)(2,1)S(1)} %get-tuple-element.39.own), channel_id=1, source_target_pairs={{0,16},{8,24},{16,0},{24,8},{1,17},{9,25},{17,1},{25,9},{2,18},{10... | collective-permute-start | bytes 2359304 | tf_op jit(solution)/shard_map/ppermute | solution.py:20
  10.8 4.2 %collective-permute-start.1 = (bf16[256,4096]{1,0:T(8,128)(2,1)S(1)}, bf16[256,4096]{1,0:T(8,128)(2,1)S(1)}, u32[]{:S(2)}, u32[]{:S(2)}) collective-permute-start(bf16[256,4096]{1,0:T(8,128)(2,1)S(1)} %bitcast.3), channel_id=1, source_target_pairs={{0,1},{1,0},{2,3},{3,2},{4,5},{5,4},{6,7},{7,6},{8,9},{9,8},{10,11... | collective-permute-start | bytes 6291464 | tf_op jit(solution)/shard_map/ppermute | solution.py:20
  10.8 13.0 %collective-permute-start.2 = (bf16[256,384]{1,0:T(8,128)(2,1)S(1)}, bf16[256,384]{1,0:T(8,128)(2,1)S(1)}, u32[]{:S(2)}, u32[]{:S(2)}) collective-permute-start(bf16[256,384]{1,0:T(8,128)(2,1)S(1)} %collective-permute-done.refs_1_), channel_id=1, source_target_pairs={{0,4},{1,5},{2,6},{3,7},{4,0},{5,1},{6,2},{7,3},{8,12},{9,13},{10,... | collective-permute-start | bytes 589832 | tf_op jit(solution)/shard_map/ppermute | solution.py:20
  14.3 10.2 %copy-start.1 = (bf16[256,1024]{1,0:T(8,128)(2,1)S(1)}, bf16[256,1024]{1,0:T(8,128)(2,1)}, u32[]{:S(2)}) copy-start(bf16[256,1024]{1,0:T(8,128)(2,1)} %w_out.1) | copy-start | bytes 1572868
  15.4 11.7 %collective-permute-start.7 = (bf16[256,384]{1,0:T(8,128)(2,1)S(1)}, bf16[256,384]{1,0:T(8,128)(2,1)S(1)}, u32[]{:S(2)}, u32[]{:S(2)}) collective-permute-start(bf16[256,384]{1,0:T(8,128)(2,1)S(1)} %collective-permute-done.refs_1_), channel_id=1, source_target_pairs={{0,2},{1,3},{2,0},{3,1},{4,6},{5,7},{6,4},{7,5},{8,10},{9,11},{10,... | collective-permute-start | bytes 589832 | tf_op jit(solution)/shard_map/ppermute | solution.py:20
  17.5 11.0 %collective-permute-start.4 = (bf16[256,384]{1,0:T(8,128)(2,1)S(1)}, bf16[256,384]{1,0:T(8,128)(2,1)S(1)}, u32[]{:S(2)}, u32[]{:S(2)}) collective-permute-start(bf16[256,384]{1,0:T(8,128)(2,1)S(1)} %get-tuple-element.43), channel_id=1, source_target_pairs={{0,8},{8,0},{16,24},{24,16},{1,9},{9,1},{17,25},{25,17},{2,10},{10... | collective-permute-start | bytes 589832 | tf_op jit(solution)/shard_map/ppermute | solution.py:20
  23.8 7.2 %collective-permute-start.3 = (bf16[256,384]{1,0:T(8,128)(2,1)S(1)}, bf16[256,384]{1,0:T(8,128)(2,1)S(1)}, u32[]{:S(2)}, u32[]{:S(2)}) collective-permute-start(bf16[256,384]{1,0:T(8,128)(2,1)S(1)} %collective-permute-done.2.refs_2_), channel_id=1, source_target_pairs={{0,2},{1,3},{2,0},{3,1},{4,6},{5,7},{6,4},{7,5},{8,10},{9,11},{10,... | collective-permute-start | bytes 589832 | tf_op jit(solution)/shard_map/ppermute | solution.py:20
  24.5 7.4 %collective-permute-start.11 = (bf16[128,512]{1,0:T(8,128)(2,1)S(1)}, bf16[128,512]{1,0:T(8,128)(2,1)S(1)}, u32[]{:S(2)}, u32[]{:S(2)}) collective-permute-start(bf16[128,512]{1,0:T(8,128)(2,1)S(1)} %get-tuple-element.59), channel_id=1, source_target_pairs={{0,24},{8,16},{16,8},{24,0},{1,25},{9,17},{17,9},{25,1},{2,26},{10... | collective-permute-start | bytes 393224 | tf_op jit(solution)/shard_map/ppermute | solution.py:20
  27.0 12.6 %collective-permute-start.8 = (bf16[128,1024]{1,0:T(8,128)(2,1)S(1)}, bf16[128,1024]{1,0:T(8,128)(2,1)S(1)}, u32[]{:S(2)}, u32[]{:S(2)}) collective-permute-start(bf16[128,1024]{1,0:T(8,128)(2,1)S(1)} %get-tuple-element.55.refs_0_), channel_id=1, source_target_pairs={{0,8},{8,0},{16,24},{24,16},{1,9},{9,1},{17,25},{25,17},{2,10},{10... | collective-permute-start | bytes 786440 | tf_op jit(solution)/shard_map/ppermute | solution.py:20
  28.6 11.1 %collective-permute-start.9 = (bf16[128,1024]{1,0:T(8,128)(2,1)S(1)}, bf16[128,1024]{1,0:T(8,128)(2,1)S(1)}, u32[]{:S(2)}, u32[]{:S(2)}) collective-permute-start(bf16[128,1024]{1,0:T(8,128)(2,1)S(1)} %get-tuple-element.55.refs_0_), channel_id=1, source_target_pairs={{0,16},{8,24},{16,0},{24,8},{1,17},{9,25},{17,1},{25,9},{2,18},{10... | collective-permute-start | bytes 786440 | tf_op jit(solution)/shard_map/ppermute | solution.py:20
  31.5 4.0 %collective-permute-start.10 = (bf16[128,128]{1,0:T(8,128)(2,1)S(1)}, bf16[128,128]{1,0:T(8,128)(2,1)S(1)}, u32[]{:S(2)}, u32[]{:S(2)}) collective-permute-start(bf16[128,128]{1,0:T(8,128)(2,1)S(1)} %get-tuple-element.58), channel_id=1, source_target_pairs={{0,2},{1,3},{2,0},{3,1},{4,6},{5,7},{6,4},{7,5},{8,10},{9,11},{10,... | collective-permute-start | bytes 98312 | tf_op jit(solution)/shard_map/ppermute | solution.py:20
  32.0 8.2 %collective-permute-start.12 = (bf16[128,512]{1,0:T(8,128)(2,1)S(1)}, bf16[128,512]{1,0:T(8,128)(2,1)S(1)}, u32[]{:S(2)}, u32[]{:S(2)}) collective-permute-start(bf16[128,512]{1,0:T(8,128)(2,1)S(1)} %collective-permute-done.11.refs_0_), channel_id=1, source_target_pairs={{0,2},{1,3},{2,0},{3,1},{4,6},{5,7},{6,4},{7,5},{8,10},{9,11},{10,... | collective-permute-start | bytes 393224 | tf_op jit(solution)/shard_map/ppermute | solution.py:20
  35.5 6.1 %collective-permute-start.13 = (bf16[128,128]{1,0:T(8,128)(2,1)S(1)}, bf16[128,128]{1,0:T(8,128)(2,1)S(1)}, u32[]{:S(2)}, u32[]{:S(2)}) collective-permute-start(bf16[128,128]{1,0:T(8,128)(2,1)S(1)} %add_convert_fusion), channel_id=1, source_target_pairs={{0,4},{1,5},{2,6},{3,7},{4,0},{5,1},{6,2},{7,3},{8,12},{9,13},{10,... | collective-permute-start | bytes 98312 | tf_op jit(solution)/shard_map/ppermute | solution.py:20
  39.7 3.5 %collective-permute-start.15 = (bf16[128,1024]{1,0:T(8,128)(2,1)S(1)}, bf16[128,1024]{1,0:T(8,128)(2,1)S(1)}, u32[]{:S(2)}, u32[]{:S(2)}) collective-permute-start(bf16[128,1024]{1,0:T(8,128)(2,1)S(1)} %collective-permute-done.8.refs_1_), channel_id=1, source_target_pairs={{0,1},{1,0},{2,3},{3,2},{4,5},{5,4},{6,7},{7,6},{8,9},{9,8},{10,11... | collective-permute-start | bytes 786440 | tf_op jit(solution)/shard_map/ppermute | solution.py:20
  39.7 3.5 %collective-permute-start.16 = (bf16[128,1024]{1,0:T(8,128)(2,1)S(1)}, bf16[128,1024]{1,0:T(8,128)(2,1)S(1)}, u32[]{:S(2)}, u32[]{:S(2)}) collective-permute-start(bf16[128,1024]{1,0:T(8,128)(2,1)S(1)} %collective-permute-done.9.refs_2_), channel_id=1, source_target_pairs={{0,1},{1,0},{2,3},{3,2},{4,5},{5,4},{6,7},{7,6},{8,9},{9,8},{10,11... | collective-permute-start | bytes 786440 | tf_op jit(solution)/shard_map/ppermute | solution.py:20
  40.2 1.4 %copy-start.2 = (f32[256]{0:T(256)S(1)}, f32[256]{0:T(256)}, u32[]{:S(2)}) copy-start(f32[256]{0:T(256)} %param.6) | copy-start | bytes 3076
  40.7 2.5 %collective-permute-start.17 = (bf16[128,1024]{1,0:T(8,128)(2,1)S(1)}, bf16[128,1024]{1,0:T(8,128)(2,1)S(1)}, u32[]{:S(2)}, u32[]{:S(2)}) collective-permute-start(bf16[128,1024]{1,0:T(8,128)(2,1)S(1)} %get-tuple-element.67.refs_3_), channel_id=1, source_target_pairs={{0,1},{1,0},{2,3},{3,2},{4,5},{5,4},{6,7},{7,6},{8,9},{9,8},{10,11... | collective-permute-start | bytes 786440 | tf_op jit(solution)/shard_map/ppermute | solution.py:20
  41.9 1.3 %collective-permute-start.14 = (bf16[256,128]{1,0:T(8,128)(2,1)S(1)}, bf16[256,128]{1,0:T(8,128)(2,1)S(1)}, u32[]{:S(2)}, u32[]{:S(2)}) collective-permute-start(bf16[256,128]{1,0:T(8,128)(2,1)S(1)} %get-tuple-element.64), channel_id=1, source_target_pairs={{0,1},{1,0},{2,3},{3,2},{4,5},{5,4},{6,7},{7,6},{8,9},{9,8},{10,11... | collective-permute-start | bytes 196616 | tf_op jit(solution)/shard_map/ppermute | solution.py:20

commit v5 on v2

--- a/solution.py
+++ b/solution.py
@@ -69,11 +69,9 @@
     cols = [
         pl.ds(pl.multiple_of(place, 128), piece.shape[0]) for piece, place in zip(pieces, places)
     ]
-    tok = jnp.concatenate(
-        [jnp.concatenate([ref[:, c] for c in cols], axis=1) for ref in (tok_a, tok_b)], axis=0
-    )
     weights = jnp.concatenate([piece[...] for piece in pieces], axis=0)
-    return dot(tok, weights)
+    blocks = [jnp.concatenate([ref[:, c] for c in cols], axis=1) for ref in (tok_a, tok_b)]
+    return jnp.concatenate([dot(block, weights) for block in blocks], axis=0)
 
 
 def places_near(shard, offsets):

time: 42.6 us -> 42.5 us (level)
  no operation moved by 1% of the time
where the time goes in v5:
time: 42.5 us; the launch traced here: 42.4 us
  starting transfers between devices  20.1 us (47%)
  waiting for transfers between devices  14.3 us (34%)
  Pallas kernels  7.91 us (19%)
    ppermute x18, starting transfers between devices, flip(): return lax.ppermute(x, axis, [(i, i ^ mask) for i in range(size)])  20.1 us
    ppermute x18, waiting for transfers between devices, flip(): return lax.ppermute(x, axis, [(i, i ^ mask) for i in range(size)])  14.3 us
    pallas_call x10, Pallas kernels, call(): pl.pallas_call(kernel, out_shape=outs, in_specs=in_specs, out_specs=out_s...  7.91 us
  transfers between devices with their start and end apart: 18, of which 7 were waited for; matrix products, arithmetic and copies ran while one was open for 0% of the time, Pallas kernels for 15%

profile of v5, /device:TPU:0, one launch (start us, length us, event | category | flops | bytes accessed | tf_op | source)
XLA Modules:
  0.0 42.4 jit_solution(9746757846206648182)
XLA Ops:
  0.0 0.5 %collective-permute-start = (bf16[256,4096]{1,0:T(8,128)(2,1)}, bf16[256,4096]{1,0:T(8,128)(2,1)S(1)}, u32[]{:S(2)}, u32[]{:S(2)}) collective-permute-start(bf16[256,4096]{1,0:T(8,128)(2,1)} %bitcast.3), channel_id=1, source_target_pairs={{0,1},{1,0},{2,3},{3,2},{4,5},{5,4},{6,7},{7,6},{8,9},{9,8},{10,11... | collective-permute-start | bytes 6291464 | tf_op jit(solution)/shard_map/ppermute | solution.py:20
  0.5 1.1 %shard_map.46 = bf16[256,384]{1,0:T(8,128)(2,1)S(1)} custom-call(bf16[1024,768]{1,0:T(8,128)(2,1)} %w_qkv.3), custom_call_target="tpu_custom_call" | custom-call | tf_op jit(solution)/shard_map/pallas_call | solution.py:188
  1.6 3.5 %collective-permute-start.1 = (bf16[256,384]{1,0:T(8,128)(2,1)S(1)}, bf16[256,384]{1,0:T(8,128)(2,1)S(1)}, u32[]{:S(2)}, u32[]{:S(2)}) collective-permute-start(bf16[256,384]{1,0:T(8,128)(2,1)S(1)} %shard_map.46), channel_id=1, source_target_pairs={{0,24},{8,16},{16,8},{24,0},{1,25},{9,17},{17,9},{25,1},{2,26},{10... | collective-permute-start | bytes 589832 | tf_op jit(solution)/shard_map/ppermute | solution.py:20
  5.1 1.2 %shard_map.47 = (bf16[1024,384]{1,0:T(8,128)(2,1)S(1)}, bf16[768,384]{1,0:T(8,128)(2,1)S(1)}, bf16[256,384]{1,0:T(8,128)(2,1)S(1)}) custom-call(bf16[1024,768]{1,0:T(8,128)(2,1)} %w_qkv.3), custom_call_target="tpu_custom_call" | custom-call | tf_op jit(solution)/shard_map/pallas_call | solution.py:188
  6.3 0.6 %collective-permute-start.6 = (bf16[768,384]{1,0:T(8,128)(2,1)S(1)}, bf16[768,384]{1,0:T(8,128)(2,1)S(1)}, u32[]{:S(2)}, u32[]{:S(2)}) collective-permute-start(bf16[768,384]{1,0:T(8,128)(2,1)S(1)} %get-tuple-element.42), channel_id=1, source_target_pairs={{0,8},{8,0},{16,24},{24,16},{1,9},{9,1},{17,25},{25,17},{2,10},{10... | collective-permute-start | bytes 1769480 | tf_op jit(solution)/shard_map/ppermute | solution.py:20
  7.0 3.9 %collective-permute-done.1.refs_1_ = bf16[256,384]{1,0:T(8,128)(2,1)S(1)} collective-permute-done((bf16[256,384]{1,0:T(8,128)(2,1)S(1)}, bf16[256,384]{1,0:T(8,128)(2,1)S(1)}, u32[]{:S(2)}, u32[]{:S(2)}) %collective-permute-start.1) | collective-permute-done | bytes 196640 | tf_op jit(solution)/shard_map/ppermute | solution.py:20
  10.8 3.0 %collective-permute-start.2 = (bf16[256,384]{1,0:T(8,128)(2,1)S(1)}, bf16[256,384]{1,0:T(8,128)(2,1)S(1)}, u32[]{:S(2)}, u32[]{:S(2)}) collective-permute-start(bf16[256,384]{1,0:T(8,128)(2,1)S(1)} %collective-permute-done.1.refs_1_), channel_id=1, source_target_pairs={{0,4},{1,5},{2,6},{3,7},{4,0},{5,1},{6,2},{7,3},{8,12},{9,13},{10,... | collective-permute-start | bytes 589832 | tf_op jit(solution)/shard_map/ppermute | solution.py:20
  13.8 0.7 %shard_map.48.refs_4_ = f32[512,384]{1,0:T(8,128)S(1)} custom-call(bf16[256,4096]{1,0:T(8,128)(2,1)S(1)} %bitcast.4, bf16[256,4096]{1,0:T(8,128)(2,1)S(1)} %collective-permute-done.tok_b, bf16[1024,384]{1,0:T(8,128)(2,1)S(1)} %get-tuple-element.37.refs_0_), custom_call_target="tpu_custom_call" | custom-call | flops 32768000000 | tf_op jit(solution)/shard_map/pallas_call | solution.py:188
  14.5 1.6 %collective-permute-start.7 = (bf16[256,384]{1,0:T(8,128)(2,1)S(1)}, bf16[256,384]{1,0:T(8,128)(2,1)S(1)}, u32[]{:S(2)}, u32[]{:S(2)}) collective-permute-start(bf16[256,384]{1,0:T(8,128)(2,1)S(1)} %collective-permute-done.1.refs_1_), channel_id=1, source_target_pairs={{0,2},{1,3},{2,0},{3,1},{4,6},{5,7},{6,4},{7,5},{8,10},{9,11},{10,... | collective-permute-start | bytes 589832 | tf_op jit(solution)/shard_map/ppermute | solution.py:20
  16.2 1.5 %collective-permute-start.4 = (bf16[256,384]{1,0:T(8,128)(2,1)S(1)}, bf16[256,384]{1,0:T(8,128)(2,1)S(1)}, u32[]{:S(2)}, u32[]{:S(2)}) collective-permute-start(bf16[256,384]{1,0:T(8,128)(2,1)S(1)} %get-tuple-element.41), channel_id=1, source_target_pairs={{0,8},{8,0},{16,24},{24,16},{1,9},{9,1},{17,25},{25,17},{2,10},{10... | collective-permute-start | bytes 589832 | tf_op jit(solution)/shard_map/ppermute | solution.py:20
  17.7 4.6 %collective-permute-done.2.refs_2_ = bf16[256,384]{1,0:T(8,128)(2,1)S(1)} collective-permute-done((bf16[256,384]{1,0:T(8,128)(2,1)S(1)}, bf16[256,384]{1,0:T(8,128)(2,1)S(1)}, u32[]{:S(2)}, u32[]{:S(2)}) %collective-permute-start.2) | collective-permute-done | bytes 196640 | tf_op jit(solution)/shard_map/ppermute | solution.py:20
  22.3 0.6 %collective-permute-start.3 = (bf16[256,384]{1,0:T(8,128)(2,1)S(1)}, bf16[256,384]{1,0:T(8,128)(2,1)S(1)}, u32[]{:S(2)}, u32[]{:S(2)}) collective-permute-start(bf16[256,384]{1,0:T(8,128)(2,1)S(1)} %collective-permute-done.2.refs_2_), channel_id=1, source_target_pairs={{0,2},{1,3},{2,0},{3,1},{4,6},{5,7},{6,4},{7,5},{8,10},{9,11},{10,... | collective-permute-start | bytes 589832 | tf_op jit(solution)/shard_map/ppermute | solution.py:20
  22.9 1.1 %collective-permute-done.6.refs_0_ = bf16[768,384]{1,0:T(8,128)(2,1)S(1)} collective-permute-done((bf16[768,384]{1,0:T(8,128)(2,1)S(1)}, bf16[768,384]{1,0:T(8,128)(2,1)S(1)}, u32[]{:S(2)}, u32[]{:S(2)}) %collective-permute-start.6) | collective-permute-done | bytes 589856 | tf_op jit(solution)/shard_map/ppermute | solution.py:20
  24.0 1.5 %collective-permute-start.11 = (bf16[128,512]{1,0:T(8,128)(2,1)S(1)}, bf16[128,512]{1,0:T(8,128)(2,1)S(1)}, u32[]{:S(2)}, u32[]{:S(2)}) collective-permute-start(bf16[128,512]{1,0:T(8,128)(2,1)S(1)} %get-tuple-element.57), channel_id=1, source_target_pairs={{0,24},{8,16},{16,8},{24,0},{1,25},{9,17},{17,9},{25,1},{2,26},{10... | collective-permute-start | bytes 393224 | tf_op jit(solution)/shard_map/ppermute | solution.py:20
  25.5 0.5 %collective-permute-start.8 = (bf16[128,1024]{1,0:T(8,128)(2,1)S(1)}, bf16[128,1024]{1,0:T(8,128)(2,1)S(1)}, u32[]{:S(2)}, u32[]{:S(2)}) collective-permute-start(bf16[128,1024]{1,0:T(8,128)(2,1)S(1)} %get-tuple-element.53.refs_0_), channel_id=1, source_target_pairs={{0,8},{8,0},{16,24},{24,16},{1,9},{9,1},{17,25},{25,17},{2,10},{10... | collective-permute-start | bytes 786440 | tf_op jit(solution)/shard_map/ppermute | solution.py:20
  26.0 1.0 %shard_map.50.refs_2_ = f32[512,384]{1,0:T(8,128)S(1)} custom-call(bf16[256,4096]{1,0:T(8,128)(2,1)S(1)} %bitcast.5, bf16[256,4096]{1,0:T(8,128)(2,1)S(1)} %collective-permute-done.tok_b, bf16[768,384]{1,0:T(8,128)(2,1)S(1)} %collective-permute-done.6.refs_0_, bf16[256,384]{1,0:T(8,128)(2,1)S(1)} %collective-permute-done.1.refs_1_, ...), custom_call_target="tpu_custom_call" | custom-call | flops 32768 | tf_op jit(solution)/shard_map/pallas_call | solution.py:188
  27.0 1.2 %collective-permute-done.4.refs_0_ = bf16[256,384]{1,0:T(8,128)(2,1)S(1)} collective-permute-done((bf16[256,384]{1,0:T(8,128)(2,1)S(1)}, bf16[256,384]{1,0:T(8,128)(2,1)S(1)}, u32[]{:S(2)}, u32[]{:S(2)}) %collective-permute-start.4) | collective-permute-done | bytes 196640 | tf_op jit(solution)/shard_map/ppermute | solution.py:20
  28.2 0.3 collective-permute-start.9
  28.5 0.8 %shard_map.51.refs_1_ = f32[512,384]{1,0:T(8,128)S(1)} custom-call(bf16[256,4096]{1,0:T(8,128)(2,1)S(1)} %bitcast.6, bf16[256,4096]{1,0:T(8,128)(2,1)S(1)} %collective-permute-done.tok_b, bf16[256,384]{1,0:T(8,128)(2,1)S(1)} %collective-permute-done.4.refs_0_, bf16[1024,384]{1,0:T(8,128)(2,1)S(1)} %collective-permute-done.5.refs_1_, ...), custom_call_target="tpu_custom_call" | custom-call | flops 32768 | tf_op jit(solution)/shard_map/pallas_call | solution.py:188
  29.4 0.5 %shard_map.52 = (bf16[2,256,256]{2,1,0:T(8,128)(2,1)S(1)}, bf16[2,256,128]{2,1,0:T(8,128)(2,1)S(1)}, f32[2,128,128]{2,1,0:T(8,128)S(1)}, bf16[128,128]{1,0:T(8,128)(2,1)S(1)}) custom-call(bf16[256,4096]{1,0:T(8,128)(2,1)S(1)} %bitcast.7, bf16[256,4096]{1,0:T(8,128)(2,1)S(1)} %collective-permute-done.tok_b, ...), custom_call_target="tpu_custom_call" | custom-call | flops 100663296 | tf_op jit(solution)/shard_map/pallas_call | solution.py:188
  29.9 1.8 %collective-permute-start.10 = (bf16[128,128]{1,0:T(8,128)(2,1)S(1)}, bf16[128,128]{1,0:T(8,128)(2,1)S(1)}, u32[]{:S(2)}, u32[]{:S(2)}) collective-permute-start(bf16[128,128]{1,0:T(8,128)(2,1)S(1)} %get-tuple-element.56), channel_id=1, source_target_pairs={{0,2},{1,3},{2,0},{3,1},{4,6},{5,7},{6,4},{7,5},{8,10},{9,11},{10,... | collective-permute-start | bytes 98312 | tf_op jit(solution)/shard_map/ppermute | solution.py:20
  31.7 1.2 %collective-permute-start.12 = (bf16[128,512]{1,0:T(8,128)(2,1)S(1)}, bf16[128,512]{1,0:T(8,128)(2,1)S(1)}, u32[]{:S(2)}, u32[]{:S(2)}) collective-permute-start(bf16[128,512]{1,0:T(8,128)(2,1)S(1)} %collective-permute-done.11.refs_0_), channel_id=1, source_target_pairs={{0,2},{1,3},{2,0},{3,1},{4,6},{5,7},{6,4},{7,5},{8,10},{9,11},{10,... | collective-permute-start | bytes 393224 | tf_op jit(solution)/shard_map/ppermute | solution.py:20
  32.9 1.3 %collective-permute-done.10.refs_0_ = bf16[128,128]{1,0:T(8,128)(2,1)S(1)} collective-permute-done((bf16[128,128]{1,0:T(8,128)(2,1)S(1)}, bf16[128,128]{1,0:T(8,128)(2,1)S(1)}, u32[]{:S(2)}, u32[]{:S(2)}) %collective-permute-start.10) | collective-permute-done | bytes 32800 | tf_op jit(solution)/shard_map/ppermute | solution.py:20
  34.1 2.7 %collective-permute-start.13 = (bf16[128,128]{1,0:T(8,128)(2,1)S(1)}, bf16[128,128]{1,0:T(8,128)(2,1)S(1)}, u32[]{:S(2)}, u32[]{:S(2)}) collective-permute-start(bf16[128,128]{1,0:T(8,128)(2,1)S(1)} %add_convert_fusion), channel_id=1, source_target_pairs={{0,4},{1,5},{2,6},{3,7},{4,0},{5,1},{6,2},{7,3},{8,12},{9,13},{10,... | collective-permute-start | bytes 98312 | tf_op jit(solution)/shard_map/ppermute | solution.py:20
  36.8 0.5 %collective-permute-start.16 = (bf16[128,1024]{1,0:T(8,128)(2,1)S(1)}, bf16[128,1024]{1,0:T(8,128)(2,1)S(1)}, u32[]{:S(2)}, u32[]{:S(2)}) collective-permute-start(bf16[128,1024]{1,0:T(8,128)(2,1)S(1)} %collective-permute-done.9.refs_2_), channel_id=1, source_target_pairs={{0,1},{1,0},{2,3},{3,2},{4,5},{5,4},{6,7},{7,6},{8,9},{9,8},{10,11... | collective-permute-start | bytes 786440 | tf_op jit(solution)/shard_map/ppermute | solution.py:20
  37.3 0.5 %shard_map.53 = (f32[2,256,128]{2,1,0:T(8,128)S(1)}, bf16[128,1024]{1,0:T(8,128)(2,1)S(1)}) custom-call(bf16[2,256,256]{2,1,0:T(8,128)(2,1)S(1)} %get-tuple-element.54.act, bf16[2,256,128]{2,1,0:T(8,128)(2,1)S(1)} %get-tuple-element.55.values, bf16[128,512]{1,0:T(8,128)(2,1)S(1)} %collective-permute-done.11.refs_0_, ...), custom_call_target="tpu_custom_call" | custom-call | flops 32768000000 | tf_op jit(solution)/shard_map/pallas_call | solution.py:188
  37.9 0.1 collective-permute-start.17
  38.0 1.0 %collective-permute-done.13.refs_1_ = bf16[128,128]{1,0:T(8,128)(2,1)S(1)} collective-permute-done((bf16[128,128]{1,0:T(8,128)(2,1)S(1)}, bf16[128,128]{1,0:T(8,128)(2,1)S(1)}, u32[]{:S(2)}, u32[]{:S(2)}) %collective-permute-start.13) | collective-permute-done | bytes 32800 | tf_op jit(solution)/shard_map/ppermute | solution.py:20
  39.0 0.3 shard_map.54
  39.4 0.1 collective-permute-start.14
  39.4 1.2 %collective-permute-done.14.other = bf16[256,128]{1,0:T(8,128)(2,1)S(1)} collective-permute-done((bf16[256,128]{1,0:T(8,128)(2,1)S(1)}, bf16[256,128]{1,0:T(8,128)(2,1)S(1)}, u32[]{:S(2)}, u32[]{:S(2)}) %collective-permute-start.14) | collective-permute-done | bytes 65568 | tf_op jit(solution)/shard_map/ppermute | solution.py:20
  40.7 1.7 %shard_map.55 = bf16[256,4096]{1,0:T(8,128)(2,1)} custom-call(bf16[256,128]{1,0:T(8,128)(2,1)S(1)} %get-tuple-element.61.own, bf16[256,128]{1,0:T(8,128)(2,1)S(1)} %collective-permute-done.14.other, bf16[128,1024]{1,0:T(8,128)(2,1)S(1)} %get-tuple-element.53.refs_0_, bf16[128,1024]{1,0:T(8,128)(2,1)S(1)} %collective-permute-done.8.refs_1_, ...), custom_call_target="tpu_custom_call" | custom-call | flops 536870912 | bytes 2097152 | tf_op jit(solution)/shard_map/pallas_call | solution.py:188
  (21 shorter events, 0.2 us)
Async XLA Ops:
  0.0 13.8 %copy-start = (bf16[1,256,4096]{2,1,0:T(8,128)(2,1)S(1)}, bf16[1,256,4096]{2,1,0:T(8,128)(2,1)}, u32[]{:S(2)}) copy-start(bf16[1,256,4096]{2,1,0:T(8,128)(2,1)} %param.4) | copy-start | bytes 6291460
  0.0 13.8 %collective-permute-start = (bf16[256,4096]{1,0:T(8,128)(2,1)}, bf16[256,4096]{1,0:T(8,128)(2,1)S(1)}, u32[]{:S(2)}, u32[]{:S(2)}) collective-permute-start(bf16[256,4096]{1,0:T(8,128)(2,1)} %bitcast.3), channel_id=1, source_target_pairs={{0,1},{1,0},{2,3},{3,2},{4,5},{5,4},{6,7},{7,6},{8,9},{9,8},{10,11... | collective-permute-start | bytes 6291464 | tf_op jit(solution)/shard_map/ppermute | solution.py:20
  1.6 9.2 %collective-permute-start.1 = (bf16[256,384]{1,0:T(8,128)(2,1)S(1)}, bf16[256,384]{1,0:T(8,128)(2,1)S(1)}, u32[]{:S(2)}, u32[]{:S(2)}) collective-permute-start(bf16[256,384]{1,0:T(8,128)(2,1)S(1)} %shard_map.46), channel_id=1, source_target_pairs={{0,24},{8,16},{16,8},{24,0},{1,25},{9,17},{17,9},{25,1},{2,26},{10... | collective-permute-start | bytes 589832 | tf_op jit(solution)/shard_map/ppermute | solution.py:20
  6.3 17.7 %collective-permute-start.6 = (bf16[768,384]{1,0:T(8,128)(2,1)S(1)}, bf16[768,384]{1,0:T(8,128)(2,1)S(1)}, u32[]{:S(2)}, u32[]{:S(2)}) collective-permute-start(bf16[768,384]{1,0:T(8,128)(2,1)S(1)} %get-tuple-element.42), channel_id=1, source_target_pairs={{0,8},{8,0},{16,24},{24,16},{1,9},{9,1},{17,25},{25,17},{2,10},{10... | collective-permute-start | bytes 1769480 | tf_op jit(solution)/shard_map/ppermute | solution.py:20
  6.9 16.0 %copy-start.1 = (bf16[256,1024]{1,0:T(8,128)(2,1)S(1)}, bf16[256,1024]{1,0:T(8,128)(2,1)}, u32[]{:S(2)}) copy-start(bf16[256,1024]{1,0:T(8,128)(2,1)} %w_out.1) | copy-start | bytes 1572868
  6.9 21.6 %collective-permute-start.5 = (bf16[1024,384]{1,0:T(8,128)(2,1)S(1)}, bf16[1024,384]{1,0:T(8,128)(2,1)S(1)}, u32[]{:S(2)}, u32[]{:S(2)}) collective-permute-start(bf16[1024,384]{1,0:T(8,128)(2,1)S(1)} %get-tuple-element.37.refs_0_), channel_id=1, source_target_pairs={{0,16},{8,24},{16,0},{24,8},{1,17},{9,25},{17,1},{25,9},{2,18},{10... | collective-permute-start | bytes 2359304 | tf_op jit(solution)/shard_map/ppermute | solution.py:20
  10.8 11.5 %collective-permute-start.2 = (bf16[256,384]{1,0:T(8,128)(2,1)S(1)}, bf16[256,384]{1,0:T(8,128)(2,1)S(1)}, u32[]{:S(2)}, u32[]{:S(2)}) collective-permute-start(bf16[256,384]{1,0:T(8,128)(2,1)S(1)} %collective-permute-done.1.refs_1_), channel_id=1, source_target_pairs={{0,4},{1,5},{2,6},{3,7},{4,0},{5,1},{6,2},{7,3},{8,12},{9,13},{10,... | collective-permute-start | bytes 589832 | tf_op jit(solution)/shard_map/ppermute | solution.py:20
  14.5 10.9 %collective-permute-start.7 = (bf16[256,384]{1,0:T(8,128)(2,1)S(1)}, bf16[256,384]{1,0:T(8,128)(2,1)S(1)}, u32[]{:S(2)}, u32[]{:S(2)}) collective-permute-start(bf16[256,384]{1,0:T(8,128)(2,1)S(1)} %collective-permute-done.1.refs_1_), channel_id=1, source_target_pairs={{0,2},{1,3},{2,0},{3,1},{4,6},{5,7},{6,4},{7,5},{8,10},{9,11},{10,... | collective-permute-start | bytes 589832 | tf_op jit(solution)/shard_map/ppermute | solution.py:20
  16.2 12.0 %collective-permute-start.4 = (bf16[256,384]{1,0:T(8,128)(2,1)S(1)}, bf16[256,384]{1,0:T(8,128)(2,1)S(1)}, u32[]{:S(2)}, u32[]{:S(2)}) collective-permute-start(bf16[256,384]{1,0:T(8,128)(2,1)S(1)} %get-tuple-element.41), channel_id=1, source_target_pairs={{0,8},{8,0},{16,24},{24,16},{1,9},{9,1},{17,25},{25,17},{2,10},{10... | collective-permute-start | bytes 589832 | tf_op jit(solution)/shard_map/ppermute | solution.py:20
  22.3 7.1 %collective-permute-start.3 = (bf16[256,384]{1,0:T(8,128)(2,1)S(1)}, bf16[256,384]{1,0:T(8,128)(2,1)S(1)}, u32[]{:S(2)}, u32[]{:S(2)}) collective-permute-start(bf16[256,384]{1,0:T(8,128)(2,1)S(1)} %collective-permute-done.2.refs_2_), channel_id=1, source_target_pairs={{0,2},{1,3},{2,0},{3,1},{4,6},{5,7},{6,4},{7,5},{8,10},{9,11},{10,... | collective-permute-start | bytes 589832 | tf_op jit(solution)/shard_map/ppermute | solution.py:20
  24.0 7.7 %collective-permute-start.11 = (bf16[128,512]{1,0:T(8,128)(2,1)S(1)}, bf16[128,512]{1,0:T(8,128)(2,1)S(1)}, u32[]{:S(2)}, u32[]{:S(2)}) collective-permute-start(bf16[128,512]{1,0:T(8,128)(2,1)S(1)} %get-tuple-element.57), channel_id=1, source_target_pairs={{0,24},{8,16},{16,8},{24,0},{1,25},{9,17},{17,9},{25,1},{2,26},{10... | collective-permute-start | bytes 393224 | tf_op jit(solution)/shard_map/ppermute | solution.py:20
  25.5 11.4 %collective-permute-start.8 = (bf16[128,1024]{1,0:T(8,128)(2,1)S(1)}, bf16[128,1024]{1,0:T(8,128)(2,1)S(1)}, u32[]{:S(2)}, u32[]{:S(2)}) collective-permute-start(bf16[128,1024]{1,0:T(8,128)(2,1)S(1)} %get-tuple-element.53.refs_0_), channel_id=1, source_target_pairs={{0,8},{8,0},{16,24},{24,16},{1,9},{9,1},{17,25},{25,17},{2,10},{10... | collective-permute-start | bytes 786440 | tf_op jit(solution)/shard_map/ppermute | solution.py:20
  28.2 8.6 %collective-permute-start.9 = (bf16[128,1024]{1,0:T(8,128)(2,1)S(1)}, bf16[128,1024]{1,0:T(8,128)(2,1)S(1)}, u32[]{:S(2)}, u32[]{:S(2)}) collective-permute-start(bf16[128,1024]{1,0:T(8,128)(2,1)S(1)} %get-tuple-element.53.refs_0_), channel_id=1, source_target_pairs={{0,16},{8,24},{16,0},{24,8},{1,17},{9,25},{17,1},{25,9},{2,18},{10... | collective-permute-start | bytes 786440 | tf_op jit(solution)/shard_map/ppermute | solution.py:20
  29.9 4.2 %collective-permute-start.10 = (bf16[128,128]{1,0:T(8,128)(2,1)S(1)}, bf16[128,128]{1,0:T(8,128)(2,1)S(1)}, u32[]{:S(2)}, u32[]{:S(2)}) collective-permute-start(bf16[128,128]{1,0:T(8,128)(2,1)S(1)} %get-tuple-element.56), channel_id=1, source_target_pairs={{0,2},{1,3},{2,0},{3,1},{4,6},{5,7},{6,4},{7,5},{8,10},{9,11},{10,... | collective-permute-start | bytes 98312 | tf_op jit(solution)/shard_map/ppermute | solution.py:20
  31.7 5.7 %collective-permute-start.12 = (bf16[128,512]{1,0:T(8,128)(2,1)S(1)}, bf16[128,512]{1,0:T(8,128)(2,1)S(1)}, u32[]{:S(2)}, u32[]{:S(2)}) collective-permute-start(bf16[128,512]{1,0:T(8,128)(2,1)S(1)} %collective-permute-done.11.refs_0_), channel_id=1, source_target_pairs={{0,2},{1,3},{2,0},{3,1},{4,6},{5,7},{6,4},{7,5},{8,10},{9,11},{10,... | collective-permute-start | bytes 393224 | tf_op jit(solution)/shard_map/ppermute | solution.py:20
  34.1 4.9 %collective-permute-start.13 = (bf16[128,128]{1,0:T(8,128)(2,1)S(1)}, bf16[128,128]{1,0:T(8,128)(2,1)S(1)}, u32[]{:S(2)}, u32[]{:S(2)}) collective-permute-start(bf16[128,128]{1,0:T(8,128)(2,1)S(1)} %add_convert_fusion), channel_id=1, source_target_pairs={{0,4},{1,5},{2,6},{3,7},{4,0},{5,1},{6,2},{7,3},{8,12},{9,13},{10,... | collective-permute-start | bytes 98312 | tf_op jit(solution)/shard_map/ppermute | solution.py:20
  36.8 3.8 %collective-permute-start.15 = (bf16[128,1024]{1,0:T(8,128)(2,1)S(1)}, bf16[128,1024]{1,0:T(8,128)(2,1)S(1)}, u32[]{:S(2)}, u32[]{:S(2)}) collective-permute-start(bf16[128,1024]{1,0:T(8,128)(2,1)S(1)} %collective-permute-done.8.refs_1_), channel_id=1, source_target_pairs={{0,1},{1,0},{2,3},{3,2},{4,5},{5,4},{6,7},{7,6},{8,9},{9,8},{10,11... | collective-permute-start | bytes 786440 | tf_op jit(solution)/shard_map/ppermute | solution.py:20
  36.8 3.8 %collective-permute-start.16 = (bf16[128,1024]{1,0:T(8,128)(2,1)S(1)}, bf16[128,1024]{1,0:T(8,128)(2,1)S(1)}, u32[]{:S(2)}, u32[]{:S(2)}) collective-permute-start(bf16[128,1024]{1,0:T(8,128)(2,1)S(1)} %collective-permute-done.9.refs_2_), channel_id=1, source_target_pairs={{0,1},{1,0},{2,3},{3,2},{4,5},{5,4},{6,7},{7,6},{8,9},{9,8},{10,11... | collective-permute-start | bytes 786440 | tf_op jit(solution)/shard_map/ppermute | solution.py:20
  37.3 1.7 %copy-start.2 = (f32[256]{0:T(256)S(1)}, f32[256]{0:T(256)}, u32[]{:S(2)}) copy-start(f32[256]{0:T(256)} %param.6) | copy-start | bytes 3076
  37.9 2.8 %collective-permute-start.17 = (bf16[128,1024]{1,0:T(8,128)(2,1)S(1)}, bf16[128,1024]{1,0:T(8,128)(2,1)S(1)}, u32[]{:S(2)}, u32[]{:S(2)}) collective-permute-start(bf16[128,1024]{1,0:T(8,128)(2,1)S(1)} %get-tuple-element.65.refs_3_), channel_id=1, source_target_pairs={{0,1},{1,0},{2,3},{3,2},{4,5},{5,4},{6,7},{7,6},{8,9},{9,8},{10,11... | collective-permute-start | bytes 786440 | tf_op jit(solution)/shard_map/ppermute | solution.py:20
  39.4 1.3 %collective-permute-start.14 = (bf16[256,128]{1,0:T(8,128)(2,1)S(1)}, bf16[256,128]{1,0:T(8,128)(2,1)S(1)}, u32[]{:S(2)}, u32[]{:S(2)}) collective-permute-start(bf16[256,128]{1,0:T(8,128)(2,1)S(1)} %get-tuple-element.62), channel_id=1, source_target_pairs={{0,1},{1,0},{2,3},{3,2},{4,5},{5,4},{6,7},{7,6},{8,9},{9,8},{10,11... | collective-permute-start | bytes 196616 | tf_op jit(solution)/shard_map/ppermute | solution.py:20

commit v6 on v5

--- a/solution.py
+++ b/solution.py
@@ -158,7 +158,7 @@
     slot = 0
     for my_rows, their_rows, place in zip(mine, theirs, places()):
         width = my_rows.shape[1]
-        step = min(width, 512)
+        step = min(width, 256)
         for at_col in range(0, width, step):
             part = slice(at_col, at_col + step)
             weights = jnp.concatenate([my_rows[:, part], their_rows[:, part]], axis=0)

time: 42.5 us -> 42.6 us (level)
  no operation moved by 1% of the time
where the time goes in v6:
time: 42.6 us; the launch traced here: 42.4 us
  starting transfers between devices  20.1 us (47%)
  waiting for transfers between devices  14.3 us (34%)
  Pallas kernels  7.94 us (19%)
    ppermute x18, starting transfers between devices, flip(): return lax.ppermute(x, axis, [(i, i ^ mask) for i in range(size)])  20.1 us
    ppermute x18, waiting for transfers between devices, flip(): return lax.ppermute(x, axis, [(i, i ^ mask) for i in range(size)])  14.3 us
    pallas_call x10, Pallas kernels, call(): pl.pallas_call(kernel, out_shape=outs, in_specs=in_specs, out_specs=out_s...  7.94 us
  transfers between devices with their start and end apart: 18, of which 7 were waited for; matrix products, arithmetic and copies ran while one was open for 0% of the time, Pallas kernels for 15%

profile of v6, /device:TPU:0, one launch (start us, length us, event | category | flops | bytes accessed | tf_op | source)
XLA Modules:
  0.0 42.4 jit_solution(3803438538264749452)
XLA Ops:
  0.0 0.5 %collective-permute-start = (bf16[256,4096]{1,0:T(8,128)(2,1)}, bf16[256,4096]{1,0:T(8,128)(2,1)S(1)}, u32[]{:S(2)}, u32[]{:S(2)}) collective-permute-start(bf16[256,4096]{1,0:T(8,128)(2,1)} %bitcast.3), channel_id=1, source_target_pairs={{0,1},{1,0},{2,3},{3,2},{4,5},{5,4},{6,7},{7,6},{8,9},{9,8},{10,11... | collective-permute-start | bytes 6291464 | tf_op jit(solution)/shard_map/ppermute | solution.py:20
  0.5 1.1 %shard_map.46 = bf16[256,384]{1,0:T(8,128)(2,1)S(1)} custom-call(bf16[1024,768]{1,0:T(8,128)(2,1)} %w_qkv.3), custom_call_target="tpu_custom_call" | custom-call | tf_op jit(solution)/shard_map/pallas_call | solution.py:188
  1.6 3.5 %collective-permute-start.1 = (bf16[256,384]{1,0:T(8,128)(2,1)S(1)}, bf16[256,384]{1,0:T(8,128)(2,1)S(1)}, u32[]{:S(2)}, u32[]{:S(2)}) collective-permute-start(bf16[256,384]{1,0:T(8,128)(2,1)S(1)} %shard_map.46), channel_id=1, source_target_pairs={{0,24},{8,16},{16,8},{24,0},{1,25},{9,17},{17,9},{25,1},{2,26},{10... | collective-permute-start | bytes 589832 | tf_op jit(solution)/shard_map/ppermute | solution.py:20
  5.1 1.2 %shard_map.47 = (bf16[1024,384]{1,0:T(8,128)(2,1)S(1)}, bf16[768,384]{1,0:T(8,128)(2,1)S(1)}, bf16[256,384]{1,0:T(8,128)(2,1)S(1)}) custom-call(bf16[1024,768]{1,0:T(8,128)(2,1)} %w_qkv.3), custom_call_target="tpu_custom_call" | custom-call | tf_op jit(solution)/shard_map/pallas_call | solution.py:188
  6.3 0.6 %collective-permute-start.6 = (bf16[768,384]{1,0:T(8,128)(2,1)S(1)}, bf16[768,384]{1,0:T(8,128)(2,1)S(1)}, u32[]{:S(2)}, u32[]{:S(2)}) collective-permute-start(bf16[768,384]{1,0:T(8,128)(2,1)S(1)} %get-tuple-element.42), channel_id=1, source_target_pairs={{0,8},{8,0},{16,24},{24,16},{1,9},{9,1},{17,25},{25,17},{2,10},{10... | collective-permute-start | bytes 1769480 | tf_op jit(solution)/shard_map/ppermute | solution.py:20
  7.0 3.9 %collective-permute-done.1.refs_1_ = bf16[256,384]{1,0:T(8,128)(2,1)S(1)} collective-permute-done((bf16[256,384]{1,0:T(8,128)(2,1)S(1)}, bf16[256,384]{1,0:T(8,128)(2,1)S(1)}, u32[]{:S(2)}, u32[]{:S(2)}) %collective-permute-start.1) | collective-permute-done | bytes 196640 | tf_op jit(solution)/shard_map/ppermute | solution.py:20
  10.8 3.0 %collective-permute-start.2 = (bf16[256,384]{1,0:T(8,128)(2,1)S(1)}, bf16[256,384]{1,0:T(8,128)(2,1)S(1)}, u32[]{:S(2)}, u32[]{:S(2)}) collective-permute-start(bf16[256,384]{1,0:T(8,128)(2,1)S(1)} %collective-permute-done.1.refs_1_), channel_id=1, source_target_pairs={{0,4},{1,5},{2,6},{3,7},{4,0},{5,1},{6,2},{7,3},{8,12},{9,13},{10,... | collective-permute-start | bytes 589832 | tf_op jit(solution)/shard_map/ppermute | solution.py:20
  13.8 0.7 %shard_map.48.refs_4_ = f32[512,384]{1,0:T(8,128)S(1)} custom-call(bf16[256,4096]{1,0:T(8,128)(2,1)S(1)} %bitcast.4, bf16[256,4096]{1,0:T(8,128)(2,1)S(1)} %collective-permute-done.tok_b, bf16[1024,384]{1,0:T(8,128)(2,1)S(1)} %get-tuple-element.37.refs_0_), custom_call_target="tpu_custom_call" | custom-call | flops 32768000000 | tf_op jit(solution)/shard_map/pallas_call | solution.py:188
  14.5 1.6 %collective-permute-start.7 = (bf16[256,384]{1,0:T(8,128)(2,1)S(1)}, bf16[256,384]{1,0:T(8,128)(2,1)S(1)}, u32[]{:S(2)}, u32[]{:S(2)}) collective-permute-start(bf16[256,384]{1,0:T(8,128)(2,1)S(1)} %collective-permute-done.1.refs_1_), channel_id=1, source_target_pairs={{0,2},{1,3},{2,0},{3,1},{4,6},{5,7},{6,4},{7,5},{8,10},{9,11},{10,... | collective-permute-start | bytes 589832 | tf_op jit(solution)/shard_map/ppermute | solution.py:20
  16.2 1.5 %collective-permute-start.4 = (bf16[256,384]{1,0:T(8,128)(2,1)S(1)}, bf16[256,384]{1,0:T(8,128)(2,1)S(1)}, u32[]{:S(2)}, u32[]{:S(2)}) collective-permute-start(bf16[256,384]{1,0:T(8,128)(2,1)S(1)} %get-tuple-element.41), channel_id=1, source_target_pairs={{0,8},{8,0},{16,24},{24,16},{1,9},{9,1},{17,25},{25,17},{2,10},{10... | collective-permute-start | bytes 589832 | tf_op jit(solution)/shard_map/ppermute | solution.py:20
  17.7 4.6 %collective-permute-done.2.refs_2_ = bf16[256,384]{1,0:T(8,128)(2,1)S(1)} collective-permute-done((bf16[256,384]{1,0:T(8,128)(2,1)S(1)}, bf16[256,384]{1,0:T(8,128)(2,1)S(1)}, u32[]{:S(2)}, u32[]{:S(2)}) %collective-permute-start.2) | collective-permute-done | bytes 196640 | tf_op jit(solution)/shard_map/ppermute | solution.py:20
  22.3 0.6 %collective-permute-start.3 = (bf16[256,384]{1,0:T(8,128)(2,1)S(1)}, bf16[256,384]{1,0:T(8,128)(2,1)S(1)}, u32[]{:S(2)}, u32[]{:S(2)}) collective-permute-start(bf16[256,384]{1,0:T(8,128)(2,1)S(1)} %collective-permute-done.2.refs_2_), channel_id=1, source_target_pairs={{0,2},{1,3},{2,0},{3,1},{4,6},{5,7},{6,4},{7,5},{8,10},{9,11},{10,... | collective-permute-start | bytes 589832 | tf_op jit(solution)/shard_map/ppermute | solution.py:20
  22.9 1.1 %collective-permute-done.6.refs_0_ = bf16[768,384]{1,0:T(8,128)(2,1)S(1)} collective-permute-done((bf16[768,384]{1,0:T(8,128)(2,1)S(1)}, bf16[768,384]{1,0:T(8,128)(2,1)S(1)}, u32[]{:S(2)}, u32[]{:S(2)}) %collective-permute-start.6) | collective-permute-done | bytes 589856 | tf_op jit(solution)/shard_map/ppermute | solution.py:20
  24.0 1.5 %collective-permute-start.11 = (bf16[128,512]{1,0:T(8,128)(2,1)S(1)}, bf16[128,512]{1,0:T(8,128)(2,1)S(1)}, u32[]{:S(2)}, u32[]{:S(2)}) collective-permute-start(bf16[128,512]{1,0:T(8,128)(2,1)S(1)} %get-tuple-element.57), channel_id=1, source_target_pairs={{0,24},{8,16},{16,8},{24,0},{1,25},{9,17},{17,9},{25,1},{2,26},{10... | collective-permute-start | bytes 393224 | tf_op jit(solution)/shard_map/ppermute | solution.py:20
  25.5 0.5 %collective-permute-start.8 = (bf16[128,1024]{1,0:T(8,128)(2,1)S(1)}, bf16[128,1024]{1,0:T(8,128)(2,1)S(1)}, u32[]{:S(2)}, u32[]{:S(2)}) collective-permute-start(bf16[128,1024]{1,0:T(8,128)(2,1)S(1)} %get-tuple-element.53.refs_0_), channel_id=1, source_target_pairs={{0,8},{8,0},{16,24},{24,16},{1,9},{9,1},{17,25},{25,17},{2,10},{10... | collective-permute-start | bytes 786440 | tf_op jit(solution)/shard_map/ppermute | solution.py:20
  26.0 1.0 %shard_map.50.refs_2_ = f32[512,384]{1,0:T(8,128)S(1)} custom-call(bf16[256,4096]{1,0:T(8,128)(2,1)S(1)} %bitcast.5, bf16[256,4096]{1,0:T(8,128)(2,1)S(1)} %collective-permute-done.tok_b, bf16[768,384]{1,0:T(8,128)(2,1)S(1)} %collective-permute-done.6.refs_0_, bf16[256,384]{1,0:T(8,128)(2,1)S(1)} %collective-permute-done.1.refs_1_, ...), custom_call_target="tpu_custom_call" | custom-call | flops 32768 | tf_op jit(solution)/shard_map/pallas_call | solution.py:188
  27.0 1.2 %collective-permute-done.4.refs_0_ = bf16[256,384]{1,0:T(8,128)(2,1)S(1)} collective-permute-done((bf16[256,384]{1,0:T(8,128)(2,1)S(1)}, bf16[256,384]{1,0:T(8,128)(2,1)S(1)}, u32[]{:S(2)}, u32[]{:S(2)}) %collective-permute-start.4) | collective-permute-done | bytes 196640 | tf_op jit(solution)/shard_map/ppermute | solution.py:20
  28.2 0.3 collective-permute-start.9
  28.5 0.8 %shard_map.51.refs_1_ = f32[512,384]{1,0:T(8,128)S(1)} custom-call(bf16[256,4096]{1,0:T(8,128)(2,1)S(1)} %bitcast.6, bf16[256,4096]{1,0:T(8,128)(2,1)S(1)} %collective-permute-done.tok_b, bf16[256,384]{1,0:T(8,128)(2,1)S(1)} %collective-permute-done.4.refs_0_, bf16[1024,384]{1,0:T(8,128)(2,1)S(1)} %collective-permute-done.5.refs_1_, ...), custom_call_target="tpu_custom_call" | custom-call | flops 32768 | tf_op jit(solution)/shard_map/pallas_call | solution.py:188
  29.4 0.5 %shard_map.52 = (bf16[2,256,256]{2,1,0:T(8,128)(2,1)S(1)}, bf16[2,256,128]{2,1,0:T(8,128)(2,1)S(1)}, f32[2,128,128]{2,1,0:T(8,128)S(1)}, bf16[128,128]{1,0:T(8,128)(2,1)S(1)}) custom-call(bf16[256,4096]{1,0:T(8,128)(2,1)S(1)} %bitcast.7, bf16[256,4096]{1,0:T(8,128)(2,1)S(1)} %collective-permute-done.tok_b, ...), custom_call_target="tpu_custom_call" | custom-call | flops 100663296 | tf_op jit(solution)/shard_map/pallas_call | solution.py:188
  29.9 1.8 %collective-permute-start.10 = (bf16[128,128]{1,0:T(8,128)(2,1)S(1)}, bf16[128,128]{1,0:T(8,128)(2,1)S(1)}, u32[]{:S(2)}, u32[]{:S(2)}) collective-permute-start(bf16[128,128]{1,0:T(8,128)(2,1)S(1)} %get-tuple-element.56), channel_id=1, source_target_pairs={{0,2},{1,3},{2,0},{3,1},{4,6},{5,7},{6,4},{7,5},{8,10},{9,11},{10,... | collective-permute-start | bytes 98312 | tf_op jit(solution)/shard_map/ppermute | solution.py:20
  31.7 1.2 %collective-permute-start.12 = (bf16[128,512]{1,0:T(8,128)(2,1)S(1)}, bf16[128,512]{1,0:T(8,128)(2,1)S(1)}, u32[]{:S(2)}, u32[]{:S(2)}) collective-permute-start(bf16[128,512]{1,0:T(8,128)(2,1)S(1)} %collective-permute-done.11.refs_0_), channel_id=1, source_target_pairs={{0,2},{1,3},{2,0},{3,1},{4,6},{5,7},{6,4},{7,5},{8,10},{9,11},{10,... | collective-permute-start | bytes 393224 | tf_op jit(solution)/shard_map/ppermute | solution.py:20
  32.9 1.3 %collective-permute-done.10.refs_0_ = bf16[128,128]{1,0:T(8,128)(2,1)S(1)} collective-permute-done((bf16[128,128]{1,0:T(8,128)(2,1)S(1)}, bf16[128,128]{1,0:T(8,128)(2,1)S(1)}, u32[]{:S(2)}, u32[]{:S(2)}) %collective-permute-start.10) | collective-permute-done | bytes 32800 | tf_op jit(solution)/shard_map/ppermute | solution.py:20
  34.1 2.7 %collective-permute-start.13 = (bf16[128,128]{1,0:T(8,128)(2,1)S(1)}, bf16[128,128]{1,0:T(8,128)(2,1)S(1)}, u32[]{:S(2)}, u32[]{:S(2)}) collective-permute-start(bf16[128,128]{1,0:T(8,128)(2,1)S(1)} %add_convert_fusion), channel_id=1, source_target_pairs={{0,4},{1,5},{2,6},{3,7},{4,0},{5,1},{6,2},{7,3},{8,12},{9,13},{10,... | collective-permute-start | bytes 98312 | tf_op jit(solution)/shard_map/ppermute | solution.py:20
  36.8 0.5 %collective-permute-start.16 = (bf16[128,1024]{1,0:T(8,128)(2,1)S(1)}, bf16[128,1024]{1,0:T(8,128)(2,1)S(1)}, u32[]{:S(2)}, u32[]{:S(2)}) collective-permute-start(bf16[128,1024]{1,0:T(8,128)(2,1)S(1)} %collective-permute-done.9.refs_2_), channel_id=1, source_target_pairs={{0,1},{1,0},{2,3},{3,2},{4,5},{5,4},{6,7},{7,6},{8,9},{9,8},{10,11... | collective-permute-start | bytes 786440 | tf_op jit(solution)/shard_map/ppermute | solution.py:20
  37.3 0.5 %shard_map.53 = (f32[2,256,128]{2,1,0:T(8,128)S(1)}, bf16[128,1024]{1,0:T(8,128)(2,1)S(1)}) custom-call(bf16[2,256,256]{2,1,0:T(8,128)(2,1)S(1)} %get-tuple-element.54.act, bf16[2,256,128]{2,1,0:T(8,128)(2,1)S(1)} %get-tuple-element.55.values, bf16[128,512]{1,0:T(8,128)(2,1)S(1)} %collective-permute-done.11.refs_0_, ...), custom_call_target="tpu_custom_call" | custom-call | flops 32768000000 | tf_op jit(solution)/shard_map/pallas_call | solution.py:188
  37.9 0.1 collective-permute-start.17
  38.0 1.0 %collective-permute-done.13.refs_1_ = bf16[128,128]{1,0:T(8,128)(2,1)S(1)} collective-permute-done((bf16[128,128]{1,0:T(8,128)(2,1)S(1)}, bf16[128,128]{1,0:T(8,128)(2,1)S(1)}, u32[]{:S(2)}, u32[]{:S(2)}) %collective-permute-start.13) | collective-permute-done | bytes 32800 | tf_op jit(solution)/shard_map/ppermute | solution.py:20
  39.0 0.3 shard_map.54
  39.4 0.1 collective-permute-start.14
  39.4 1.2 %collective-permute-done.14.other = bf16[256,128]{1,0:T(8,128)(2,1)S(1)} collective-permute-done((bf16[256,128]{1,0:T(8,128)(2,1)S(1)}, bf16[256,128]{1,0:T(8,128)(2,1)S(1)}, u32[]{:S(2)}, u32[]{:S(2)}) %collective-permute-start.14) | collective-permute-done | bytes 65568 | tf_op jit(solution)/shard_map/ppermute | solution.py:20
  40.7 1.7 %shard_map.55 = bf16[256,4096]{1,0:T(8,128)(2,1)} custom-call(bf16[256,128]{1,0:T(8,128)(2,1)S(1)} %get-tuple-element.61.own, bf16[256,128]{1,0:T(8,128)(2,1)S(1)} %collective-permute-done.14.other, bf16[128,1024]{1,0:T(8,128)(2,1)S(1)} %get-tuple-element.53.refs_0_, bf16[128,1024]{1,0:T(8,128)(2,1)S(1)} %collective-permute-done.8.refs_1_, ...), custom_call_target="tpu_custom_call" | custom-call | flops 536870912 | bytes 2097152 | tf_op jit(solution)/shard_map/pallas_call | solution.py:188
  (21 shorter events, 0.2 us)
Async XLA Ops:
  0.0 13.8 %copy-start = (bf16[1,256,4096]{2,1,0:T(8,128)(2,1)S(1)}, bf16[1,256,4096]{2,1,0:T(8,128)(2,1)}, u32[]{:S(2)}) copy-start(bf16[1,256,4096]{2,1,0:T(8,128)(2,1)} %param.4) | copy-start | bytes 6291460
  0.0 13.8 %collective-permute-start = (bf16[256,4096]{1,0:T(8,128)(2,1)}, bf16[256,4096]{1,0:T(8,128)(2,1)S(1)}, u32[]{:S(2)}, u32[]{:S(2)}) collective-permute-start(bf16[256,4096]{1,0:T(8,128)(2,1)} %bitcast.3), channel_id=1, source_target_pairs={{0,1},{1,0},{2,3},{3,2},{4,5},{5,4},{6,7},{7,6},{8,9},{9,8},{10,11... | collective-permute-start | bytes 6291464 | tf_op jit(solution)/shard_map/ppermute | solution.py:20
  1.6 9.2 %collective-permute-start.1 = (bf16[256,384]{1,0:T(8,128)(2,1)S(1)}, bf16[256,384]{1,0:T(8,128)(2,1)S(1)}, u32[]{:S(2)}, u32[]{:S(2)}) collective-permute-start(bf16[256,384]{1,0:T(8,128)(2,1)S(1)} %shard_map.46), channel_id=1, source_target_pairs={{0,24},{8,16},{16,8},{24,0},{1,25},{9,17},{17,9},{25,1},{2,26},{10... | collective-permute-start | bytes 589832 | tf_op jit(solution)/shard_map/ppermute | solution.py:20
  6.3 17.7 %collective-permute-start.6 = (bf16[768,384]{1,0:T(8,128)(2,1)S(1)}, bf16[768,384]{1,0:T(8,128)(2,1)S(1)}, u32[]{:S(2)}, u32[]{:S(2)}) collective-permute-start(bf16[768,384]{1,0:T(8,128)(2,1)S(1)} %get-tuple-element.42), channel_id=1, source_target_pairs={{0,8},{8,0},{16,24},{24,16},{1,9},{9,1},{17,25},{25,17},{2,10},{10... | collective-permute-start | bytes 1769480 | tf_op jit(solution)/shard_map/ppermute | solution.py:20
  6.9 16.0 %copy-start.1 = (bf16[256,1024]{1,0:T(8,128)(2,1)S(1)}, bf16[256,1024]{1,0:T(8,128)(2,1)}, u32[]{:S(2)}) copy-start(bf16[256,1024]{1,0:T(8,128)(2,1)} %w_out.1) | copy-start | bytes 1572868
  6.9 21.6 %collective-permute-start.5 = (bf16[1024,384]{1,0:T(8,128)(2,1)S(1)}, bf16[1024,384]{1,0:T(8,128)(2,1)S(1)}, u32[]{:S(2)}, u32[]{:S(2)}) collective-permute-start(bf16[1024,384]{1,0:T(8,128)(2,1)S(1)} %get-tuple-element.37.refs_0_), channel_id=1, source_target_pairs={{0,16},{8,24},{16,0},{24,8},{1,17},{9,25},{17,1},{25,9},{2,18},{10... | collective-permute-start | bytes 2359304 | tf_op jit(solution)/shard_map/ppermute | solution.py:20
  10.8 11.5 %collective-permute-start.2 = (bf16[256,384]{1,0:T(8,128)(2,1)S(1)}, bf16[256,384]{1,0:T(8,128)(2,1)S(1)}, u32[]{:S(2)}, u32[]{:S(2)}) collective-permute-start(bf16[256,384]{1,0:T(8,128)(2,1)S(1)} %collective-permute-done.1.refs_1_), channel_id=1, source_target_pairs={{0,4},{1,5},{2,6},{3,7},{4,0},{5,1},{6,2},{7,3},{8,12},{9,13},{10,... | collective-permute-start | bytes 589832 | tf_op jit(solution)/shard_map/ppermute | solution.py:20
  14.5 10.9 %collective-permute-start.7 = (bf16[256,384]{1,0:T(8,128)(2,1)S(1)}, bf16[256,384]{1,0:T(8,128)(2,1)S(1)}, u32[]{:S(2)}, u32[]{:S(2)}) collective-permute-start(bf16[256,384]{1,0:T(8,128)(2,1)S(1)} %collective-permute-done.1.refs_1_), channel_id=1, source_target_pairs={{0,2},{1,3},{2,0},{3,1},{4,6},{5,7},{6,4},{7,5},{8,10},{9,11},{10,... | collective-permute-start | bytes 589832 | tf_op jit(solution)/shard_map/ppermute | solution.py:20
  16.2 12.0 %collective-permute-start.4 = (bf16[256,384]{1,0:T(8,128)(2,1)S(1)}, bf16[256,384]{1,0:T(8,128)(2,1)S(1)}, u32[]{:S(2)}, u32[]{:S(2)}) collective-permute-start(bf16[256,384]{1,0:T(8,128)(2,1)S(1)} %get-tuple-element.41), channel_id=1, source_target_pairs={{0,8},{8,0},{16,24},{24,16},{1,9},{9,1},{17,25},{25,17},{2,10},{10... | collective-permute-start | bytes 589832 | tf_op jit(solution)/shard_map/ppermute | solution.py:20
  22.3 7.1 %collective-permute-start.3 = (bf16[256,384]{1,0:T(8,128)(2,1)S(1)}, bf16[256,384]{1,0:T(8,128)(2,1)S(1)}, u32[]{:S(2)}, u32[]{:S(2)}) collective-permute-start(bf16[256,384]{1,0:T(8,128)(2,1)S(1)} %collective-permute-done.2.refs_2_), channel_id=1, source_target_pairs={{0,2},{1,3},{2,0},{3,1},{4,6},{5,7},{6,4},{7,5},{8,10},{9,11},{10,... | collective-permute-start | bytes 589832 | tf_op jit(solution)/shard_map/ppermute | solution.py:20
  24.0 7.7 %collective-permute-start.11 = (bf16[128,512]{1,0:T(8,128)(2,1)S(1)}, bf16[128,512]{1,0:T(8,128)(2,1)S(1)}, u32[]{:S(2)}, u32[]{:S(2)}) collective-permute-start(bf16[128,512]{1,0:T(8,128)(2,1)S(1)} %get-tuple-element.57), channel_id=1, source_target_pairs={{0,24},{8,16},{16,8},{24,0},{1,25},{9,17},{17,9},{25,1},{2,26},{10... | collective-permute-start | bytes 393224 | tf_op jit(solution)/shard_map/ppermute | solution.py:20
  25.5 11.4 %collective-permute-start.8 = (bf16[128,1024]{1,0:T(8,128)(2,1)S(1)}, bf16[128,1024]{1,0:T(8,128)(2,1)S(1)}, u32[]{:S(2)}, u32[]{:S(2)}) collective-permute-start(bf16[128,1024]{1,0:T(8,128)(2,1)S(1)} %get-tuple-element.53.refs_0_), channel_id=1, source_target_pairs={{0,8},{8,0},{16,24},{24,16},{1,9},{9,1},{17,25},{25,17},{2,10},{10... | collective-permute-start | bytes 786440 | tf_op jit(solution)/shard_map/ppermute | solution.py:20
  28.2 8.6 %collective-permute-start.9 = (bf16[128,1024]{1,0:T(8,128)(2,1)S(1)}, bf16[128,1024]{1,0:T(8,128)(2,1)S(1)}, u32[]{:S(2)}, u32[]{:S(2)}) collective-permute-start(bf16[128,1024]{1,0:T(8,128)(2,1)S(1)} %get-tuple-element.53.refs_0_), channel_id=1, source_target_pairs={{0,16},{8,24},{16,0},{24,8},{1,17},{9,25},{17,1},{25,9},{2,18},{10... | collective-permute-start | bytes 786440 | tf_op jit(solution)/shard_map/ppermute | solution.py:20
  29.9 4.2 %collective-permute-start.10 = (bf16[128,128]{1,0:T(8,128)(2,1)S(1)}, bf16[128,128]{1,0:T(8,128)(2,1)S(1)}, u32[]{:S(2)}, u32[]{:S(2)}) collective-permute-start(bf16[128,128]{1,0:T(8,128)(2,1)S(1)} %get-tuple-element.56), channel_id=1, source_target_pairs={{0,2},{1,3},{2,0},{3,1},{4,6},{5,7},{6,4},{7,5},{8,10},{9,11},{10,... | collective-permute-start | bytes 98312 | tf_op jit(solution)/shard_map/ppermute | solution.py:20
  31.7 5.7 %collective-permute-start.12 = (bf16[128,512]{1,0:T(8,128)(2,1)S(1)}, bf16[128,512]{1,0:T(8,128)(2,1)S(1)}, u32[]{:S(2)}, u32[]{:S(2)}) collective-permute-start(bf16[128,512]{1,0:T(8,128)(2,1)S(1)} %collective-permute-done.11.refs_0_), channel_id=1, source_target_pairs={{0,2},{1,3},{2,0},{3,1},{4,6},{5,7},{6,4},{7,5},{8,10},{9,11},{10,... | collective-permute-start | bytes 393224 | tf_op jit(solution)/shard_map/ppermute | solution.py:20
  34.1 4.9 %collective-permute-start.13 = (bf16[128,128]{1,0:T(8,128)(2,1)S(1)}, bf16[128,128]{1,0:T(8,128)(2,1)S(1)}, u32[]{:S(2)}, u32[]{:S(2)}) collective-permute-start(bf16[128,128]{1,0:T(8,128)(2,1)S(1)} %add_convert_fusion), channel_id=1, source_target_pairs={{0,4},{1,5},{2,6},{3,7},{4,0},{5,1},{6,2},{7,3},{8,12},{9,13},{10,... | collective-permute-start | bytes 98312 | tf_op jit(solution)/shard_map/ppermute | solution.py:20
  36.8 3.8 %collective-permute-start.15 = (bf16[128,1024]{1,0:T(8,128)(2,1)S(1)}, bf16[128,1024]{1,0:T(8,128)(2,1)S(1)}, u32[]{:S(2)}, u32[]{:S(2)}) collective-permute-start(bf16[128,1024]{1,0:T(8,128)(2,1)S(1)} %collective-permute-done.8.refs_1_), channel_id=1, source_target_pairs={{0,1},{1,0},{2,3},{3,2},{4,5},{5,4},{6,7},{7,6},{8,9},{9,8},{10,11... | collective-permute-start | bytes 786440 | tf_op jit(solution)/shard_map/ppermute | solution.py:20
  36.8 3.8 %collective-permute-start.16 = (bf16[128,1024]{1,0:T(8,128)(2,1)S(1)}, bf16[128,1024]{1,0:T(8,128)(2,1)S(1)}, u32[]{:S(2)}, u32[]{:S(2)}) collective-permute-start(bf16[128,1024]{1,0:T(8,128)(2,1)S(1)} %collective-permute-done.9.refs_2_), channel_id=1, source_target_pairs={{0,1},{1,0},{2,3},{3,2},{4,5},{5,4},{6,7},{7,6},{8,9},{9,8},{10,11... | collective-permute-start | bytes 786440 | tf_op jit(solution)/shard_map/ppermute | solution.py:20
  37.3 1.7 %copy-start.2 = (f32[256]{0:T(256)S(1)}, f32[256]{0:T(256)}, u32[]{:S(2)}) copy-start(f32[256]{0:T(256)} %param.6) | copy-start | bytes 3076
  37.9 2.8 %collective-permute-start.17 = (bf16[128,1024]{1,0:T(8,128)(2,1)S(1)}, bf16[128,1024]{1,0:T(8,128)(2,1)S(1)}, u32[]{:S(2)}, u32[]{:S(2)}) collective-permute-start(bf16[128,1024]{1,0:T(8,128)(2,1)S(1)} %get-tuple-element.65.refs_3_), channel_id=1, source_target_pairs={{0,1},{1,0},{2,3},{3,2},{4,5},{5,4},{6,7},{7,6},{8,9},{9,8},{10,11... | collective-permute-start | bytes 786440 | tf_op jit(solution)/shard_map/ppermute | solution.py:20
  39.4 1.3 %collective-permute-start.14 = (bf16[256,128]{1,0:T(8,128)(2,1)S(1)}, bf16[256,128]{1,0:T(8,128)(2,1)S(1)}, u32[]{:S(2)}, u32[]{:S(2)}) collective-permute-start(bf16[256,128]{1,0:T(8,128)(2,1)S(1)} %get-tuple-element.62), channel_id=1, source_target_pairs={{0,1},{1,0},{2,3},{3,2},{4,5},{5,4},{6,7},{7,6},{8,9},{9,8},{10,11... | collective-permute-start | bytes 196616 | tf_op jit(solution)/shard_map/ppermute | solution.py:20

commit v7 on v5

--- a/solution.py
+++ b/solution.py
@@ -46,7 +46,7 @@
         cols = pl.ds(pl.multiple_of(j * feat + core * HEAD, HEAD), HEAD)
         target = out.at[:, j * HEAD : (j + 1) * HEAD]
         copies.append(pltpu.make_async_copy(w_qkv.at[rows, cols], target, sem.at[j]))
-        copies[-1].start()
+        copies[-1].start(priority=len(copies) % 2)
     for copy in copies:
         copy.wait()
     at = 0
@@ -166,7 +166,7 @@
             here[...] = dot(normed, weights).astype(jnp.bfloat16)
             cols = pl.ds(pl.multiple_of(place + at_col, 128), step)
             copies.append(pltpu.make_async_copy(here, out.at[:, cols], sem.at[len(copies)]))
-            copies[-1].start()
+            copies[-1].start(priority=len(copies) % 2)
             slot += step
     for copy in copies:
         copy.wait()

time: 42.5 us -> 42.5 us (level)
  no operation moved by 1% of the time
where the time goes in v7:
time: 42.5 us; the launch traced here: 42.4 us
  starting transfers between devices  20.1 us (47%)
  waiting for transfers between devices  14.3 us (34%)
  Pallas kernels  7.91 us (19%)
    ppermute x18, starting transfers between devices, flip(): return lax.ppermute(x, axis, [(i, i ^ mask) for i in range(size)])  20.1 us
    ppermute x18, waiting for transfers between devices, flip(): return lax.ppermute(x, axis, [(i, i ^ mask) for i in range(size)])  14.3 us
    pallas_call x10, Pallas kernels, call(): pl.pallas_call(kernel, out_shape=outs, in_specs=in_specs, out_specs=out_s...  7.91 us
  transfers between devices with their start and end apart: 18, of which 7 were waited for; matrix products, arithmetic and copies ran while one was open for 0% of the time, Pallas kernels for 15%

profile of v7, /device:TPU:0, one launch (start us, length us, event | category | flops | bytes accessed | tf_op | source)
XLA Modules:
  0.0 42.4 jit_solution(5289830988591771532)
XLA Ops:
  0.0 0.5 %collective-permute-start = (bf16[256,4096]{1,0:T(8,128)(2,1)}, bf16[256,4096]{1,0:T(8,128)(2,1)S(1)}, u32[]{:S(2)}, u32[]{:S(2)}) collective-permute-start(bf16[256,4096]{1,0:T(8,128)(2,1)} %bitcast.3), channel_id=1, source_target_pairs={{0,1},{1,0},{2,3},{3,2},{4,5},{5,4},{6,7},{7,6},{8,9},{9,8},{10,11... | collective-permute-start | bytes 6291464 | tf_op jit(solution)/shard_map/ppermute | solution.py:20
  0.5 1.1 %shard_map.46 = bf16[256,384]{1,0:T(8,128)(2,1)S(1)} custom-call(bf16[1024,768]{1,0:T(8,128)(2,1)} %w_qkv.3), custom_call_target="tpu_custom_call" | custom-call | tf_op jit(solution)/shard_map/pallas_call | solution.py:188
  1.6 3.5 %collective-permute-start.1 = (bf16[256,384]{1,0:T(8,128)(2,1)S(1)}, bf16[256,384]{1,0:T(8,128)(2,1)S(1)}, u32[]{:S(2)}, u32[]{:S(2)}) collective-permute-start(bf16[256,384]{1,0:T(8,128)(2,1)S(1)} %shard_map.46), channel_id=1, source_target_pairs={{0,24},{8,16},{16,8},{24,0},{1,25},{9,17},{17,9},{25,1},{2,26},{10... | collective-permute-start | bytes 589832 | tf_op jit(solution)/shard_map/ppermute | solution.py:20
  5.1 1.2 %shard_map.47 = (bf16[1024,384]{1,0:T(8,128)(2,1)S(1)}, bf16[768,384]{1,0:T(8,128)(2,1)S(1)}, bf16[256,384]{1,0:T(8,128)(2,1)S(1)}) custom-call(bf16[1024,768]{1,0:T(8,128)(2,1)} %w_qkv.3), custom_call_target="tpu_custom_call" | custom-call | tf_op jit(solution)/shard_map/pallas_call | solution.py:188
  6.3 0.6 %collective-permute-start.6 = (bf16[768,384]{1,0:T(8,128)(2,1)S(1)}, bf16[768,384]{1,0:T(8,128)(2,1)S(1)}, u32[]{:S(2)}, u32[]{:S(2)}) collective-permute-start(bf16[768,384]{1,0:T(8,128)(2,1)S(1)} %get-tuple-element.42), channel_id=1, source_target_pairs={{0,8},{8,0},{16,24},{24,16},{1,9},{9,1},{17,25},{25,17},{2,10},{10... | collective-permute-start | bytes 1769480 | tf_op jit(solution)/shard_map/ppermute | solution.py:20
  7.0 3.9 %collective-permute-done.1.refs_1_ = bf16[256,384]{1,0:T(8,128)(2,1)S(1)} collective-permute-done((bf16[256,384]{1,0:T(8,128)(2,1)S(1)}, bf16[256,384]{1,0:T(8,128)(2,1)S(1)}, u32[]{:S(2)}, u32[]{:S(2)}) %collective-permute-start.1) | collective-permute-done | bytes 196640 | tf_op jit(solution)/shard_map/ppermute | solution.py:20
  10.8 3.0 %collective-permute-start.2 = (bf16[256,384]{1,0:T(8,128)(2,1)S(1)}, bf16[256,384]{1,0:T(8,128)(2,1)S(1)}, u32[]{:S(2)}, u32[]{:S(2)}) collective-permute-start(bf16[256,384]{1,0:T(8,128)(2,1)S(1)} %collective-permute-done.1.refs_1_), channel_id=1, source_target_pairs={{0,4},{1,5},{2,6},{3,7},{4,0},{5,1},{6,2},{7,3},{8,12},{9,13},{10,... | collective-permute-start | bytes 589832 | tf_op jit(solution)/shard_map/ppermute | solution.py:20
  13.8 0.7 %shard_map.48.refs_4_ = f32[512,384]{1,0:T(8,128)S(1)} custom-call(bf16[256,4096]{1,0:T(8,128)(2,1)S(1)} %bitcast.4, bf16[256,4096]{1,0:T(8,128)(2,1)S(1)} %collective-permute-done.tok_b, bf16[1024,384]{1,0:T(8,128)(2,1)S(1)} %get-tuple-element.37.refs_0_), custom_call_target="tpu_custom_call" | custom-call | flops 32768000000 | tf_op jit(solution)/shard_map/pallas_call | solution.py:188
  14.5 1.6 %collective-permute-start.7 = (bf16[256,384]{1,0:T(8,128)(2,1)S(1)}, bf16[256,384]{1,0:T(8,128)(2,1)S(1)}, u32[]{:S(2)}, u32[]{:S(2)}) collective-permute-start(bf16[256,384]{1,0:T(8,128)(2,1)S(1)} %collective-permute-done.1.refs_1_), channel_id=1, source_target_pairs={{0,2},{1,3},{2,0},{3,1},{4,6},{5,7},{6,4},{7,5},{8,10},{9,11},{10,... | collective-permute-start | bytes 589832 | tf_op jit(solution)/shard_map/ppermute | solution.py:20
  16.2 1.5 %collective-permute-start.4 = (bf16[256,384]{1,0:T(8,128)(2,1)S(1)}, bf16[256,384]{1,0:T(8,128)(2,1)S(1)}, u32[]{:S(2)}, u32[]{:S(2)}) collective-permute-start(bf16[256,384]{1,0:T(8,128)(2,1)S(1)} %get-tuple-element.41), channel_id=1, source_target_pairs={{0,8},{8,0},{16,24},{24,16},{1,9},{9,1},{17,25},{25,17},{2,10},{10... | collective-permute-start | bytes 589832 | tf_op jit(solution)/shard_map/ppermute | solution.py:20
  17.7 4.6 %collective-permute-done.2.refs_2_ = bf16[256,384]{1,0:T(8,128)(2,1)S(1)} collective-permute-done((bf16[256,384]{1,0:T(8,128)(2,1)S(1)}, bf16[256,384]{1,0:T(8,128)(2,1)S(1)}, u32[]{:S(2)}, u32[]{:S(2)}) %collective-permute-start.2) | collective-permute-done | bytes 196640 | tf_op jit(solution)/shard_map/ppermute | solution.py:20
  22.3 0.6 %collective-permute-start.3 = (bf16[256,384]{1,0:T(8,128)(2,1)S(1)}, bf16[256,384]{1,0:T(8,128)(2,1)S(1)}, u32[]{:S(2)}, u32[]{:S(2)}) collective-permute-start(bf16[256,384]{1,0:T(8,128)(2,1)S(1)} %collective-permute-done.2.refs_2_), channel_id=1, source_target_pairs={{0,2},{1,3},{2,0},{3,1},{4,6},{5,7},{6,4},{7,5},{8,10},{9,11},{10,... | collective-permute-start | bytes 589832 | tf_op jit(solution)/shard_map/ppermute | solution.py:20
  22.9 1.1 %collective-permute-done.6.refs_0_ = bf16[768,384]{1,0:T(8,128)(2,1)S(1)} collective-permute-done((bf16[768,384]{1,0:T(8,128)(2,1)S(1)}, bf16[768,384]{1,0:T(8,128)(2,1)S(1)}, u32[]{:S(2)}, u32[]{:S(2)}) %collective-permute-start.6) | collective-permute-done | bytes 589856 | tf_op jit(solution)/shard_map/ppermute | solution.py:20
  24.0 1.5 %collective-permute-start.11 = (bf16[128,512]{1,0:T(8,128)(2,1)S(1)}, bf16[128,512]{1,0:T(8,128)(2,1)S(1)}, u32[]{:S(2)}, u32[]{:S(2)}) collective-permute-start(bf16[128,512]{1,0:T(8,128)(2,1)S(1)} %get-tuple-element.57), channel_id=1, source_target_pairs={{0,24},{8,16},{16,8},{24,0},{1,25},{9,17},{17,9},{25,1},{2,26},{10... | collective-permute-start | bytes 393224 | tf_op jit(solution)/shard_map/ppermute | solution.py:20
  25.5 0.5 %collective-permute-start.8 = (bf16[128,1024]{1,0:T(8,128)(2,1)S(1)}, bf16[128,1024]{1,0:T(8,128)(2,1)S(1)}, u32[]{:S(2)}, u32[]{:S(2)}) collective-permute-start(bf16[128,1024]{1,0:T(8,128)(2,1)S(1)} %get-tuple-element.53.refs_0_), channel_id=1, source_target_pairs={{0,8},{8,0},{16,24},{24,16},{1,9},{9,1},{17,25},{25,17},{2,10},{10... | collective-permute-start | bytes 786440 | tf_op jit(solution)/shard_map/ppermute | solution.py:20
  26.0 1.0 %shard_map.50.refs_2_ = f32[512,384]{1,0:T(8,128)S(1)} custom-call(bf16[256,4096]{1,0:T(8,128)(2,1)S(1)} %bitcast.5, bf16[256,4096]{1,0:T(8,128)(2,1)S(1)} %collective-permute-done.tok_b, bf16[768,384]{1,0:T(8,128)(2,1)S(1)} %collective-permute-done.6.refs_0_, bf16[256,384]{1,0:T(8,128)(2,1)S(1)} %collective-permute-done.1.refs_1_, ...), custom_call_target="tpu_custom_call" | custom-call | flops 32768 | tf_op jit(solution)/shard_map/pallas_call | solution.py:188
  27.0 1.2 %collective-permute-done.4.refs_0_ = bf16[256,384]{1,0:T(8,128)(2,1)S(1)} collective-permute-done((bf16[256,384]{1,0:T(8,128)(2,1)S(1)}, bf16[256,384]{1,0:T(8,128)(2,1)S(1)}, u32[]{:S(2)}, u32[]{:S(2)}) %collective-permute-start.4) | collective-permute-done | bytes 196640 | tf_op jit(solution)/shard_map/ppermute | solution.py:20
  28.2 0.3 collective-permute-start.9
  28.5 0.8 %shard_map.51.refs_1_ = f32[512,384]{1,0:T(8,128)S(1)} custom-call(bf16[256,4096]{1,0:T(8,128)(2,1)S(1)} %bitcast.6, bf16[256,4096]{1,0:T(8,128)(2,1)S(1)} %collective-permute-done.tok_b, bf16[256,384]{1,0:T(8,128)(2,1)S(1)} %collective-permute-done.4.refs_0_, bf16[1024,384]{1,0:T(8,128)(2,1)S(1)} %collective-permute-done.5.refs_1_, ...), custom_call_target="tpu_custom_call" | custom-call | flops 32768 | tf_op jit(solution)/shard_map/pallas_call | solution.py:188
  29.4 0.5 %shard_map.52 = (bf16[2,256,256]{2,1,0:T(8,128)(2,1)S(1)}, bf16[2,256,128]{2,1,0:T(8,128)(2,1)S(1)}, f32[2,128,128]{2,1,0:T(8,128)S(1)}, bf16[128,128]{1,0:T(8,128)(2,1)S(1)}) custom-call(bf16[256,4096]{1,0:T(8,128)(2,1)S(1)} %bitcast.7, bf16[256,4096]{1,0:T(8,128)(2,1)S(1)} %collective-permute-done.tok_b, ...), custom_call_target="tpu_custom_call" | custom-call | flops 100663296 | tf_op jit(solution)/shard_map/pallas_call | solution.py:188
  29.9 1.8 %collective-permute-start.10 = (bf16[128,128]{1,0:T(8,128)(2,1)S(1)}, bf16[128,128]{1,0:T(8,128)(2,1)S(1)}, u32[]{:S(2)}, u32[]{:S(2)}) collective-permute-start(bf16[128,128]{1,0:T(8,128)(2,1)S(1)} %get-tuple-element.56), channel_id=1, source_target_pairs={{0,2},{1,3},{2,0},{3,1},{4,6},{5,7},{6,4},{7,5},{8,10},{9,11},{10,... | collective-permute-start | bytes 98312 | tf_op jit(solution)/shard_map/ppermute | solution.py:20
  31.7 1.2 %collective-permute-start.12 = (bf16[128,512]{1,0:T(8,128)(2,1)S(1)}, bf16[128,512]{1,0:T(8,128)(2,1)S(1)}, u32[]{:S(2)}, u32[]{:S(2)}) collective-permute-start(bf16[128,512]{1,0:T(8,128)(2,1)S(1)} %collective-permute-done.11.refs_0_), channel_id=1, source_target_pairs={{0,2},{1,3},{2,0},{3,1},{4,6},{5,7},{6,4},{7,5},{8,10},{9,11},{10,... | collective-permute-start | bytes 393224 | tf_op jit(solution)/shard_map/ppermute | solution.py:20
  32.9 1.3 %collective-permute-done.10.refs_0_ = bf16[128,128]{1,0:T(8,128)(2,1)S(1)} collective-permute-done((bf16[128,128]{1,0:T(8,128)(2,1)S(1)}, bf16[128,128]{1,0:T(8,128)(2,1)S(1)}, u32[]{:S(2)}, u32[]{:S(2)}) %collective-permute-start.10) | collective-permute-done | bytes 32800 | tf_op jit(solution)/shard_map/ppermute | solution.py:20
  34.1 2.7 %collective-permute-start.13 = (bf16[128,128]{1,0:T(8,128)(2,1)S(1)}, bf16[128,128]{1,0:T(8,128)(2,1)S(1)}, u32[]{:S(2)}, u32[]{:S(2)}) collective-permute-start(bf16[128,128]{1,0:T(8,128)(2,1)S(1)} %add_convert_fusion), channel_id=1, source_target_pairs={{0,4},{1,5},{2,6},{3,7},{4,0},{5,1},{6,2},{7,3},{8,12},{9,13},{10,... | collective-permute-start | bytes 98312 | tf_op jit(solution)/shard_map/ppermute | solution.py:20
  36.8 0.5 %collective-permute-start.16 = (bf16[128,1024]{1,0:T(8,128)(2,1)S(1)}, bf16[128,1024]{1,0:T(8,128)(2,1)S(1)}, u32[]{:S(2)}, u32[]{:S(2)}) collective-permute-start(bf16[128,1024]{1,0:T(8,128)(2,1)S(1)} %collective-permute-done.9.refs_2_), channel_id=1, source_target_pairs={{0,1},{1,0},{2,3},{3,2},{4,5},{5,4},{6,7},{7,6},{8,9},{9,8},{10,11... | collective-permute-start | bytes 786440 | tf_op jit(solution)/shard_map/ppermute | solution.py:20
  37.3 0.5 %shard_map.53 = (f32[2,256,128]{2,1,0:T(8,128)S(1)}, bf16[128,1024]{1,0:T(8,128)(2,1)S(1)}) custom-call(bf16[2,256,256]{2,1,0:T(8,128)(2,1)S(1)} %get-tuple-element.54.act, bf16[2,256,128]{2,1,0:T(8,128)(2,1)S(1)} %get-tuple-element.55.values, bf16[128,512]{1,0:T(8,128)(2,1)S(1)} %collective-permute-done.11.refs_0_, ...), custom_call_target="tpu_custom_call" | custom-call | flops 32768000000 | tf_op jit(solution)/shard_map/pallas_call | solution.py:188
  37.9 0.1 collective-permute-start.17
  38.0 1.0 %collective-permute-done.13.refs_1_ = bf16[128,128]{1,0:T(8,128)(2,1)S(1)} collective-permute-done((bf16[128,128]{1,0:T(8,128)(2,1)S(1)}, bf16[128,128]{1,0:T(8,128)(2,1)S(1)}, u32[]{:S(2)}, u32[]{:S(2)}) %collective-permute-start.13) | collective-permute-done | bytes 32800 | tf_op jit(solution)/shard_map/ppermute | solution.py:20
  39.0 0.3 shard_map.54
  39.4 0.1 collective-permute-start.14
  39.4 1.2 %collective-permute-done.14.other = bf16[256,128]{1,0:T(8,128)(2,1)S(1)} collective-permute-done((bf16[256,128]{1,0:T(8,128)(2,1)S(1)}, bf16[256,128]{1,0:T(8,128)(2,1)S(1)}, u32[]{:S(2)}, u32[]{:S(2)}) %collective-permute-start.14) | collective-permute-done | bytes 65568 | tf_op jit(solution)/shard_map/ppermute | solution.py:20
  40.7 1.7 %shard_map.55 = bf16[256,4096]{1,0:T(8,128)(2,1)} custom-call(bf16[256,128]{1,0:T(8,128)(2,1)S(1)} %get-tuple-element.61.own, bf16[256,128]{1,0:T(8,128)(2,1)S(1)} %collective-permute-done.14.other, bf16[128,1024]{1,0:T(8,128)(2,1)S(1)} %get-tuple-element.53.refs_0_, bf16[128,1024]{1,0:T(8,128)(2,1)S(1)} %collective-permute-done.8.refs_1_, ...), custom_call_target="tpu_custom_call" | custom-call | flops 536870912 | bytes 2097152 | tf_op jit(solution)/shard_map/pallas_call | solution.py:188
  (21 shorter events, 0.2 us)
Async XLA Ops:
  0.0 13.8 %copy-start = (bf16[1,256,4096]{2,1,0:T(8,128)(2,1)S(1)}, bf16[1,256,4096]{2,1,0:T(8,128)(2,1)}, u32[]{:S(2)}) copy-start(bf16[1,256,4096]{2,1,0:T(8,128)(2,1)} %param.4) | copy-start | bytes 6291460
  0.0 13.8 %collective-permute-start = (bf16[256,4096]{1,0:T(8,128)(2,1)}, bf16[256,4096]{1,0:T(8,128)(2,1)S(1)}, u32[]{:S(2)}, u32[]{:S(2)}) collective-permute-start(bf16[256,4096]{1,0:T(8,128)(2,1)} %bitcast.3), channel_id=1, source_target_pairs={{0,1},{1,0},{2,3},{3,2},{4,5},{5,4},{6,7},{7,6},{8,9},{9,8},{10,11... | collective-permute-start | bytes 6291464 | tf_op jit(solution)/shard_map/ppermute | solution.py:20
  1.6 9.2 %collective-permute-start.1 = (bf16[256,384]{1,0:T(8,128)(2,1)S(1)}, bf16[256,384]{1,0:T(8,128)(2,1)S(1)}, u32[]{:S(2)}, u32[]{:S(2)}) collective-permute-start(bf16[256,384]{1,0:T(8,128)(2,1)S(1)} %shard_map.46), channel_id=1, source_target_pairs={{0,24},{8,16},{16,8},{24,0},{1,25},{9,17},{17,9},{25,1},{2,26},{10... | collective-permute-start | bytes 589832 | tf_op jit(solution)/shard_map/ppermute | solution.py:20
  6.3 17.7 %collective-permute-start.6 = (bf16[768,384]{1,0:T(8,128)(2,1)S(1)}, bf16[768,384]{1,0:T(8,128)(2,1)S(1)}, u32[]{:S(2)}, u32[]{:S(2)}) collective-permute-start(bf16[768,384]{1,0:T(8,128)(2,1)S(1)} %get-tuple-element.42), channel_id=1, source_target_pairs={{0,8},{8,0},{16,24},{24,16},{1,9},{9,1},{17,25},{25,17},{2,10},{10... | collective-permute-start | bytes 1769480 | tf_op jit(solution)/shard_map/ppermute | solution.py:20
  6.9 16.0 %copy-start.1 = (bf16[256,1024]{1,0:T(8,128)(2,1)S(1)}, bf16[256,1024]{1,0:T(8,128)(2,1)}, u32[]{:S(2)}) copy-start(bf16[256,1024]{1,0:T(8,128)(2,1)} %w_out.1) | copy-start | bytes 1572868
  6.9 21.6 %collective-permute-start.5 = (bf16[1024,384]{1,0:T(8,128)(2,1)S(1)}, bf16[1024,384]{1,0:T(8,128)(2,1)S(1)}, u32[]{:S(2)}, u32[]{:S(2)}) collective-permute-start(bf16[1024,384]{1,0:T(8,128)(2,1)S(1)} %get-tuple-element.37.refs_0_), channel_id=1, source_target_pairs={{0,16},{8,24},{16,0},{24,8},{1,17},{9,25},{17,1},{25,9},{2,18},{10... | collective-permute-start | bytes 2359304 | tf_op jit(solution)/shard_map/ppermute | solution.py:20
  10.8 11.5 %collective-permute-start.2 = (bf16[256,384]{1,0:T(8,128)(2,1)S(1)}, bf16[256,384]{1,0:T(8,128)(2,1)S(1)}, u32[]{:S(2)}, u32[]{:S(2)}) collective-permute-start(bf16[256,384]{1,0:T(8,128)(2,1)S(1)} %collective-permute-done.1.refs_1_), channel_id=1, source_target_pairs={{0,4},{1,5},{2,6},{3,7},{4,0},{5,1},{6,2},{7,3},{8,12},{9,13},{10,... | collective-permute-start | bytes 589832 | tf_op jit(solution)/shard_map/ppermute | solution.py:20
  14.5 10.9 %collective-permute-start.7 = (bf16[256,384]{1,0:T(8,128)(2,1)S(1)}, bf16[256,384]{1,0:T(8,128)(2,1)S(1)}, u32[]{:S(2)}, u32[]{:S(2)}) collective-permute-start(bf16[256,384]{1,0:T(8,128)(2,1)S(1)} %collective-permute-done.1.refs_1_), channel_id=1, source_target_pairs={{0,2},{1,3},{2,0},{3,1},{4,6},{5,7},{6,4},{7,5},{8,10},{9,11},{10,... | collective-permute-start | bytes 589832 | tf_op jit(solution)/shard_map/ppermute | solution.py:20
  16.2 12.0 %collective-permute-start.4 = (bf16[256,384]{1,0:T(8,128)(2,1)S(1)}, bf16[256,384]{1,0:T(8,128)(2,1)S(1)}, u32[]{:S(2)}, u32[]{:S(2)}) collective-permute-start(bf16[256,384]{1,0:T(8,128)(2,1)S(1)} %get-tuple-element.41), channel_id=1, source_target_pairs={{0,8},{8,0},{16,24},{24,16},{1,9},{9,1},{17,25},{25,17},{2,10},{10... | collective-permute-start | bytes 589832 | tf_op jit(solution)/shard_map/ppermute | solution.py:20
  22.3 7.1 %collective-permute-start.3 = (bf16[256,384]{1,0:T(8,128)(2,1)S(1)}, bf16[256,384]{1,0:T(8,128)(2,1)S(1)}, u32[]{:S(2)}, u32[]{:S(2)}) collective-permute-start(bf16[256,384]{1,0:T(8,128)(2,1)S(1)} %collective-permute-done.2.refs_2_), channel_id=1, source_target_pairs={{0,2},{1,3},{2,0},{3,1},{4,6},{5,7},{6,4},{7,5},{8,10},{9,11},{10,... | collective-permute-start | bytes 589832 | tf_op jit(solution)/shard_map/ppermute | solution.py:20
  24.0 7.7 %collective-permute-start.11 = (bf16[128,512]{1,0:T(8,128)(2,1)S(1)}, bf16[128,512]{1,0:T(8,128)(2,1)S(1)}, u32[]{:S(2)}, u32[]{:S(2)}) collective-permute-start(bf16[128,512]{1,0:T(8,128)(2,1)S(1)} %get-tuple-element.57), channel_id=1, source_target_pairs={{0,24},{8,16},{16,8},{24,0},{1,25},{9,17},{17,9},{25,1},{2,26},{10... | collective-permute-start | bytes 393224 | tf_op jit(solution)/shard_map/ppermute | solution.py:20
  25.5 11.4 %collective-permute-start.8 = (bf16[128,1024]{1,0:T(8,128)(2,1)S(1)}, bf16[128,1024]{1,0:T(8,128)(2,1)S(1)}, u32[]{:S(2)}, u32[]{:S(2)}) collective-permute-start(bf16[128,1024]{1,0:T(8,128)(2,1)S(1)} %get-tuple-element.53.refs_0_), channel_id=1, source_target_pairs={{0,8},{8,0},{16,24},{24,16},{1,9},{9,1},{17,25},{25,17},{2,10},{10... | collective-permute-start | bytes 786440 | tf_op jit(solution)/shard_map/ppermute | solution.py:20
  28.2 8.6 %collective-permute-start.9 = (bf16[128,1024]{1,0:T(8,128)(2,1)S(1)}, bf16[128,1024]{1,0:T(8,128)(2,1)S(1)}, u32[]{:S(2)}, u32[]{:S(2)}) collective-permute-start(bf16[128,1024]{1,0:T(8,128)(2,1)S(1)} %get-tuple-element.53.refs_0_), channel_id=1, source_target_pairs={{0,16},{8,24},{16,0},{24,8},{1,17},{9,25},{17,1},{25,9},{2,18},{10... | collective-permute-start | bytes 786440 | tf_op jit(solution)/shard_map/ppermute | solution.py:20
  29.9 4.2 %collective-permute-start.10 = (bf16[128,128]{1,0:T(8,128)(2,1)S(1)}, bf16[128,128]{1,0:T(8,128)(2,1)S(1)}, u32[]{:S(2)}, u32[]{:S(2)}) collective-permute-start(bf16[128,128]{1,0:T(8,128)(2,1)S(1)} %get-tuple-element.56), channel_id=1, source_target_pairs={{0,2},{1,3},{2,0},{3,1},{4,6},{5,7},{6,4},{7,5},{8,10},{9,11},{10,... | collective-permute-start | bytes 98312 | tf_op jit(solution)/shard_map/ppermute | solution.py:20
  31.7 5.7 %collective-permute-start.12 = (bf16[128,512]{1,0:T(8,128)(2,1)S(1)}, bf16[128,512]{1,0:T(8,128)(2,1)S(1)}, u32[]{:S(2)}, u32[]{:S(2)}) collective-permute-start(bf16[128,512]{1,0:T(8,128)(2,1)S(1)} %collective-permute-done.11.refs_0_), channel_id=1, source_target_pairs={{0,2},{1,3},{2,0},{3,1},{4,6},{5,7},{6,4},{7,5},{8,10},{9,11},{10,... | collective-permute-start | bytes 393224 | tf_op jit(solution)/shard_map/ppermute | solution.py:20
  34.1 4.9 %collective-permute-start.13 = (bf16[128,128]{1,0:T(8,128)(2,1)S(1)}, bf16[128,128]{1,0:T(8,128)(2,1)S(1)}, u32[]{:S(2)}, u32[]{:S(2)}) collective-permute-start(bf16[128,128]{1,0:T(8,128)(2,1)S(1)} %add_convert_fusion), channel_id=1, source_target_pairs={{0,4},{1,5},{2,6},{3,7},{4,0},{5,1},{6,2},{7,3},{8,12},{9,13},{10,... | collective-permute-start | bytes 98312 | tf_op jit(solution)/shard_map/ppermute | solution.py:20
  36.8 3.8 %collective-permute-start.15 = (bf16[128,1024]{1,0:T(8,128)(2,1)S(1)}, bf16[128,1024]{1,0:T(8,128)(2,1)S(1)}, u32[]{:S(2)}, u32[]{:S(2)}) collective-permute-start(bf16[128,1024]{1,0:T(8,128)(2,1)S(1)} %collective-permute-done.8.refs_1_), channel_id=1, source_target_pairs={{0,1},{1,0},{2,3},{3,2},{4,5},{5,4},{6,7},{7,6},{8,9},{9,8},{10,11... | collective-permute-start | bytes 786440 | tf_op jit(solution)/shard_map/ppermute | solution.py:20
  36.8 3.8 %collective-permute-start.16 = (bf16[128,1024]{1,0:T(8,128)(2,1)S(1)}, bf16[128,1024]{1,0:T(8,128)(2,1)S(1)}, u32[]{:S(2)}, u32[]{:S(2)}) collective-permute-start(bf16[128,1024]{1,0:T(8,128)(2,1)S(1)} %collective-permute-done.9.refs_2_), channel_id=1, source_target_pairs={{0,1},{1,0},{2,3},{3,2},{4,5},{5,4},{6,7},{7,6},{8,9},{9,8},{10,11... | collective-permute-start | bytes 786440 | tf_op jit(solution)/shard_map/ppermute | solution.py:20
  37.3 1.7 %copy-start.2 = (f32[256]{0:T(256)S(1)}, f32[256]{0:T(256)}, u32[]{:S(2)}) copy-start(f32[256]{0:T(256)} %param.6) | copy-start | bytes 3076
  37.9 2.8 %collective-permute-start.17 = (bf16[128,1024]{1,0:T(8,128)(2,1)S(1)}, bf16[128,1024]{1,0:T(8,128)(2,1)S(1)}, u32[]{:S(2)}, u32[]{:S(2)}) collective-permute-start(bf16[128,1024]{1,0:T(8,128)(2,1)S(1)} %get-tuple-element.65.refs_3_), channel_id=1, source_target_pairs={{0,1},{1,0},{2,3},{3,2},{4,5},{5,4},{6,7},{7,6},{8,9},{9,8},{10,11... | collective-permute-start | bytes 786440 | tf_op jit(solution)/shard_map/ppermute | solution.py:20
  39.4 1.3 %collective-permute-start.14 = (bf16[256,128]{1,0:T(8,128)(2,1)S(1)}, bf16[256,128]{1,0:T(8,128)(2,1)S(1)}, u32[]{:S(2)}, u32[]{:S(2)}) collective-permute-start(bf16[256,128]{1,0:T(8,128)(2,1)S(1)} %get-tuple-element.62), channel_id=1, source_target_pairs={{0,1},{1,0},{2,3},{3,2},{4,5},{5,4},{6,7},{7,6},{8,9},{9,8},{10,11... | collective-permute-start | bytes 196616 | tf_op jit(solution)/shard_map/ppermute | solution.py:20
